TPU v7x, 32 devices: a whole 2x2x4 slice. The times are simulated.
32 devices in a mesh: groups: 2 (over x), row: 16 (over z, y, core).
Axes of the slice: x: 2, y: 2, z: 4, core: 2. Of those that a mesh axis runs over, the one named last changes fastest.
Arguments:
- gate_pre: bfloat16 [1024, 32768], P('groups', 'row'), parts along dimension 0, may hold values from -6 to 6
- up_pre: bfloat16 [1024, 32768], P('groups', 'row'), parts along dimension 0, may hold values from -6 to 6
- residual: bfloat16 [1024, 8192], P('groups', 'row'), parts along dimension 0, may hold values from -32 to 32
- gain: float32 [8192], replicated, may hold values from 0.5 to 1.5
- down_weight: bfloat16 [131072, 2048], P('row'), may hold values from -0.046875 to 0.046875
Outputs:
- mixed: bfloat16 [1024, 8192], P('groups', 'row'), parts along dimension 0
- normed: bfloat16 [1024, 8192], P('groups', 'row'), parts along dimension 0
There are 2 independent parts, one for each index of `groups`. A program takes and returns all parts, laid end to end along the dimension named above; an argument that names none is the same for every part. Nothing has to cross between parts.
All inputs are finite; a program needn't handle non-finite values.
Results may differ from a plain program's by a relative error of at most 0.0028.
Values may be sent and summed in bfloat16 or wider, within the bound.
No kernel may reach another device: no remote copies, remote signals or barrier semaphores. Data moves between devices by JAX's collectives and lax.ppermute only.
A program may use at most 256 MiB of HBM per device.

v0:
```python
import jax
import jax.numpy as jnp
from jax import lax
from jax.sharding import PartitionSpec as P

D = 8192
QUAD = 4


def partner(value, axis, bit):
    mask = 2**bit
    pairs = [(source, source ^ mask) for source in range(lax.axis_size(axis))]
    return lax.ppermute(value, axis, pairs)


def gated(gate_pre, up_pre):
    return (jax.nn.silu(gate_pre.astype(jnp.float32)) * up_pre.astype(jnp.float32)).astype(
        jnp.bfloat16
    )


def local(gate_pre, up_pre, residual, gain, down_weight):
    hidden = gated(gate_pre, up_pre)
    unit_count = hidden.shape[1]
    width = D
    own_cols = residual.shape[1]
    quarter = down_weight.shape[1]
    devices_row = lax.axis_size("row")
    blocks_f = devices_row // QUAD
    low_bits = blocks_f.bit_length() - 1
    position = lax.axis_index("row")
    blocks = down_weight.reshape(2, 2, unit_count, quarter)
    for section in range(2):
        bit = low_bits + section
        upper_side = position // (1 << bit) % 2 == 1
        if section == 0:
            lower, upper = (blocks[:, 0], blocks[:, 1])
        else:
            lower, upper = (blocks[0], blocks[1])
        outgoing = jnp.where(upper_side, lower, upper)
        incoming = partner(outgoing, "row", bit)
        new_lower = jnp.where(upper_side, incoming, lower)
        new_upper = jnp.where(upper_side, upper, incoming)
        blocks = jnp.stack([new_lower, new_upper], axis=1 - section)
    own_weight = blocks.transpose(2, 0, 1, 3).reshape(unit_count, QUAD * quarter)
    summed = lax.psum_scatter(
        lax.dot_general(
            own_weight, hidden, (((0,), (1,)), ((), ())), preferred_element_type=jnp.float32
        ),
        "row",
        scatter_dimension=0,
        tiled=True,
    )
    partial_value = summed.T
    stream = partial_value + residual.astype(jnp.float32)
    squares = lax.psum(jnp.sum(stream * stream, axis=1), "row")
    scale = lax.rsqrt(squares / width + 1e-05)
    offset = position * own_cols
    gain_part = lax.dynamic_slice_in_dim(gain, offset, own_cols, 0)
    mixed = stream.astype(jnp.bfloat16)
    normed = (stream * scale[:, None] * gain_part[None, :]).astype(jnp.bfloat16)
    return (mixed, normed)


def solution(mesh):
    return jax.shard_map(
        local,
        mesh=mesh,
        in_specs=(P("groups", "row"), P("groups", "row"), P("groups", "row"), P(), P("row", None)),
        out_specs=(P("groups", "row"), P("groups", "row")),
        check_vma=False,
    )
```

profile of v0, /device:TPU:0, one launch (start us, length us, event | category | flops | bytes accessed | tf_op | source)
XLA Modules:
  0.0 1491.2 jit_solution(13625413478660539172)
XLA Ops:
  7.2 0.0 reduce-scatter.2.cloned.1.call-start
  7.2 17.2 %broadcast_select_fusion = bf16[2,2048,2048]{2,1,0:T(8,128)(2,1)} fusion(pred[]{:T(512)S(6)} %eq.10, bf16[2,2,2048,2048]{3,2,1,0:T(8,128)(2,1)} %bitcast.49), kind=kLoop, calls=%fused_computation.13 | loop fusion | flops 8388608 | bytes 50331648 | tf_op jit(solution)/shard_map/jit(_where)/select_n | solution.py:40
  24.5 3.0 collective-permute-start
  27.5 360.5 %collective-permute-done = bf16[2,2048,2048]{2,1,0:T(8,128)(2,1)} collective-permute-done((bf16[2,2048,2048]{2,1,0:T(8,128)(2,1)}, bf16[2,2048,2048]{2,1,0:T(8,128)(2,1)}, u32[]{:S(2)}, u32[]{:S(2)}) %collective-permute-start) | collective-permute-done | bytes 16777248 | tf_op jit(solution)/shard_map/ppermute | solution.py:13
  388.0 27.5 %select_bitcast_fusion.3 = (bf16[2,1,2048,2048]{3,2,0,1:T(8,128)(2,1)}, bf16[2,1,2048,2048]{3,2,0,1:T(8,128)(2,1)}) fusion(bf16[2,2048,2048]{2,1,0:T(8,128)(2,1)} %collective-permute-done, pred[]{:T(512)S(6)} %eq.10, bf16[2,2,2048,2048]{3,2,1,0:T(8,128)(2,1)} %bitcast.50), kind=kLoop, calls=%fused_computation.12 | loop fusion | flops 16777216 | bytes 83886080 | tf_op jit(solution)/shard_map/stack | solution.py:44
  415.5 12.0 broadcast_select_fusion.1
  427.5 2.8 collective-permute-start.1
  430.3 719.2 %collective-permute-done.1 = bf16[2,2048,2048]{2,1,0:T(8,128)(2,1)} collective-permute-done((bf16[2,2048,2048]{2,1,0:T(8,128)(2,1)S(1)}, bf16[2,2048,2048]{2,1,0:T(8,128)(2,1)}, u32[]{:S(2)}, u32[]{:S(2)}) %collective-permute-start.1) | collective-permute-done | bytes 16777248 | tf_op jit(solution)/shard_map/ppermute | solution.py:13
  1149.5 27.3 %select_bitcast_fusion.1 = (bf16[1,2,2048,2048]{3,2,1,0:T(8,128)(2,1)}, bf16[1,2,2048,2048]{3,2,1,0:T(8,128)(2,1)}) fusion(bf16[2,2048,2048]{2,1,0:T(8,128)(2,1)} %collective-permute-done.1, pred[]{:T(512)S(6)} %eq.9, bf16[2,1,2048,2048]{3,2,0,1:T(8,128)(2,1)} %get-tuple-element.11, bf16[2,1,2048,2048]{3,2,0,1:T(8,128)(2,1)} %get-tuple-element.10), kind=kLoop, calls=%fused_computation.10 | loop fusion | flops 33554432 | bytes 83886080 | tf_op jit(solution)/shard_map/stack | solution.py:44
  1176.9 23.0 %maximum_bitcast_fusion = bf16[2048,2,2,2048]{3,0,2,1:T(8,128)(2,1)} fusion(bf16[1,2,2048,2048]{3,2,1,0:T(8,128)(2,1)} %get-tuple-element.9, bf16[1,2,2048,2048]{3,2,1,0:T(8,128)(2,1)} %get-tuple-element.8), kind=kLoop, calls=%fused_computation.2 | loop fusion | flops 16777216 | bytes 67108864 | tf_op jit(solution)/shard_map/transpose | solution.py:45
  1199.8 0.0 copy-start.1
  1199.8 42.8 %copy.18 = bf16[2048,2,2,2048]{0,3,2,1:T(8,128)(2,1)} copy(bf16[2048,2,2,2048]{3,0,2,1:T(8,128)(2,1)} %maximum_bitcast_fusion) | data formatting | bytes 67108864 | tf_op jit(solution)/shard_map/transpose | solution.py:45
  1242.7 0.0 copy-done.1
  1242.7 25.6 %fusion.8 = f32[8192,512]{1,0:T(8,128)} fusion(bf16[2048,8192]{0,1:T(8,128)(2,1)} %bitcast.51, bf16[512,2048]{1,0:T(8,128)(2,1)S(1)} %copy-done.1, bf16[512,2048]{1,0:T(8,128)(2,1)} %param.5), kind=kOutput, calls=%fused_computation.22 | convolution fusion | flops 17188257792 | bytes 54525952 | tf_op jit(solution)/shard_map/dot_general | solution.py:47
  1268.3 0.0 copy-start
  1268.3 0.0 reduce-scatter.2.cloned.1.call-update
  1268.3 1.0 copy-done
  1269.3 0.2 copy.19
  1269.6 0.8 dynamic_slice.3
  1270.3 177.7 %reduce-scatter.2.cloned.1.call-done = f32[512,512]{1,0:T(8,128)} async-done(((f32[8192,512]{1,0:T(8,128)}), f32[512,512]{1,0:T(8,128)}) %reduce-scatter.2.cloned.1.call-update) | async-done | bytes 1048592 | tf_op jit(solution)/shard_map/reduce_scatter | solution.py:46
  1448.0 1.4 multiply_reduce_fusion
  1449.5 31.5 %psum.7 = f32[512]{0:T(512)S(1)} all-reduce(f32[512]{0:T(512)S(1)} %multiply_reduce_fusion), channel_id=1, replica_groups=mesh['groups'=2,'row'=16] {'row'}, use_global_device_ids=true, to_apply=%region_2.3 | all-reduce | flops 512 | bytes 4096 | tf_op jit(solution)/shard_map/psum | solution.py:56
  1481.0 1.4 multiply_convert_fusion
  1482.4 1.0 copy.20
  1483.4 1.0 copy.21
  (1 shorter events, 0.0 us)
Async XLA Ops:
  7.2 1440.9 %reduce-scatter.2.cloned.1.call-start = ((), (), s32[]{:S(2)}) async-start(), calls=%async_computation.1 | async-start | bytes 17825792 | tf_op jit(solution)/shard_map/reduce_scatter | solution.py:46
  24.5 363.6 %collective-permute-start = (bf16[2,2048,2048]{2,1,0:T(8,128)(2,1)}, bf16[2,2048,2048]{2,1,0:T(8,128)(2,1)}, u32[]{:S(2)}, u32[]{:S(2)}) collective-permute-start(bf16[2,2048,2048]{2,1,0:T(8,128)(2,1)} %broadcast_select_fusion), channel_id=1, source_target_pairs={{0,4},{1,5},{2,6},{3,7},{4,0},{5,1},{6,2},{7,3},{8,12},{9,13},{10,... | collective-permute-start | bytes 50331656 | tf_op jit(solution)/shard_map/ppermute | solution.py:13
  427.5 722.0 %collective-permute-start.1 = (bf16[2,2048,2048]{2,1,0:T(8,128)(2,1)S(1)}, bf16[2,2048,2048]{2,1,0:T(8,128)(2,1)}, u32[]{:S(2)}, u32[]{:S(2)}) collective-permute-start(bf16[2,2048,2048]{2,1,0:T(8,128)(2,1)S(1)} %broadcast_select_fusion.1), channel_id=1, source_target_pairs={{0,8},{1,9},{2,10},{3,11},{4,12},{5,13},{6,14},{7,15},{8,0},{9,1},... | collective-permute-start | bytes 50331656 | tf_op jit(solution)/shard_map/ppermute | solution.py:13
  1199.8 42.9 %copy-start.1 = (bf16[512,2048]{1,0:T(8,128)(2,1)S(1)}, bf16[512,2048]{1,0:T(8,128)(2,1)}, u32[]{:S(2)}) copy-start(bf16[512,2048]{1,0:T(8,128)(2,1)} %param.6) | copy-start | bytes 6291460
  1268.3 1.0 copy-start
Sparse Core Ops, SparseCore 0:
  1268.4 179.5 reduce-scatter.1
where the time goes:
time: 1490 us
  waiting for transfers between devices  1260 us (85%)
  other arithmetic  110 us (7%)
  local copies, waits for them, and re-layouts  46.8 us (3%)
  blocking collectives  31.5 us (2%)
  matrix products  25.6 us (2%)
    ppermute x2, waiting for transfers between devices, partner(): return lax.ppermute(value, axis, pairs)  1080 us
    reduce_scatter x1, waiting for transfers between devices, local(): lax.psum_scatter(lax.dot_general(own_weight, hidden, (((0,), (1,)), ((),...  178 us
    another operation x2, other arithmetic, local(): blocks = jnp.stack([new_lower, new_upper], axis=1 - section)  54.9 us
    transpose x1, local copies, waits for them, and re-layouts, local(): blocks.transpose(2, 0, 1, 3).reshape(unit_count, QUAD * quarter)  42.8 us
    psum x1, blocking collectives, local(): squares = lax.psum(jnp.sum(stream * stream, axis=1), 'row')  31.5 us
  transfers between devices with their start and end apart: 3, of which 3 were waited for; matrix products, arithmetic and copies ran while one was open for 0% of the time, Pallas kernels for 0%

commit v1 on v0

v1 whole, which is shorter than its diff:
```python
import functools

import jax
import jax.numpy as jnp
from jax import lax
from jax.experimental import pallas as pl
from jax.experimental.pallas import tpu as pltpu
from jax.sharding import PartitionSpec as P

QUAD = 4


def gated(gate_pre, up_pre):
    return (jax.nn.silu(gate_pre.astype(jnp.float32)) * up_pre.astype(jnp.float32)).astype(
        jnp.bfloat16
    )


def product_kernel(half, with_total, place, *refs):
    if with_total:
        hidden, weight, total_send, total_keep, send, keep = refs
    else:
        hidden, weight, send, keep = refs
    step = pl.program_id(0)
    value = jnp.dot(hidden[...], weight[...], preferred_element_type=jnp.float32)

    @pl.when(step < half)
    def _():
        send[0] = value + total_send[0] if with_total else value

    @pl.when(step >= half)
    def _():
        keep[0] = value + total_keep[0] if with_total else value


def product(hidden, weight, slot, own, blocks, cols, total=None, token_block=0):
    tokens, units = hidden.shape
    half = blocks // 2

    def first(step):
        return jnp.minimum(step, half - 1)

    def second(step):
        return jnp.maximum(step - half, 0)

    def weight_at(step, place):
        block = jnp.where(step < half, 2 * step + 1, 2 * (step - half))
        return place[0], lax.bitwise_xor(place[1], block)

    in_specs = [
        pl.BlockSpec((tokens, units), lambda step, place: (0, 0)),
        pl.BlockSpec((units, cols), weight_at),
    ]
    operands = [hidden, weight]
    if total is not None:
        in_specs += [
            pl.BlockSpec((1, tokens, cols), lambda step, place: (first(step), token_block, 0)),
            pl.BlockSpec((1, tokens, cols), lambda step, place: (second(step), token_block, 0)),
        ]
        operands += list(total)
    out = jax.ShapeDtypeStruct((half, tokens, cols), jnp.float32)
    return pl.pallas_call(
        functools.partial(product_kernel, half, total is not None),
        grid_spec=pltpu.PrefetchScalarGridSpec(
            num_scalar_prefetch=1,
            grid=(blocks,),
            in_specs=in_specs,
            out_specs=[
                pl.BlockSpec((1, tokens, cols), lambda step, place: (first(step), 0, 0)),
                pl.BlockSpec((1, tokens, cols), lambda step, place: (second(step), 0, 0)),
            ],
        ),
        out_shape=[out, out],
        compiler_params=pltpu.CompilerParams(vmem_limit_bytes=32 * 2**20),
        cost_estimate=pl.CostEstimate(
            flops=2 * tokens * units * blocks * cols,
            bytes_accessed=2 * (units * blocks * cols + tokens * units) + 8 * tokens * blocks * cols,
            transcendentals=0,
        ),
    )(jnp.stack([slot, own]).astype(jnp.int32), *operands)


def local(gate_pre, up_pre, residual, gain, down_weight):
    tokens, units = gate_pre.shape
    cols = residual.shape[1]
    devices = lax.axis_size("row")
    plane = devices // QUAD
    width = devices * cols
    position = lax.axis_index("row")
    layer = position // plane
    own = position % plane
    middle = (layer == 1) | (layer == 2)
    low = layer < 2

    def move(value, pairs):
        return lax.ppermute(
            value, "row", [(s * plane + i, t * plane + i) for s, t in pairs for i in range(plane)]
        )

    def swap(value, bit):
        return lax.ppermute(value, "row", [(i, i ^ (1 << bit)) for i in range(devices)])

    def beside(value):
        return move(value, [(0, 1), (1, 0), (2, 3), (3, 2)])

    def across(value):
        return move(value, [(1, 2), (2, 1)])

    def outward(value):
        return move(value, [(1, 0), (2, 3)])

    mul = functools.partial(product, weight=down_weight, own=own, blocks=plane, cols=cols)

    halves = 2
    quarters = 4
    part = tokens // halves
    fine = tokens // quarters
    hidden = [
        gated(gate_pre[i * part : (i + 1) * part], up_pre[i * part : (i + 1) * part])
        for i in range(halves)
    ]
    near = [beside(v) for v in hidden]
    mid = [across(v) for v in hidden]
    mid_out = [outward(v) for v in mid]
    far = [across(v) for v in near]
    far_out = [
        outward(v[i * fine : (i + 1) * fine]) for v in far for i in range(quarters // halves)
    ]

    other_mid = jnp.where(low, 2, 1)
    other_end = jnp.where(low, 3, 0)
    done = []
    for i in range(halves):
        total = mul(hidden[i], slot=layer)
        total = mul(near[i], slot=layer ^ 1, total=total)
        total = mul(jnp.where(middle, mid[i], mid_out[i]), slot=other_mid, total=total)
        for j in range(quarters // halves):
            piece = jnp.where(
                middle, far[i][j * fine : (j + 1) * fine], far_out[i * (quarters // halves) + j]
            )
            done.append(mul(piece, slot=other_end, total=total, token_block=j))

    plane_bits = plane.bit_length() - 1
    all_bits = devices.bit_length() - 1
    streams = []
    for j, (send, keep) in enumerate(done):
        value = keep + swap(send, 0)
        for bit in range(1, plane_bits):
            value = value.reshape(-1, 2, fine, cols)
            value = value[:, 0] + swap(value[:, 1], bit)
        streams.append(value[0] + residual[j * fine : (j + 1) * fine].astype(jnp.float32))
    squares = jnp.concatenate([jnp.sum(s * s, axis=1) for s in streams])
    for bit in range(all_bits):
        squares = squares + swap(squares, bit)
    scale = lax.rsqrt(squares / width + 1e-05)
    gain_part = lax.dynamic_slice_in_dim(gain, position * cols, cols, 0)
    stream = jnp.concatenate(streams)
    mixed = stream.astype(jnp.bfloat16)
    normed = (stream * scale[:, None] * gain_part[None, :]).astype(jnp.bfloat16)
    return (mixed, normed)


def solution(mesh):
    return jax.shard_map(
        local,
        mesh=mesh,
        in_specs=(P("groups", "row"), P("groups", "row"), P("groups", "row"), P(), P("row", None)),
        out_specs=(P("groups", "row"), P("groups", "row")),
        check_vma=False,
    )
```

time: 1490 us -> 193 us (0.13)
  waiting for transfers between devices: 1260 us -> 82.2 us
  other arithmetic: 110 us -> 13.7 us
  Pallas kernels: 0 us -> 59.7 us
  local copies, waits for them, and re-layouts: 46.8 us -> 7.55 us
  blocking collectives: 31.5 us -> 0 us
  matrix products: 25.6 us -> 0 us
  starting transfers between devices: 5.88 us -> 28.1 us
    ppermute x2 -> x24, waiting for transfers between devices: 1080 us -> 82.2 us  [the longest x12 57.5 us: move(): lax.ppermute(value, 'row', [(s * plane + i, t * plane + i) for s, t in pa...]
    reduce_scatter x1 -> x0, waiting for transfers between devices: 178 us -> none  [local(): lax.psum_scatter(lax.dot_general(own_weight, hidden, (((0,), (1,)), ((),...]
    pallas_call x0 -> x10, Pallas kernels: none -> 59.7 us  [product(): pl.pallas_call(functools.partial(product_kernel, half, total is not None)...]
    another operation x2 -> x4, other arithmetic: 54.9 us -> 0.3 us  [product(): jnp.stack([slot, own]).astype(jnp.int32)]
    transpose x1 -> x0, local copies, waits for them, and re-layouts: 42.8 us -> none  [local(): blocks.transpose(2, 0, 1, 3).reshape(unit_count, QUAD * quarter)]
    psum x1 -> x0, blocking collectives: 31.5 us -> none  [local(): squares = lax.psum(jnp.sum(stream * stream, axis=1), 'row')]
    dot_general x1 -> x0, matrix products: 25.6 us -> none  [local(): lax.dot_general(own_weight, hidden, (((0,), (1,)), ((), ())), preferred_e...]
    transpose x1 -> x0, other arithmetic: 23 us -> none  [local(): blocks.transpose(2, 0, 1, 3).reshape(unit_count, QUAD * quarter)]
  transfers between devices with their start and end apart: 3 -> 24, of which waited for: 3 -> 12; matrix products, arithmetic and copies ran while one was open for 0% -> 6% of each run, Pallas kernels for 0% -> 31%
where the time goes in v1:
time: 193 us; the launch traced here: 192 us
  waiting for transfers between devices  82.2 us (43%)
  Pallas kernels  59.7 us (31%)
  starting transfers between devices  28.1 us (15%)
  other arithmetic  13.7 us (7%)
  local copies, waits for them, and re-layouts  7.55 us (4%)
    pallas_call x10, Pallas kernels, product(): pl.pallas_call(functools.partial(product_kernel, half, total is not None)...  59.7 us
    ppermute x12, waiting for transfers between devices, move(): lax.ppermute(value, 'row', [(s * plane + i, t * plane + i) for s, t in pa...  57.5 us
    ppermute x12, waiting for transfers between devices, swap(): lax.ppermute(value, 'row', [(i, i ^ 1 << bit) for i in range(devices)])  24.7 us
    ppermute x12, starting transfers between devices, move(): lax.ppermute(value, 'row', [(s * plane + i, t * plane + i) for s, t in pa...  19.3 us
    ppermute x12, starting transfers between devices, swap(): lax.ppermute(value, 'row', [(i, i ^ 1 << bit) for i in range(devices)])  8.76 us
    select_n x4, other arithmetic, local(): jnp.where(middle, far[i][j * fine:(j + 1) * fine], far_out[i * (quarters...  4.82 us
    unnamed x14, local copies, waits for them, and re-layouts  4.56 us
  transfers between devices with their start and end apart: 24, of which 12 were waited for; matrix products, arithmetic and copies ran while one was open for 6% of the time, Pallas kernels for 31%

profile of v1, /device:TPU:0, one launch (start us, length us, event | category | flops | bytes accessed | tf_op | source)
XLA Modules:
  0.0 192.2 jit_solution(18188863827932883113)
XLA Ops:
  0.6 3.5 %fusion.9 = (bf16[256,2048]{1,0:T(8,128)(2,1)S(1)}, bf16[256,2048]{1,0:T(8,128)(2,1)S(1)}) fusion(bf16[512,2048]{1,0:T(8,128)(2,1)} %param.6, bf16[512,2048]{1,0:T(8,128)(2,1)} %param.5), kind=kLoop, calls=%fused_computation.13 | loop fusion | flops 8388608 | bytes 6291456 | tf_op jit(solution)/shard_map/convert_element_type | solution.py:14
  4.1 1.6 collective-permute-start.13
  5.8 4.9 %collective-permute-start.10 = (bf16[256,2048]{1,0:T(8,128)(2,1)S(1)}, bf16[256,2048]{1,0:T(8,128)(2,1)}, u32[]{:S(2)}, u32[]{:S(2)}) collective-permute-start(bf16[256,2048]{1,0:T(8,128)(2,1)S(1)} %get-tuple-element.51.refs_0_), channel_id=1, source_target_pairs={{0,4},{1,5},{2,6},{3,7},{4,0},{5,1},{6,2},{7,3},{8,12},{9,13},{10,... | collective-permute-start | bytes 3145736 | tf_op jit(solution)/shard_map/ppermute | solution.py:96
  10.7 0.1 collective-permute-start
  10.8 1.6 collective-permute-start.3
  12.4 0.1 pad_add_fusion.3.place
  12.5 1.3 collective-permute-start.14
  13.8 21.1 %collective-permute-done.10.refs_0_ = bf16[256,2048]{1,0:T(8,128)(2,1)} collective-permute-done((bf16[256,2048]{1,0:T(8,128)(2,1)S(1)}, bf16[256,2048]{1,0:T(8,128)(2,1)}, u32[]{:S(2)}, u32[]{:S(2)}) %collective-permute-start.10) | collective-permute-done | bytes 1048608 | tf_op jit(solution)/shard_map/ppermute | solution.py:96
  34.9 1.6 collective-permute-start.11
  36.5 20.7 %collective-permute-done.refs_0_ = bf16[256,2048]{1,0:T(8,128)(2,1)S(1)} collective-permute-done((bf16[256,2048]{1,0:T(8,128)(2,1)S(1)}, bf16[256,2048]{1,0:T(8,128)(2,1)S(1)}, u32[]{:S(2)}, u32[]{:S(2)}) %collective-permute-start) | collective-permute-done | bytes 1048608 | tf_op jit(solution)/shard_map/ppermute | solution.py:96
  57.2 1.6 collective-permute-start.1
  58.9 6.1 %shard_map.73 = (f32[2,256,512]{2,1,0:T(8,128)S(1)}, f32[2,256,512]{2,1,0:T(8,128)S(1)}) custom-call(s32[2]{0:T(128)S(1)} %pad_add_fusion.3.place, bf16[256,2048]{1,0:T(8,128)(2,1)S(1)} %get-tuple-element.51.refs_0_, bf16[8192,2048]{1,0:T(8,128)(2,1)} %refs_1_.19), custom_call_target="tpu_custom_call" | custom-call | flops 2147483648 | bytes 13631488 | tf_op jit(solution)/shard_map/pallas_call | solution.py:62
  65.1 1.0 copy-done.2
  66.1 6.1 %shard_map.68 = (f32[2,256,512]{2,1,0:T(8,128)S(1)}, f32[2,256,512]{2,1,0:T(8,128)S(1)}) custom-call(s32[2]{0:T(128)S(1)} %pad_add_fusion.3.place, bf16[256,2048]{1,0:T(8,128)(2,1)S(1)} %get-tuple-element.50.refs_0_, bf16[8192,2048]{1,0:T(8,128)(2,1)} %refs_1_.19), custom_call_target="tpu_custom_call" | custom-call | flops 2147483648 | bytes 13631488 | tf_op jit(solution)/shard_map/pallas_call | solution.py:62
  72.3 1.1 copy-done
  73.3 1.3 collective-permute-start.4
  74.6 0.1 pad_add_fusion.1.place
  74.8 1.2 copy-done.3
  76.0 1.2 copy-done.5
  77.2 6.5 %shard_map.74 = (f32[2,256,512]{2,1,0:T(8,128)S(1)}, f32[2,256,512]{2,1,0:T(8,128)S(1)}) custom-call(s32[2]{0:T(128)S(1)} %pad_add_fusion.2.place, bf16[256,2048]{1,0:T(8,128)(2,1)} %collective-permute-done.10.refs_0_, bf16[8192,2048]{1,0:T(8,128)(2,1)} %refs_1_.19, f32[2,256,512]{2,1,0:T(8,128)S(1)} %copy-done.3, f32[2,256,512]{2,1,0:T(8,128)S(1)} %copy-done.5), custom_call_target="tpu_custom_call" | custom-call | flops 2147483648 | bytes 13631488 | tf_op jit(solution)/shard_map/pallas_call | solution.py:62
  83.8 6.2 %shard_map.69 = (f32[2,256,512]{2,1,0:T(8,128)S(1)}, f32[2,256,512]{2,1,0:T(8,128)S(1)}) custom-call(s32[2]{0:T(128)S(1)} %pad_add_fusion.2.place, bf16[256,2048]{1,0:T(8,128)(2,1)S(1)} %collective-permute-done.refs_0_, bf16[8192,2048]{1,0:T(8,128)(2,1)} %refs_1_.19, f32[2,256,512]{2,1,0:T(8,128)S(1)} %get-tuple-element.22.refs_2_, f32[2,256,512]{2,1,0:T(8,128)S(1)} %copy-done.1), custom_call_target="tpu_custom_call" | custom-call | flops 2147483648 | bytes 13631488 | tf_op jit(solution)/shard_map/pallas_call | solution.py:62
  90.0 1.1 slice.90
  91.1 1.3 collective-permute-start.12
  92.4 1.1 slice.84
  93.5 1.3 collective-permute-start.2
  94.8 1.4 broadcast_select_fusion.refs_0_
  96.2 6.1 %collective-permute-done.4 = bf16[256,2048]{1,0:T(8,128)(2,1)} collective-permute-done((bf16[256,2048]{1,0:T(8,128)(2,1)}, bf16[256,2048]{1,0:T(8,128)(2,1)}, u32[]{:S(2)}, u32[]{:S(2)}) %collective-permute-start.4) | collective-permute-done | bytes 1048608 | tf_op jit(solution)/shard_map/ppermute | solution.py:96
  102.3 1.3 broadcast_select_fusion.1.refs_0_
  103.6 6.3 %shard_map.75 = (f32[2,256,512]{2,1,0:T(8,128)S(1)}, f32[2,256,512]{2,1,0:T(8,128)S(1)}) custom-call(s32[2]{0:T(128)S(1)} %pad_add_fusion.1.place, bf16[256,2048]{1,0:T(8,128)(2,1)S(1)} %broadcast_select_fusion.refs_0_, bf16[8192,2048]{1,0:T(8,128)(2,1)} %refs_1_.19, f32[2,256,512]{2,1,0:T(8,128)S(1)} %get-tuple-element.34.refs_2_, ...), custom_call_target="tpu_custom_call" | custom-call | flops 2147483648 | bytes 13631488 | tf_op jit(solution)/shard_map/pallas_call | solution.py:62
  109.9 6.3 %shard_map.70 = (f32[2,256,512]{2,1,0:T(8,128)S(1)}, f32[2,256,512]{2,1,0:T(8,128)S(1)}) custom-call(s32[2]{0:T(128)S(1)} %pad_add_fusion.1.place, bf16[256,2048]{1,0:T(8,128)(2,1)S(1)} %broadcast_select_fusion.1.refs_0_, bf16[8192,2048]{1,0:T(8,128)(2,1)} %refs_1_.19, f32[2,256,512]{2,1,0:T(8,128)S(1)} %get-tuple-element.24.refs_2_, ...), custom_call_target="tpu_custom_call" | custom-call | flops 2147483648 | bytes 13631488 | tf_op jit(solution)/shard_map/pallas_call | solution.py:62
  116.2 1.3 broadcast_select_fusion.3
  117.5 5.5 %shard_map.76 = (f32[2,128,512]{2,1,0:T(8,128)S(1)}, f32[2,128,512]{2,1,0:T(8,128)S(1)}) custom-call(s32[2]{0:T(128)S(1)} %pad_add_fusion.place, bf16[128,2048]{1,0:T(8,128)(2,1)S(1)} %get-tuple-element.54.refs_0_, bf16[8192,2048]{1,0:T(8,128)(2,1)} %refs_1_.19, f32[2,256,512]{2,1,0:T(8,128)S(1)} %get-tuple-element.36.refs_2_, ...), custom_call_target="tpu_custom_call" | custom-call | flops 1073741824 | bytes 11010048 | tf_op jit(solution)/shard_map/pallas_call | solution.py:62
  123.1 1.3 collective-permute-start.17
  124.4 1.3 broadcast_select_fusion.5
  125.7 1.3 collective-permute-start.7
  127.0 5.5 %shard_map.71 = (f32[2,128,512]{2,1,0:T(8,128)S(1)}, f32[2,128,512]{2,1,0:T(8,128)S(1)}) custom-call(s32[2]{0:T(128)S(1)} %pad_add_fusion.place, bf16[128,2048]{1,0:T(8,128)(2,1)S(1)} %get-tuple-element.52.refs_0_, bf16[8192,2048]{1,0:T(8,128)(2,1)} %refs_1_.19, f32[2,256,512]{2,1,0:T(8,128)S(1)} %get-tuple-element.26.refs_2_, ...), custom_call_target="tpu_custom_call" | custom-call | flops 1073741824 | bytes 11010048 | tf_op jit(solution)/shard_map/pallas_call | solution.py:62
  132.6 0.6 collective-permute-start.5
  133.1 0.1 add_bitcast_fusion.1
  133.2 1.6 collective-permute-start.16
  134.8 5.3 %collective-permute-done.17 = bf16[128,2048]{1,0:T(8,128)(2,1)S(1)} collective-permute-done((bf16[128,2048]{1,0:T(8,128)(2,1)S(1)}, bf16[128,2048]{1,0:T(8,128)(2,1)S(1)}, u32[]{:S(2)}, u32[]{:S(2)}) %collective-permute-start.17) | collective-permute-done | bytes 524320 | tf_op jit(solution)/shard_map/ppermute | solution.py:96
  140.2 1.1 broadcast_select_fusion.2.refs_0_
  141.3 5.5 %shard_map.77 = (f32[2,128,512]{2,1,0:T(8,128)S(1)}, f32[2,128,512]{2,1,0:T(8,128)S(1)}) custom-call(s32[2]{0:T(128)S(1)} %pad_add_fusion.place, bf16[128,2048]{1,0:T(8,128)(2,1)S(1)} %broadcast_select_fusion.2.refs_0_, bf16[8192,2048]{1,0:T(8,128)(2,1)} %refs_1_.19, f32[2,256,512]{2,1,0:T(8,128)S(1)} %get-tuple-element.36.refs_2_, ...), custom_call_target="tpu_custom_call" | custom-call | flops 1073741824 | bytes 11010048 | tf_op jit(solution)/shard_map/pallas_call | solution.py:62
  146.9 4.3 %collective-permute-done.7 = bf16[128,2048]{1,0:T(8,128)(2,1)S(1)} collective-permute-done((bf16[128,2048]{1,0:T(8,128)(2,1)S(1)}, bf16[128,2048]{1,0:T(8,128)(2,1)S(1)}, u32[]{:S(2)}, u32[]{:S(2)}) %collective-permute-start.7) | collective-permute-done | bytes 524320 | tf_op jit(solution)/shard_map/ppermute | solution.py:96
  151.2 1.1 broadcast_select_fusion.4.refs_0_
  152.3 5.5 %shard_map.72 = (f32[2,128,512]{2,1,0:T(8,128)S(1)}, f32[2,128,512]{2,1,0:T(8,128)S(1)}) custom-call(s32[2]{0:T(128)S(1)} %pad_add_fusion.place, bf16[128,2048]{1,0:T(8,128)(2,1)S(1)} %broadcast_select_fusion.4.refs_0_, bf16[8192,2048]{1,0:T(8,128)(2,1)} %refs_1_.19, f32[2,256,512]{2,1,0:T(8,128)S(1)} %get-tuple-element.26.refs_2_, ...), custom_call_target="tpu_custom_call" | custom-call | flops 1073741824 | bytes 11010048 | tf_op jit(solution)/shard_map/pallas_call | solution.py:62
  158.0 0.1 add_bitcast_fusion.3
  158.1 1.6 collective-permute-start.6
  159.7 0.1 add_bitcast_fusion
  159.8 0.6 collective-permute-start.19
  160.3 0.1 add_bitcast_fusion.2
  160.5 1.6 collective-permute-start.9
  162.0 5.2 %collective-permute-done.6 = f32[1,128,512]{2,1,0:T(8,128)S(1)} collective-permute-done((f32[1,128,512]{2,1,0:T(8,128)S(1)}, f32[1,128,512]{2,1,0:T(8,128)S(1)}, u32[]{:S(2)}, u32[]{:S(2)}) %collective-permute-start.6) | collective-permute-done | bytes 262176 | tf_op jit(solution)/shard_map/ppermute | solution.py:101
  167.2 5.6 %collective-permute-done.19 = f32[1,128,512]{2,1,0:T(8,128)S(1)} collective-permute-done((f32[1,128,512]{2,1,0:T(8,128)S(1)}, f32[1,128,512]{2,1,0:T(8,128)S(1)}, u32[]{:S(2)}, u32[]{:S(2)}) %collective-permute-start.19) | collective-permute-done | bytes 262176 | tf_op jit(solution)/shard_map/ppermute | solution.py:101
  172.9 5.2 %collective-permute-done.9 = f32[1,128,512]{2,1,0:T(8,128)S(1)} collective-permute-done((f32[1,128,512]{2,1,0:T(8,128)S(1)}, f32[1,128,512]{2,1,0:T(8,128)S(1)}, u32[]{:S(2)}, u32[]{:S(2)}) %collective-permute-start.9) | collective-permute-done | bytes 262176 | tf_op jit(solution)/shard_map/ppermute | solution.py:101
  178.1 0.2 multiply_reduce_fusion.3
  178.4 1.1 collective-permute-done.20
  179.6 1.6 collective-permute-start.21
  181.1 2.1 %collective-permute-done.21 = f32[512]{0:T(512)S(1)} collective-permute-done((f32[512]{0:T(512)S(1)}, f32[512]{0:T(512)S(1)}, u32[]{:S(2)}, u32[]{:S(2)}) %collective-permute-start.21) | collective-permute-done | bytes 2080 | tf_op jit(solution)/shard_map/ppermute | solution.py:101
  183.2 0.8 dynamic_slice.3
  184.0 2.8 %collective-permute-done.22 = f32[512]{0:T(512)S(1)} collective-permute-done((f32[512]{0:T(512)S(1)}, f32[512]{0:T(512)S(1)}, u32[]{:S(2)}, u32[]{:S(2)}) %collective-permute-start.22) | collective-permute-done | bytes 2080 | tf_op jit(solution)/shard_map/ppermute | solution.py:101
  186.8 1.0 collective-permute-start.23
  187.8 0.9 fusion.10
  188.7 2.6 %collective-permute-done.23 = f32[512]{0:T(512)S(1)} collective-permute-done((f32[512]{0:T(512)S(1)}, f32[512]{0:T(512)S(1)}, u32[]{:S(2)}, u32[]{:S(2)}) %collective-permute-start.23) | collective-permute-done | bytes 2080 | tf_op jit(solution)/shard_map/ppermute | solution.py:101
  191.3 1.0 multiply_convert_fusion
  (38 shorter events, 0.6 us)
Async XLA Ops:
  4.1 8.4 %collective-permute-start.13 = (bf16[256,2048]{1,0:T(8,128)(2,1)S(1)}, bf16[256,2048]{1,0:T(8,128)(2,1)}, u32[]{:S(2)}, u32[]{:S(2)}) collective-permute-start(bf16[256,2048]{1,0:T(8,128)(2,1)S(1)} %get-tuple-element.51.refs_0_), channel_id=1, source_target_pairs={{4,8},{5,9},{6,10},{7,11},{8,4},{9,5},{10,6},{11,7},{20,24},{21,25... | collective-permute-start | bytes 3145736 | tf_op jit(solution)/shard_map/ppermute | solution.py:96
  5.8 29.1 %collective-permute-start.10 = (bf16[256,2048]{1,0:T(8,128)(2,1)S(1)}, bf16[256,2048]{1,0:T(8,128)(2,1)}, u32[]{:S(2)}, u32[]{:S(2)}) collective-permute-start(bf16[256,2048]{1,0:T(8,128)(2,1)S(1)} %get-tuple-element.51.refs_0_), channel_id=1, source_target_pairs={{0,4},{1,5},{2,6},{3,7},{4,0},{5,1},{6,2},{7,3},{8,12},{9,13},{10,... | collective-permute-start | bytes 3145736 | tf_op jit(solution)/shard_map/ppermute | solution.py:96
  10.7 46.5 %collective-permute-start = (bf16[256,2048]{1,0:T(8,128)(2,1)S(1)}, bf16[256,2048]{1,0:T(8,128)(2,1)S(1)}, u32[]{:S(2)}, u32[]{:S(2)}) collective-permute-start(bf16[256,2048]{1,0:T(8,128)(2,1)S(1)} %get-tuple-element.50.refs_0_), channel_id=1, source_target_pairs={{0,4},{1,5},{2,6},{3,7},{4,0},{5,1},{6,2},{7,3},{8,12},{9,13},{10,... | collective-permute-start | bytes 3145736 | tf_op jit(solution)/shard_map/ppermute | solution.py:96
  10.8 62.5 %collective-permute-start.3 = (bf16[256,2048]{1,0:T(8,128)(2,1)S(1)}, bf16[256,2048]{1,0:T(8,128)(2,1)}, u32[]{:S(2)}, u32[]{:S(2)}) collective-permute-start(bf16[256,2048]{1,0:T(8,128)(2,1)S(1)} %get-tuple-element.50.refs_0_), channel_id=1, source_target_pairs={{4,8},{5,9},{6,10},{7,11},{8,4},{9,5},{10,6},{11,7},{20,24},{21,25... | collective-permute-start | bytes 3145736 | tf_op jit(solution)/shard_map/ppermute | solution.py:96
  12.5 82.3 %collective-permute-start.14 = (bf16[256,2048]{1,0:T(8,128)(2,1)}, bf16[256,2048]{1,0:T(8,128)(2,1)}, u32[]{:S(2)}, u32[]{:S(2)}) collective-permute-start(bf16[256,2048]{1,0:T(8,128)(2,1)} %collective-permute-done.13), channel_id=1, source_target_pairs={{4,0},{5,1},{6,2},{7,3},{8,12},{9,13},{10,14},{11,15},{20,16},{21,... | collective-permute-start | bytes 3145736 | tf_op jit(solution)/shard_map/ppermute | solution.py:96
  34.9 55.1 %collective-permute-start.11 = (bf16[256,2048]{1,0:T(8,128)(2,1)}, bf16[256,2048]{1,0:T(8,128)(2,1)}, u32[]{:S(2)}, u32[]{:S(2)}) collective-permute-start(bf16[256,2048]{1,0:T(8,128)(2,1)} %collective-permute-done.10.refs_0_), channel_id=1, source_target_pairs={{4,8},{5,9},{6,10},{7,11},{8,4},{9,5},{10,6},{11,7},{20,24},{21,25... | collective-permute-start | bytes 3145736 | tf_op jit(solution)/shard_map/ppermute | solution.py:96
  57.2 35.2 %collective-permute-start.1 = (bf16[256,2048]{1,0:T(8,128)(2,1)S(1)}, bf16[256,2048]{1,0:T(8,128)(2,1)}, u32[]{:S(2)}, u32[]{:S(2)}) collective-permute-start(bf16[256,2048]{1,0:T(8,128)(2,1)S(1)} %collective-permute-done.refs_0_), channel_id=1, source_target_pairs={{4,8},{5,9},{6,10},{7,11},{8,4},{9,5},{10,6},{11,7},{20,24},{21,25... | collective-permute-start | bytes 3145736 | tf_op jit(solution)/shard_map/ppermute | solution.py:96
  65.1 1.0 copy-start.2
  66.1 6.1 %copy-start.4 = (f32[2,256,512]{2,1,0:T(8,128)}, f32[2,256,512]{2,1,0:T(8,128)S(1)}, u32[]{:S(2)}) copy-start(f32[2,256,512]{2,1,0:T(8,128)S(1)} %get-tuple-element.33.refs_3_) | copy-start | bytes 3145732
  72.3 1.1 copy-start
  73.3 28.9 %collective-permute-start.4 = (bf16[256,2048]{1,0:T(8,128)(2,1)}, bf16[256,2048]{1,0:T(8,128)(2,1)}, u32[]{:S(2)}, u32[]{:S(2)}) collective-permute-start(bf16[256,2048]{1,0:T(8,128)(2,1)} %collective-permute-done.3), channel_id=1, source_target_pairs={{4,0},{5,1},{6,2},{7,3},{8,12},{9,13},{10,14},{11,15},{20,16},{21,... | collective-permute-start | bytes 3145736 | tf_op jit(solution)/shard_map/ppermute | solution.py:96
  74.8 1.2 copy-start.3
  76.0 1.2 copy-start.5
  77.2 6.5 %copy-start.1 = (f32[2,256,512]{2,1,0:T(8,128)S(1)}, f32[2,256,512]{2,1,0:T(8,128)}, u32[]{:S(2)}) copy-start(f32[2,256,512]{2,1,0:T(8,128)} %copy-done) | copy-start | bytes 3145732
  91.1 25.1 %collective-permute-start.12 = (bf16[128,2048]{1,0:T(8,128)(2,1)S(1)}, bf16[128,2048]{1,0:T(8,128)(2,1)S(1)}, u32[]{:S(2)}, u32[]{:S(2)}) collective-permute-start(bf16[128,2048]{1,0:T(8,128)(2,1)S(1)} %slice.90), channel_id=1, source_target_pairs={{4,0},{5,1},{6,2},{7,3},{8,12},{9,13},{10,14},{11,15},{20,16},{21,... | collective-permute-start | bytes 1572872 | tf_op jit(solution)/shard_map/ppermute | solution.py:96
  93.5 30.9 %collective-permute-start.2 = (bf16[128,2048]{1,0:T(8,128)(2,1)S(1)}, bf16[128,2048]{1,0:T(8,128)(2,1)S(1)}, u32[]{:S(2)}, u32[]{:S(2)}) collective-permute-start(bf16[128,2048]{1,0:T(8,128)(2,1)S(1)} %slice.84), channel_id=1, source_target_pairs={{4,0},{5,1},{6,2},{7,3},{8,12},{9,13},{10,14},{11,15},{20,16},{21,... | collective-permute-start | bytes 1572872 | tf_op jit(solution)/shard_map/ppermute | solution.py:96
  123.0 10.1 %collective-permute-start.15 = (f32[2,128,512]{2,1,0:T(8,128)S(1)}, f32[2,128,512]{2,1,0:T(8,128)S(1)}, u32[]{:S(2)}, u32[]{:S(2)}) collective-permute-start(f32[2,128,512]{2,1,0:T(8,128)S(1)} %get-tuple-element.39), channel_id=1, source_target_pairs={{0,1},{1,0},{2,3},{3,2},{4,5},{5,4},{6,7},{7,6},{8,9},{9,8},{10,11... | collective-permute-start | bytes 1572872 | tf_op jit(solution)/shard_map/ppermute | solution.py:101
  123.1 17.1 %collective-permute-start.17 = (bf16[128,2048]{1,0:T(8,128)(2,1)S(1)}, bf16[128,2048]{1,0:T(8,128)(2,1)S(1)}, u32[]{:S(2)}, u32[]{:S(2)}) collective-permute-start(bf16[128,2048]{1,0:T(8,128)(2,1)S(1)} %get-tuple-element.55), channel_id=1, source_target_pairs={{4,0},{5,1},{6,2},{7,3},{8,12},{9,13},{10,14},{11,15},{20,16},{21,... | collective-permute-start | bytes 1572872 | tf_op jit(solution)/shard_map/ppermute | solution.py:96
  125.7 25.5 %collective-permute-start.7 = (bf16[128,2048]{1,0:T(8,128)(2,1)S(1)}, bf16[128,2048]{1,0:T(8,128)(2,1)S(1)}, u32[]{:S(2)}, u32[]{:S(2)}) collective-permute-start(bf16[128,2048]{1,0:T(8,128)(2,1)S(1)} %get-tuple-element.53), channel_id=1, source_target_pairs={{4,0},{5,1},{6,2},{7,3},{8,12},{9,13},{10,14},{11,15},{20,16},{21,... | collective-permute-start | bytes 1572872 | tf_op jit(solution)/shard_map/ppermute | solution.py:96
  132.6 25.4 %collective-permute-start.5 = (f32[2,128,512]{2,1,0:T(8,128)S(1)}, f32[2,128,512]{2,1,0:T(8,128)S(1)}, u32[]{:S(2)}, u32[]{:S(2)}) collective-permute-start(f32[2,128,512]{2,1,0:T(8,128)S(1)} %get-tuple-element.29), channel_id=1, source_target_pairs={{0,1},{1,0},{2,3},{3,2},{4,5},{5,4},{6,7},{7,6},{8,9},{9,8},{10,11... | collective-permute-start | bytes 1572872 | tf_op jit(solution)/shard_map/ppermute | solution.py:101
  133.2 28.8 %collective-permute-start.16 = (f32[1,128,512]{2,1,0:T(8,128)S(1)}, f32[1,128,512]{2,1,0:T(8,128)S(1)}, u32[]{:S(2)}, u32[]{:S(2)}) collective-permute-start(f32[1,128,512]{2,1,0:T(8,128)S(1)} %slice_bitcast_fusion.2), channel_id=1, source_target_pairs={{0,2},{1,3},{2,0},{3,1},{4,6},{5,7},{6,4},{7,5},{8,10},{9,11},{10,... | collective-permute-start | bytes 786440 | tf_op jit(solution)/shard_map/ppermute | solution.py:101
  146.8 12.8 %collective-permute-start.18 = (f32[2,128,512]{2,1,0:T(8,128)S(1)}, f32[2,128,512]{2,1,0:T(8,128)S(1)}, u32[]{:S(2)}, u32[]{:S(2)}) collective-permute-start(f32[2,128,512]{2,1,0:T(8,128)S(1)} %get-tuple-element.41), channel_id=1, source_target_pairs={{0,1},{1,0},{2,3},{3,2},{4,5},{5,4},{6,7},{7,6},{8,9},{9,8},{10,11... | collective-permute-start | bytes 1572872 | tf_op jit(solution)/shard_map/ppermute | solution.py:101
  157.9 2.5 %collective-permute-start.8 = (f32[2,128,512]{2,1,0:T(8,128)S(1)}, f32[2,128,512]{2,1,0:T(8,128)S(1)}, u32[]{:S(2)}, u32[]{:S(2)}) collective-permute-start(f32[2,128,512]{2,1,0:T(8,128)S(1)} %get-tuple-element.31), channel_id=1, source_target_pairs={{0,1},{1,0},{2,3},{3,2},{4,5},{5,4},{6,7},{7,6},{8,9},{9,8},{10,11... | collective-permute-start | bytes 1572872 | tf_op jit(solution)/shard_map/ppermute | solution.py:101
  158.1 9.2 %collective-permute-start.6 = (f32[1,128,512]{2,1,0:T(8,128)S(1)}, f32[1,128,512]{2,1,0:T(8,128)S(1)}, u32[]{:S(2)}, u32[]{:S(2)}) collective-permute-start(f32[1,128,512]{2,1,0:T(8,128)S(1)} %slice_bitcast_fusion.6), channel_id=1, source_target_pairs={{0,2},{1,3},{2,0},{3,1},{4,6},{5,7},{6,4},{7,5},{8,10},{9,11},{10,... | collective-permute-start | bytes 786440 | tf_op jit(solution)/shard_map/ppermute | solution.py:101
  159.7 18.4 %copy-start.6 = (bf16[512,512]{1,0:T(8,128)(2,1)S(1)}, bf16[512,512]{1,0:T(8,128)(2,1)}, u32[]{:S(2)}) copy-start(bf16[512,512]{1,0:T(8,128)(2,1)} %param.7) | copy-start | bytes 1572868
  159.8 13.1 %collective-permute-start.19 = (f32[1,128,512]{2,1,0:T(8,128)S(1)}, f32[1,128,512]{2,1,0:T(8,128)S(1)}, u32[]{:S(2)}, u32[]{:S(2)}) collective-permute-start(f32[1,128,512]{2,1,0:T(8,128)S(1)} %slice_bitcast_fusion), channel_id=1, source_target_pairs={{0,2},{1,3},{2,0},{3,1},{4,6},{5,7},{6,4},{7,5},{8,10},{9,11},{10,... | collective-permute-start | bytes 786440 | tf_op jit(solution)/shard_map/ppermute | solution.py:101
  160.5 17.6 %collective-permute-start.9 = (f32[1,128,512]{2,1,0:T(8,128)S(1)}, f32[1,128,512]{2,1,0:T(8,128)S(1)}, u32[]{:S(2)}, u32[]{:S(2)}) collective-permute-start(f32[1,128,512]{2,1,0:T(8,128)S(1)} %slice_bitcast_fusion.4), channel_id=1, source_target_pairs={{0,2},{1,3},{2,0},{3,1},{4,6},{5,7},{6,4},{7,5},{8,10},{9,11},{10,... | collective-permute-start | bytes 786440 | tf_op jit(solution)/shard_map/ppermute | solution.py:101
  178.3 1.2 collective-permute-start.20
  179.6 3.7 %collective-permute-start.21 = (f32[512]{0:T(512)S(1)}, f32[512]{0:T(512)S(1)}, u32[]{:S(2)}, u32[]{:S(2)}) collective-permute-start(f32[512]{0:T(512)S(1)} %fusion.23), channel_id=1, source_target_pairs={{0,2},{1,3},{2,0},{3,1},{4,6},{5,7},{6,4},{7,5},{8,10},{9,11},{10,... | collective-permute-start | bytes 6152 | tf_op jit(solution)/shard_map/ppermute | solution.py:101
  183.2 3.6 %collective-permute-start.22 = (f32[512]{0:T(512)S(1)}, f32[512]{0:T(512)S(1)}, u32[]{:S(2)}, u32[]{:S(2)}) collective-permute-start(f32[512]{0:T(512)S(1)} %add.85), channel_id=1, source_target_pairs={{0,4},{1,5},{2,6},{3,7},{4,0},{5,1},{6,2},{7,3},{8,12},{9,13},{10,... | collective-permute-start | bytes 6152 | tf_op jit(solution)/shard_map/ppermute | solution.py:101
  186.8 4.5 %collective-permute-start.23 = (f32[512]{0:T(512)S(1)}, f32[512]{0:T(512)S(1)}, u32[]{:S(2)}, u32[]{:S(2)}) collective-permute-start(f32[512]{0:T(512)S(1)} %add.86), channel_id=1, source_target_pairs={{0,8},{1,9},{2,10},{3,11},{4,12},{5,13},{6,14},{7,15},{8,0},{9,1},... | collective-permute-start | bytes 6152 | tf_op jit(solution)/shard_map/ppermute | solution.py:101

commit v2 on v1

--- a/solution.py
+++ b/solution.py
@@ -16,13 +16,15 @@
     )
 
 
-def product_kernel(half, with_total, place, *refs):
+def product_kernel(half, with_total, waits, place, *refs):
+    refs = refs[waits:]
     if with_total:
-        hidden, weight, total_send, total_keep, send, keep = refs
+        hidden, other_hidden, weight, total_send, total_keep, send, keep = refs
     else:
-        hidden, weight, send, keep = refs
+        hidden, other_hidden, weight, send, keep = refs
     step = pl.program_id(0)
-    value = jnp.dot(hidden[...], weight[...], preferred_element_type=jnp.float32)
+    left = jnp.where(place[2] == 1, hidden[...], other_hidden[...])
+    value = jnp.dot(left, weight[...], preferred_element_type=jnp.float32)
 
     @pl.when(step < half)
     def _():
@@ -33,7 +35,7 @@
         keep[0] = value + total_keep[0] if with_total else value
 
 
-def product(hidden, weight, slot, own, blocks, cols, total=None, token_block=0):
+def product(hidden, other_hidden, first_hidden, weight, slot, own, blocks, cols, total=None, token_block=0, wait=()):
     tokens, units = hidden.shape
     half = blocks // 2
 
@@ -47,11 +49,12 @@
         block = jnp.where(step < half, 2 * step + 1, 2 * (step - half))
         return place[0], lax.bitwise_xor(place[1], block)
 
-    in_specs = [
+    in_specs = [pl.BlockSpec((16, 128), lambda step, place: (0, 0)) for _ in wait] + [
+        pl.BlockSpec((tokens, units), lambda step, place: (0, 0)),
         pl.BlockSpec((tokens, units), lambda step, place: (0, 0)),
         pl.BlockSpec((units, cols), weight_at),
     ]
-    operands = [hidden, weight]
+    operands = [*wait, hidden, other_hidden, weight]
     if total is not None:
         in_specs += [
             pl.BlockSpec((1, tokens, cols), lambda step, place: (first(step), token_block, 0)),
@@ -60,7 +63,7 @@
         operands += list(total)
     out = jax.ShapeDtypeStruct((half, tokens, cols), jnp.float32)
     return pl.pallas_call(
-        functools.partial(product_kernel, half, total is not None),
+        functools.partial(product_kernel, half, total is not None, len(wait)),
         grid_spec=pltpu.PrefetchScalarGridSpec(
             num_scalar_prefetch=1,
             grid=(blocks,),
@@ -77,7 +80,7 @@
             bytes_accessed=2 * (units * blocks * cols + tokens * units) + 8 * tokens * blocks * cols,
             transcendentals=0,
         ),
-    )(jnp.stack([slot, own]).astype(jnp.int32), *operands)
+    )(jnp.stack([slot, own, first_hidden]).astype(jnp.int32), *operands)
 
 
 def local(gate_pre, up_pre, residual, gain, down_weight):
@@ -112,9 +115,8 @@
     mul = functools.partial(product, weight=down_weight, own=own, blocks=plane, cols=cols)
 
     halves = 2
-    quarters = 4
     part = tokens // halves
-    fine = tokens // quarters
+    cuts = [[0, part // 2, part]] * 2
     hidden = [
         gated(gate_pre[i * part : (i + 1) * part], up_pre[i * part : (i + 1) * part])
         for i in range(halves)
@@ -123,32 +125,33 @@
     mid = [across(v) for v in hidden]
     mid_out = [outward(v) for v in mid]
     far = [across(v) for v in near]
-    far_out = [
-        outward(v[i * fine : (i + 1) * fine]) for v in far for i in range(quarters // halves)
-    ]
 
     other_mid = jnp.where(low, 2, 1)
     other_end = jnp.where(low, 3, 0)
-    done = []
-    for i in range(halves):
-        total = mul(hidden[i], slot=layer)
-        total = mul(near[i], slot=layer ^ 1, total=total)
-        total = mul(jnp.where(middle, mid[i], mid_out[i]), slot=other_mid, total=total)
-        for j in range(quarters // halves):
-            piece = jnp.where(
-                middle, far[i][j * fine : (j + 1) * fine], far_out[i * (quarters // halves) + j]
-            )
-            done.append(mul(piece, slot=other_end, total=total, token_block=j))
-
     plane_bits = plane.bit_length() - 1
     all_bits = devices.bit_length() - 1
-    streams = []
-    for j, (send, keep) in enumerate(done):
-        value = keep + swap(send, 0)
-        for bit in range(1, plane_bits):
-            value = value.reshape(-1, 2, fine, cols)
-            value = value[:, 0] + swap(value[:, 1], bit)
-        streams.append(value[0] + residual[j * fine : (j + 1) * fine].astype(jnp.float32))
+    always = jnp.ones_like(layer)
+    streams = {}
+    for i in reversed(range(halves)):
+        total = mul(hidden[i], hidden[i], always, slot=layer)
+        total = mul(near[i], near[i], always, slot=layer ^ 1, total=total)
+        total = mul(mid[i], mid_out[i], middle, slot=other_mid, total=total)
+        for start, stop in zip(cuts[i][:-1], cuts[i][1:]):
+            size = stop - start
+            piece = far[i][start:stop]
+            piece_out = outward(piece)
+            send, keep = mul(
+                piece, piece_out, middle, slot=other_end, total=total, token_block=start // size,
+                wait=list(streams.values())[-2:-1],
+            )
+            value = keep + swap(send, 0)
+            for bit in range(1, plane_bits):
+                value = value.reshape(-1, 2, size, cols)
+                sent = swap(value[:, 1].astype(jnp.bfloat16), bit)
+                value = value[:, 0] + sent.astype(jnp.float32)
+            rows = residual[i * part + start : i * part + stop]
+            streams[i * part + start] = value[0] + rows.astype(jnp.float32)
+    streams = [streams[k] for k in sorted(streams)]
     squares = jnp.concatenate([jnp.sum(s * s, axis=1) for s in streams])
     for bit in range(all_bits):
         squares = squares + swap(squares, bit)

time: 193 us -> 183 us (0.948)
  other arithmetic: 13.7 us -> 6.35 us
  local copies, waits for them, and re-layouts: 7.55 us -> 2.24 us
    ppermute x12, waiting for transfers between devices: 24.7 us -> 12.4 us  [swap(): lax.ppermute(value, 'row', [(i, i ^ 1 << bit) for i in range(devices)])]
    ppermute x12, waiting for transfers between devices: 57.5 us -> 68.7 us  [move(): lax.ppermute(value, 'row', [(s * plane + i, t * plane + i) for s, t in pa...]
    select_n x6 -> x0, other arithmetic: 7.51 us -> none  [the longest x4 4.82 us: local(): jnp.where(middle, far[i][j * fine:(j + 1) * fine], far_out[i * (quarters...]
    unnamed x14 -> x2, local copies, waits for them, and re-layouts: 4.56 us -> 0.01 us
  transfers between devices with their start and end apart: 24 -> 24, of which waited for: 12 -> 13; matrix products, arithmetic and copies ran while one was open for 6% -> 2% of each run, Pallas kernels for 31% -> 34%
where the time goes in v2:
time: 183 us; the launch traced here: 182 us
  waiting for transfers between devices  81.1 us (44%)
  Pallas kernels  61.6 us (34%)
  starting transfers between devices  30 us (16%)
  other arithmetic  6.35 us (3%)
  local copies, waits for them, and re-layouts  2.24 us (1%)
    ppermute x12, waiting for transfers between devices, move(): lax.ppermute(value, 'row', [(s * plane + i, t * plane + i) for s, t in pa...  68.7 us
    pallas_call x10, Pallas kernels, product(): pl.pallas_call(functools.partial(product_kernel, half, total is not None,...  61.6 us
    ppermute x12, starting transfers between devices, move(): lax.ppermute(value, 'row', [(s * plane + i, t * plane + i) for s, t in pa...  19.9 us
    ppermute x12, waiting for transfers between devices, swap(): lax.ppermute(value, 'row', [(i, i ^ 1 << bit) for i in range(devices)])  12.4 us
    ppermute x12, starting transfers between devices, swap(): lax.ppermute(value, 'row', [(i, i ^ 1 << bit) for i in range(devices)])  10.1 us
  transfers between devices with their start and end apart: 24, of which 13 were waited for; matrix products, arithmetic and copies ran while one was open for 2% of the time, Pallas kernels for 34%

profile of v2, /device:TPU:0, one launch (start us, length us, event | category | flops | bytes accessed | tf_op | source)
XLA Modules:
  0.0 182.3 jit_solution(9578543442633214572)
XLA Ops:
  0.6 3.5 %fusion.8 = (bf16[256,2048]{1,0:T(8,128)(2,1)S(1)}, bf16[256,2048]{1,0:T(8,128)(2,1)S(1)}) fusion(bf16[512,2048]{1,0:T(8,128)(2,1)} %param.6, bf16[512,2048]{1,0:T(8,128)(2,1)} %param.5), kind=kLoop, calls=%fused_computation.12 | loop fusion | flops 8388608 | bytes 6291456 | tf_op jit(solution)/shard_map/convert_element_type | solution.py:14
  4.1 3.1 %collective-permute-start = (bf16[256,2048]{1,0:T(8,128)(2,1)S(1)}, bf16[256,2048]{1,0:T(8,128)(2,1)}, u32[]{:S(2)}, u32[]{:S(2)}) collective-permute-start(bf16[256,2048]{1,0:T(8,128)(2,1)S(1)} %get-tuple-element.51.refs_0_.refs_1_), channel_id=1, source_target_pairs={{0,4},{1,5},{2,6},{3,7},{4,0},{5,1},{6,2},{7,3},{8,12},{9,13},{10,... | collective-permute-start | bytes 3145736 | tf_op jit(solution)/shard_map/ppermute | solution.py:99
  7.2 1.6 collective-permute-start.3
  8.8 3.5 %collective-permute-start.7 = (bf16[256,2048]{1,0:T(8,128)(2,1)S(1)}, bf16[256,2048]{1,0:T(8,128)(2,1)S(1)}, u32[]{:S(2)}, u32[]{:S(2)}) collective-permute-start(bf16[256,2048]{1,0:T(8,128)(2,1)S(1)} %get-tuple-element.50.refs_0_.refs_1_), channel_id=1, source_target_pairs={{0,4},{1,5},{2,6},{3,7},{4,0},{5,1},{6,2},{7,3},{8,12},{9,13},{10,... | collective-permute-start | bytes 3145736 | tf_op jit(solution)/shard_map/ppermute | solution.py:99
  12.3 1.6 collective-permute-start.10
  14.0 17.3 %collective-permute-done.refs_0_.refs_1_ = bf16[256,2048]{1,0:T(8,128)(2,1)} collective-permute-done((bf16[256,2048]{1,0:T(8,128)(2,1)S(1)}, bf16[256,2048]{1,0:T(8,128)(2,1)}, u32[]{:S(2)}, u32[]{:S(2)}) %collective-permute-start) | collective-permute-done | bytes 1048608 | tf_op jit(solution)/shard_map/ppermute | solution.py:99
  31.3 1.6 collective-permute-start.1
  32.9 0.1 add_add_fusion.place
  33.0 0.1 add_add_fusion.1.place
  33.1 0.1 pad_add_fusion.1.place
  33.2 0.1 pad_add_fusion.place
  33.2 6.1 %shard_map.68 = (f32[2,256,512]{2,1,0:T(8,128)S(1)}, f32[2,256,512]{2,1,0:T(8,128)S(1)}) custom-call(s32[3]{0:T(128)S(1)} %pad_add_fusion.place, bf16[256,2048]{1,0:T(8,128)(2,1)S(1)} %get-tuple-element.51.refs_0_.refs_1_, bf16[256,2048]{1,0:T(8,128)(2,1)S(1)} %get-tuple-element.51.refs_0_.refs_1_, bf16[8192,2048]{1,0:T(8,128)(2,1)} %refs_3_.3), custom_call_target="tpu_custom_call" | custom-call | flops 2147483648 | bytes 13631488 | tf_op jit(solution)/shard_map/pallas_call | solution.py:65
  39.4 1.3 collective-permute-start.4
  40.7 6.1 %shard_map.72 = (f32[2,256,512]{2,1,0:T(8,128)S(1)}, f32[2,256,512]{2,1,0:T(8,128)S(1)}) custom-call(s32[3]{0:T(128)S(1)} %pad_add_fusion.place, bf16[256,2048]{1,0:T(8,128)(2,1)S(1)} %get-tuple-element.50.refs_0_.refs_1_, bf16[256,2048]{1,0:T(8,128)(2,1)S(1)} %get-tuple-element.50.refs_0_.refs_1_, bf16[8192,2048]{1,0:T(8,128)(2,1)} %refs_3_.3), custom_call_target="tpu_custom_call" | custom-call | flops 2147483648 | bytes 13631488 | tf_op jit(solution)/shard_map/pallas_call | solution.py:65
  46.8 6.8 %collective-permute-done.7.refs_0_.refs_1_ = bf16[256,2048]{1,0:T(8,128)(2,1)S(1)} collective-permute-done((bf16[256,2048]{1,0:T(8,128)(2,1)S(1)}, bf16[256,2048]{1,0:T(8,128)(2,1)S(1)}, u32[]{:S(2)}, u32[]{:S(2)}) %collective-permute-start.7) | collective-permute-done | bytes 1048608 | tf_op jit(solution)/shard_map/ppermute | solution.py:99
  53.7 0.7 collective-permute-start.8
  54.4 0.0 collective-permute-done.10.refs_0_
  54.4 1.3 collective-permute-start.11
  55.7 1.3 fusion.33
  57.0 1.3 collective-permute-start.2
  58.3 1.3 collective-permute-start.14
  59.6 7.5 %shard_map.69 = (f32[2,256,512]{2,1,0:T(8,128)S(1)}, f32[2,256,512]{2,1,0:T(8,128)S(1)}) custom-call(s32[3]{0:T(128)S(1)} %pad_add_fusion.1.place, bf16[256,2048]{1,0:T(8,128)(2,1)} %collective-permute-done.refs_0_.refs_1_, bf16[256,2048]{1,0:T(8,128)(2,1)} %collective-permute-done.refs_0_.refs_1_, bf16[8192,2048]{1,0:T(8,128)(2,1)} %refs_3_.3, ...), custom_call_target="tpu_custom_call" | custom-call | flops 2147483648 | bytes 13631488 | tf_op jit(solution)/shard_map/pallas_call | solution.py:65
  67.1 6.2 %shard_map.73 = (f32[2,256,512]{2,1,0:T(8,128)S(1)}, f32[2,256,512]{2,1,0:T(8,128)S(1)}) custom-call(s32[3]{0:T(128)S(1)} %pad_add_fusion.1.place, bf16[256,2048]{1,0:T(8,128)(2,1)S(1)} %collective-permute-done.7.refs_0_.refs_1_, bf16[256,2048]{1,0:T(8,128)(2,1)S(1)} %collective-permute-done.7.refs_0_.refs_1_, bf16[8192,2048]{1,0:T(8,128)(2,1)} %refs_3_.3, ...), custom_call_target="tpu_custom_call" | custom-call | flops 2147483648 | bytes 13631488 | tf_op jit(solution)/shard_map/pallas_call | solution.py:65
  73.3 2.8 %collective-permute-done.4.refs_1_ = bf16[256,2048]{1,0:T(8,128)(2,1)S(1)} collective-permute-done((bf16[256,2048]{1,0:T(8,128)(2,1)}, bf16[256,2048]{1,0:T(8,128)(2,1)S(1)}, u32[]{:S(2)}, u32[]{:S(2)}) %collective-permute-start.4) | collective-permute-done | bytes 1048608 | tf_op jit(solution)/shard_map/ppermute | solution.py:99
  76.2 6.5 %shard_map.70 = (f32[2,256,512]{2,1,0:T(8,128)S(1)}, f32[2,256,512]{2,1,0:T(8,128)S(1)}) custom-call(s32[3]{0:T(128)S(1)} %add_add_fusion.1.place, bf16[256,2048]{1,0:T(8,128)(2,1)} %collective-permute-done.3.refs_0_, bf16[256,2048]{1,0:T(8,128)(2,1)S(1)} %collective-permute-done.4.refs_1_, bf16[8192,2048]{1,0:T(8,128)(2,1)} %refs_3_.3, ...), custom_call_target="tpu_custom_call" | custom-call | flops 2147483648 | bytes 13631488 | tf_op jit(solution)/shard_map/pallas_call | solution.py:65
  82.7 27.2 %collective-permute-done.2.refs_1_ = bf16[128,2048]{1,0:T(8,128)(2,1)S(1)} collective-permute-done((bf16[128,2048]{1,0:T(8,128)(2,1)S(1)}, bf16[128,2048]{1,0:T(8,128)(2,1)S(1)}, u32[]{:S(2)}, u32[]{:S(2)}) %collective-permute-start.2) | collective-permute-done | bytes 524320 | tf_op jit(solution)/shard_map/ppermute | solution.py:99
  109.9 5.6 %shard_map.71 = (f32[2,128,512]{2,1,0:T(8,128)S(1)}, f32[2,128,512]{2,1,0:T(8,128)S(1)}) custom-call(s32[3]{0:T(128)S(1)} %add_add_fusion.place, bf16[128,2048]{1,0:T(8,128)(2,1)S(1)} %get-tuple-element.54.refs_0_, bf16[128,2048]{1,0:T(8,128)(2,1)S(1)} %collective-permute-done.2.refs_1_, bf16[8192,2048]{1,0:T(8,128)(2,1)} %refs_3_.3, ...), custom_call_target="tpu_custom_call" | custom-call | flops 1073741824 | bytes 11010048 | tf_op jit(solution)/shard_map/pallas_call | solution.py:65
  115.5 0.1 collective-permute-start.5
  115.6 4.7 %collective-permute-done.14.refs_1_ = bf16[128,2048]{1,0:T(8,128)(2,1)S(1)} collective-permute-done((bf16[128,2048]{1,0:T(8,128)(2,1)S(1)}, bf16[128,2048]{1,0:T(8,128)(2,1)S(1)}, u32[]{:S(2)}, u32[]{:S(2)}) %collective-permute-start.14) | collective-permute-done | bytes 524320 | tf_op jit(solution)/shard_map/ppermute | solution.py:99
  120.3 5.6 %shard_map.76 = (f32[2,128,512]{2,1,0:T(8,128)S(1)}, f32[2,128,512]{2,1,0:T(8,128)S(1)}) custom-call(s32[3]{0:T(128)S(1)} %add_add_fusion.place, bf16[128,2048]{1,0:T(8,128)(2,1)S(1)} %get-tuple-element.55.refs_0_, bf16[128,2048]{1,0:T(8,128)(2,1)S(1)} %collective-permute-done.14.refs_1_, bf16[8192,2048]{1,0:T(8,128)(2,1)} %refs_3_.3, ...), custom_call_target="tpu_custom_call" | custom-call | flops 1073741824 | bytes 11010048 | tf_op jit(solution)/shard_map/pallas_call | solution.py:65
  125.9 0.1 collective-permute-start.15
  126.0 0.1 fusion.32
  126.1 1.3 collective-permute-start.9
  127.4 1.3 collective-permute-start.17
  128.7 0.1 add_bitcast_fusion.3
  128.8 1.7 collective-permute-start.6
  130.6 0.1 add_bitcast_fusion.1
  130.7 0.4 collective-permute-start.16
  131.1 6.6 %shard_map.74 = (f32[2,256,512]{2,1,0:T(8,128)S(1)}, f32[2,256,512]{2,1,0:T(8,128)S(1)}) custom-call(s32[3]{0:T(128)S(1)} %add_add_fusion.1.place, bf16[256,2048]{1,0:T(8,128)(2,1)} %collective-permute-done.10.refs_0_, bf16[256,2048]{1,0:T(8,128)(2,1)S(1)} %collective-permute-done.11.refs_1_, bf16[8192,2048]{1,0:T(8,128)(2,1)} %refs_3_.3, ...), custom_call_target="tpu_custom_call" | custom-call | flops 2147483648 | bytes 13631488 | tf_op jit(solution)/shard_map/pallas_call | solution.py:65
  137.8 0.2 multiply_reduce_fusion.1
  138.0 4.7 %collective-permute-done.9.refs_2_ = bf16[128,2048]{1,0:T(8,128)(2,1)S(1)} collective-permute-done((bf16[128,2048]{1,0:T(8,128)(2,1)S(1)}, bf16[128,2048]{1,0:T(8,128)(2,1)S(1)}, u32[]{:S(2)}, u32[]{:S(2)}) %collective-permute-start.9) | collective-permute-done | bytes 524320 | tf_op jit(solution)/shard_map/ppermute | solution.py:99
  142.7 5.6 %shard_map.75 = (f32[2,128,512]{2,1,0:T(8,128)S(1)}, f32[2,128,512]{2,1,0:T(8,128)S(1)}) custom-call(s32[3]{0:T(128)S(1)} %add_add_fusion.place, f32[128,512]{1,0:T(8,128)S(1)} %get-tuple-element.47.refs_0_, bf16[128,2048]{1,0:T(8,128)(2,1)S(1)} %get-tuple-element.52.refs_1_, bf16[128,2048]{1,0:T(8,128)(2,1)S(1)} %collective-permute-done.9.refs_2_, ...), custom_call_target="tpu_custom_call" | custom-call | flops 1073741824 | bytes 11010048 | tf_op jit(solution)/shard_map/pallas_call | solution.py:65
  148.3 0.1 collective-permute-start.12
  148.4 5.1 %collective-permute-done.17.refs_2_ = bf16[128,2048]{1,0:T(8,128)(2,1)S(1)} collective-permute-done((bf16[128,2048]{1,0:T(8,128)(2,1)S(1)}, bf16[128,2048]{1,0:T(8,128)(2,1)S(1)}, u32[]{:S(2)}, u32[]{:S(2)}) %collective-permute-start.17) | collective-permute-done | bytes 524320 | tf_op jit(solution)/shard_map/ppermute | solution.py:99
  153.5 5.6 %shard_map.77 = (f32[2,128,512]{2,1,0:T(8,128)S(1)}, f32[2,128,512]{2,1,0:T(8,128)S(1)}) custom-call(s32[3]{0:T(128)S(1)} %add_add_fusion.place, f32[128,512]{1,0:T(8,128)S(1)} %get-tuple-element.59.refs_0_, bf16[128,2048]{1,0:T(8,128)(2,1)S(1)} %get-tuple-element.53.refs_1_, bf16[128,2048]{1,0:T(8,128)(2,1)S(1)} %collective-permute-done.17.refs_2_, ...), custom_call_target="tpu_custom_call" | custom-call | flops 1073741824 | bytes 11010048 | tf_op jit(solution)/shard_map/pallas_call | solution.py:65
  159.2 0.1 collective-permute-start.18
  159.3 0.1 add_bitcast_fusion.2
  159.4 1.7 collective-permute-start.13
  161.1 0.0 collective-permute-done.18
  161.2 0.1 add_bitcast_fusion
  161.3 1.7 collective-permute-start.19
  163.0 2.7 %collective-permute-done.13 = bf16[1,128,512]{2,1,0:T(8,128)(2,1)S(1)} collective-permute-done((bf16[1,128,512]{2,1,0:T(8,128)(2,1)S(1)}, bf16[1,128,512]{2,1,0:T(8,128)(2,1)S(1)}, u32[]{:S(2)}, u32[]{:S(2)}) %collective-permute-start.13) | collective-permute-done | bytes 131104 | tf_op jit(solution)/shard_map/ppermute | solution.py:104
  165.7 2.4 %collective-permute-done.19 = bf16[1,128,512]{2,1,0:T(8,128)(2,1)S(1)} collective-permute-done((bf16[1,128,512]{2,1,0:T(8,128)(2,1)S(1)}, bf16[1,128,512]{2,1,0:T(8,128)(2,1)S(1)}, u32[]{:S(2)}, u32[]{:S(2)}) %collective-permute-start.19) | collective-permute-done | bytes 131104 | tf_op jit(solution)/shard_map/ppermute | solution.py:104
  168.1 0.2 multiply_reduce_fusion.3
  168.3 0.1 collective-permute-start.20
  168.4 1.1 collective-permute-done.20
  169.6 1.7 collective-permute-start.21
  171.3 1.9 %collective-permute-done.21 = f32[512]{0:T(512)S(1)} collective-permute-done((f32[512]{0:T(512)S(1)}, f32[512]{0:T(512)S(1)}, u32[]{:S(2)}, u32[]{:S(2)}) %collective-permute-start.21) | collective-permute-done | bytes 2080 | tf_op jit(solution)/shard_map/ppermute | solution.py:104
  173.2 0.8 dynamic_slice.3
  174.0 2.8 %collective-permute-done.22 = f32[512]{0:T(512)S(1)} collective-permute-done((f32[512]{0:T(512)S(1)}, f32[512]{0:T(512)S(1)}, u32[]{:S(2)}, u32[]{:S(2)}) %collective-permute-start.22) | collective-permute-done | bytes 2080 | tf_op jit(solution)/shard_map/ppermute | solution.py:104
  176.8 2.3 %collective-permute-start.23 = (f32[512]{0:T(512)S(1)}, f32[512]{0:T(512)S(1)}, u32[]{:S(2)}, u32[]{:S(2)}) collective-permute-start(f32[512]{0:T(512)S(1)} %add.86), channel_id=1, source_target_pairs={{0,8},{1,9},{2,10},{3,11},{4,12},{5,13},{6,14},{7,15},{8,0},{9,1},... | collective-permute-start | bytes 6152 | tf_op jit(solution)/shard_map/ppermute | solution.py:104
  179.1 0.9 fusion.10
  180.0 1.3 collective-permute-done.23
  181.3 1.0 multiply_convert_fusion
  (21 shorter events, 0.1 us)
Async XLA Ops:
  4.1 27.2 %collective-permute-start = (bf16[256,2048]{1,0:T(8,128)(2,1)S(1)}, bf16[256,2048]{1,0:T(8,128)(2,1)}, u32[]{:S(2)}, u32[]{:S(2)}) collective-permute-start(bf16[256,2048]{1,0:T(8,128)(2,1)S(1)} %get-tuple-element.51.refs_0_.refs_1_), channel_id=1, source_target_pairs={{0,4},{1,5},{2,6},{3,7},{4,0},{5,1},{6,2},{7,3},{8,12},{9,13},{10,... | collective-permute-start | bytes 3145736 | tf_op jit(solution)/shard_map/ppermute | solution.py:99
  7.2 32.2 %collective-permute-start.3 = (bf16[256,2048]{1,0:T(8,128)(2,1)S(1)}, bf16[256,2048]{1,0:T(8,128)(2,1)}, u32[]{:S(2)}, u32[]{:S(2)}) collective-permute-start(bf16[256,2048]{1,0:T(8,128)(2,1)S(1)} %get-tuple-element.51.refs_0_.refs_1_), channel_id=1, source_target_pairs={{4,8},{5,9},{6,10},{7,11},{8,4},{9,5},{10,6},{11,7},{20,24},{21,25... | collective-permute-start | bytes 3145736 | tf_op jit(solution)/shard_map/ppermute | solution.py:99
  8.8 44.8 %collective-permute-start.7 = (bf16[256,2048]{1,0:T(8,128)(2,1)S(1)}, bf16[256,2048]{1,0:T(8,128)(2,1)S(1)}, u32[]{:S(2)}, u32[]{:S(2)}) collective-permute-start(bf16[256,2048]{1,0:T(8,128)(2,1)S(1)} %get-tuple-element.50.refs_0_.refs_1_), channel_id=1, source_target_pairs={{0,4},{1,5},{2,6},{3,7},{4,0},{5,1},{6,2},{7,3},{8,12},{9,13},{10,... | collective-permute-start | bytes 3145736 | tf_op jit(solution)/shard_map/ppermute | solution.py:99
  12.3 42.1 %collective-permute-start.10 = (bf16[256,2048]{1,0:T(8,128)(2,1)S(1)}, bf16[256,2048]{1,0:T(8,128)(2,1)}, u32[]{:S(2)}, u32[]{:S(2)}) collective-permute-start(bf16[256,2048]{1,0:T(8,128)(2,1)S(1)} %get-tuple-element.50.refs_0_.refs_1_), channel_id=1, source_target_pairs={{4,8},{5,9},{6,10},{7,11},{8,4},{9,5},{10,6},{11,7},{20,24},{21,25... | collective-permute-start | bytes 3145736 | tf_op jit(solution)/shard_map/ppermute | solution.py:99
  31.3 24.4 %collective-permute-start.1 = (bf16[256,2048]{1,0:T(8,128)(2,1)}, bf16[256,2048]{1,0:T(8,128)(2,1)}, u32[]{:S(2)}, u32[]{:S(2)}) collective-permute-start(bf16[256,2048]{1,0:T(8,128)(2,1)} %collective-permute-done.refs_0_.refs_1_), channel_id=1, source_target_pairs={{4,8},{5,9},{6,10},{7,11},{8,4},{9,5},{10,6},{11,7},{20,24},{21,25... | collective-permute-start | bytes 3145736 | tf_op jit(solution)/shard_map/ppermute | solution.py:99
  39.4 36.8 %collective-permute-start.4 = (bf16[256,2048]{1,0:T(8,128)(2,1)}, bf16[256,2048]{1,0:T(8,128)(2,1)S(1)}, u32[]{:S(2)}, u32[]{:S(2)}) collective-permute-start(bf16[256,2048]{1,0:T(8,128)(2,1)} %collective-permute-done.3.refs_0_), channel_id=1, source_target_pairs={{4,0},{5,1},{6,2},{7,3},{8,12},{9,13},{10,14},{11,15},{20,16},{21,... | collective-permute-start | bytes 3145736 | tf_op jit(solution)/shard_map/ppermute | solution.py:99
  53.7 72.3 %collective-permute-start.8 = (bf16[256,2048]{1,0:T(8,128)(2,1)S(1)}, bf16[256,2048]{1,0:T(8,128)(2,1)S(1)}, u32[]{:S(2)}, u32[]{:S(2)}) collective-permute-start(bf16[256,2048]{1,0:T(8,128)(2,1)S(1)} %collective-permute-done.7.refs_0_.refs_1_), channel_id=1, source_target_pairs={{4,8},{5,9},{6,10},{7,11},{8,4},{9,5},{10,6},{11,7},{20,24},{21,25... | collective-permute-start | bytes 3145736 | tf_op jit(solution)/shard_map/ppermute | solution.py:99
  54.4 76.7 %collective-permute-start.11 = (bf16[256,2048]{1,0:T(8,128)(2,1)}, bf16[256,2048]{1,0:T(8,128)(2,1)S(1)}, u32[]{:S(2)}, u32[]{:S(2)}) collective-permute-start(bf16[256,2048]{1,0:T(8,128)(2,1)} %collective-permute-done.10.refs_0_), channel_id=1, source_target_pairs={{4,0},{5,1},{6,2},{7,3},{8,12},{9,13},{10,14},{11,15},{20,16},{21,... | collective-permute-start | bytes 3145736 | tf_op jit(solution)/shard_map/ppermute | solution.py:99
  57.0 52.8 %collective-permute-start.2 = (bf16[128,2048]{1,0:T(8,128)(2,1)S(1)}, bf16[128,2048]{1,0:T(8,128)(2,1)S(1)}, u32[]{:S(2)}, u32[]{:S(2)}) collective-permute-start(bf16[128,2048]{1,0:T(8,128)(2,1)S(1)} %get-tuple-element.54.refs_0_), channel_id=1, source_target_pairs={{4,0},{5,1},{6,2},{7,3},{8,12},{9,13},{10,14},{11,15},{20,16},{21,... | collective-permute-start | bytes 1572872 | tf_op jit(solution)/shard_map/ppermute | solution.py:99
  58.3 61.9 %collective-permute-start.14 = (bf16[128,2048]{1,0:T(8,128)(2,1)S(1)}, bf16[128,2048]{1,0:T(8,128)(2,1)S(1)}, u32[]{:S(2)}, u32[]{:S(2)}) collective-permute-start(bf16[128,2048]{1,0:T(8,128)(2,1)S(1)} %get-tuple-element.55.refs_0_), channel_id=1, source_target_pairs={{4,0},{5,1},{6,2},{7,3},{8,12},{9,13},{10,14},{11,15},{20,16},{21,... | collective-permute-start | bytes 1572872 | tf_op jit(solution)/shard_map/ppermute | solution.py:99
  115.5 13.2 %collective-permute-start.5 = (f32[2,128,512]{2,1,0:T(8,128)S(1)}, f32[2,128,512]{2,1,0:T(8,128)S(1)}, u32[]{:S(2)}, u32[]{:S(2)}) collective-permute-start(f32[2,128,512]{2,1,0:T(8,128)S(1)} %get-tuple-element.29), channel_id=1, source_target_pairs={{0,1},{1,0},{2,3},{3,2},{4,5},{5,4},{6,7},{7,6},{8,9},{9,8},{10,11... | collective-permute-start | bytes 1572872 | tf_op jit(solution)/shard_map/ppermute | solution.py:104
  125.9 4.7 %collective-permute-start.15 = (f32[2,128,512]{2,1,0:T(8,128)S(1)}, f32[2,128,512]{2,1,0:T(8,128)S(1)}, u32[]{:S(2)}, u32[]{:S(2)}) collective-permute-start(f32[2,128,512]{2,1,0:T(8,128)S(1)} %get-tuple-element.39), channel_id=1, source_target_pairs={{0,1},{1,0},{2,3},{3,2},{4,5},{5,4},{6,7},{7,6},{8,9},{9,8},{10,11... | collective-permute-start | bytes 1572872 | tf_op jit(solution)/shard_map/ppermute | solution.py:104
  126.1 16.6 %collective-permute-start.9 = (bf16[128,2048]{1,0:T(8,128)(2,1)S(1)}, bf16[128,2048]{1,0:T(8,128)(2,1)S(1)}, u32[]{:S(2)}, u32[]{:S(2)}) collective-permute-start(bf16[128,2048]{1,0:T(8,128)(2,1)S(1)} %get-tuple-element.52.refs_1_), channel_id=1, source_target_pairs={{4,0},{5,1},{6,2},{7,3},{8,12},{9,13},{10,14},{11,15},{20,16},{21,... | collective-permute-start | bytes 1572872 | tf_op jit(solution)/shard_map/ppermute | solution.py:99
  127.4 26.1 %collective-permute-start.17 = (bf16[128,2048]{1,0:T(8,128)(2,1)S(1)}, bf16[128,2048]{1,0:T(8,128)(2,1)S(1)}, u32[]{:S(2)}, u32[]{:S(2)}) collective-permute-start(bf16[128,2048]{1,0:T(8,128)(2,1)S(1)} %get-tuple-element.53.refs_1_), channel_id=1, source_target_pairs={{4,0},{5,1},{6,2},{7,3},{8,12},{9,13},{10,14},{11,15},{20,16},{21,... | collective-permute-start | bytes 1572872 | tf_op jit(solution)/shard_map/ppermute | solution.py:99
  128.8 8.9 %collective-permute-start.6 = (bf16[1,128,512]{2,1,0:T(8,128)(2,1)S(1)}, bf16[1,128,512]{2,1,0:T(8,128)(2,1)S(1)}, u32[]{:S(2)}, u32[]{:S(2)}) collective-permute-start(bf16[1,128,512]{2,1,0:T(8,128)(2,1)S(1)} %fusion.23), channel_id=1, source_target_pairs={{0,2},{1,3},{2,0},{3,1},{4,6},{5,7},{6,4},{7,5},{8,10},{9,11},{10,... | collective-permute-start | bytes 393224 | tf_op jit(solution)/shard_map/ppermute | solution.py:104
  130.7 7.1 %collective-permute-start.16 = (bf16[1,128,512]{2,1,0:T(8,128)(2,1)S(1)}, bf16[1,128,512]{2,1,0:T(8,128)(2,1)S(1)}, u32[]{:S(2)}, u32[]{:S(2)}) collective-permute-start(bf16[1,128,512]{2,1,0:T(8,128)(2,1)S(1)} %fusion.25), channel_id=1, source_target_pairs={{0,2},{1,3},{2,0},{3,1},{4,6},{5,7},{6,4},{7,5},{8,10},{9,11},{10,... | collective-permute-start | bytes 393224 | tf_op jit(solution)/shard_map/ppermute | solution.py:104
  131.1 6.7 %copy-start = (bf16[512,512]{1,0:T(8,128)(2,1)S(1)}, bf16[512,512]{1,0:T(8,128)(2,1)}, u32[]{:S(2)}) copy-start(bf16[512,512]{1,0:T(8,128)(2,1)} %param.7) | copy-start | bytes 1572868
  148.3 10.9 %collective-permute-start.12 = (f32[2,128,512]{2,1,0:T(8,128)S(1)}, f32[2,128,512]{2,1,0:T(8,128)S(1)}, u32[]{:S(2)}, u32[]{:S(2)}) collective-permute-start(f32[2,128,512]{2,1,0:T(8,128)S(1)} %get-tuple-element.37), channel_id=1, source_target_pairs={{0,1},{1,0},{2,3},{3,2},{4,5},{5,4},{6,7},{7,6},{8,9},{9,8},{10,11... | collective-permute-start | bytes 1572872 | tf_op jit(solution)/shard_map/ppermute | solution.py:104
  159.2 2.0 %collective-permute-start.18 = (f32[2,128,512]{2,1,0:T(8,128)S(1)}, f32[2,128,512]{2,1,0:T(8,128)S(1)}, u32[]{:S(2)}, u32[]{:S(2)}) collective-permute-start(f32[2,128,512]{2,1,0:T(8,128)S(1)} %get-tuple-element.41), channel_id=1, source_target_pairs={{0,1},{1,0},{2,3},{3,2},{4,5},{5,4},{6,7},{7,6},{8,9},{9,8},{10,11... | collective-permute-start | bytes 1572872 | tf_op jit(solution)/shard_map/ppermute | solution.py:104
  159.4 6.4 %collective-permute-start.13 = (bf16[1,128,512]{2,1,0:T(8,128)(2,1)S(1)}, bf16[1,128,512]{2,1,0:T(8,128)(2,1)S(1)}, u32[]{:S(2)}, u32[]{:S(2)}) collective-permute-start(bf16[1,128,512]{2,1,0:T(8,128)(2,1)S(1)} %fusion.24), channel_id=1, source_target_pairs={{0,2},{1,3},{2,0},{3,1},{4,6},{5,7},{6,4},{7,5},{8,10},{9,11},{10,... | collective-permute-start | bytes 393224 | tf_op jit(solution)/shard_map/ppermute | solution.py:104
  161.3 6.9 %collective-permute-start.19 = (bf16[1,128,512]{2,1,0:T(8,128)(2,1)S(1)}, bf16[1,128,512]{2,1,0:T(8,128)(2,1)S(1)}, u32[]{:S(2)}, u32[]{:S(2)}) collective-permute-start(bf16[1,128,512]{2,1,0:T(8,128)(2,1)S(1)} %fusion.26), channel_id=1, source_target_pairs={{0,2},{1,3},{2,0},{3,1},{4,6},{5,7},{6,4},{7,5},{8,10},{9,11},{10,... | collective-permute-start | bytes 393224 | tf_op jit(solution)/shard_map/ppermute | solution.py:104
  168.3 1.2 collective-permute-start.20
  169.6 3.7 %collective-permute-start.21 = (f32[512]{0:T(512)S(1)}, f32[512]{0:T(512)S(1)}, u32[]{:S(2)}, u32[]{:S(2)}) collective-permute-start(f32[512]{0:T(512)S(1)} %fusion.27), channel_id=1, source_target_pairs={{0,2},{1,3},{2,0},{3,1},{4,6},{5,7},{6,4},{7,5},{8,10},{9,11},{10,... | collective-permute-start | bytes 6152 | tf_op jit(solution)/shard_map/ppermute | solution.py:104
  173.2 3.6 %collective-permute-start.22 = (f32[512]{0:T(512)S(1)}, f32[512]{0:T(512)S(1)}, u32[]{:S(2)}, u32[]{:S(2)}) collective-permute-start(f32[512]{0:T(512)S(1)} %add.85), channel_id=1, source_target_pairs={{0,4},{1,5},{2,6},{3,7},{4,0},{5,1},{6,2},{7,3},{8,12},{9,13},{10,... | collective-permute-start | bytes 6152 | tf_op jit(solution)/shard_map/ppermute | solution.py:104
  176.8 4.5 %collective-permute-start.23 = (f32[512]{0:T(512)S(1)}, f32[512]{0:T(512)S(1)}, u32[]{:S(2)}, u32[]{:S(2)}) collective-permute-start(f32[512]{0:T(512)S(1)} %add.86), channel_id=1, source_target_pairs={{0,8},{1,9},{2,10},{3,11},{4,12},{5,13},{6,14},{7,15},{8,0},{9,1},... | collective-permute-start | bytes 6152 | tf_op jit(solution)/shard_map/ppermute | solution.py:104

commit v3 on v2

--- a/solution.py
+++ b/solution.py
@@ -76,8 +76,10 @@
         out_shape=[out, out],
         compiler_params=pltpu.CompilerParams(vmem_limit_bytes=32 * 2**20),
         cost_estimate=pl.CostEstimate(
-            flops=2 * tokens * units * blocks * cols,
-            bytes_accessed=2 * (units * blocks * cols + tokens * units) + 8 * tokens * blocks * cols,
+            flops=int(0.45 * 2 * tokens * units * blocks * cols),
+            bytes_accessed=int(
+                0.45 * (2 * (units * blocks * cols + tokens * units) + 8 * tokens * blocks * cols)
+            ),
             transcendentals=0,
         ),
     )(jnp.stack([slot, own, first_hidden]).astype(jnp.int32), *operands)

time: 183 us -> 172 us (0.940)
  waiting for transfers between devices: 81.1 us -> 64.7 us
  local copies, waits for them, and re-layouts: 2.24 us -> 6.38 us
    ppermute x12, waiting for transfers between devices: 68.7 us -> 52.3 us  [move(): lax.ppermute(value, 'row', [(s * plane + i, t * plane + i) for s, t in pa...]
    slice x2, local copies, waits for them, and re-layouts: 1.4 us -> 3.57 us  [local(): piece = far[i][start:stop]]
    unnamed x2 -> x12, local copies, waits for them, and re-layouts: 0.01 us -> 1.96 us
  transfers between devices with their start and end apart: 24 -> 24, of which waited for: 13 -> 12; matrix products, arithmetic and copies ran while one was open for 2% -> 4% of each run, Pallas kernels for 34% -> 36%
where the time goes in v3:
time: 172 us; the launch traced here: 171 us
  waiting for transfers between devices  64.7 us (38%)
  Pallas kernels  61.9 us (36%)
  starting transfers between devices  31 us (18%)
  local copies, waits for them, and re-layouts  6.38 us (4%)
  other arithmetic  6.36 us (4%)
    pallas_call x10, Pallas kernels, product(): pl.pallas_call(functools.partial(product_kernel, half, total is not None,...  61.9 us
    ppermute x12, waiting for transfers between devices, move(): lax.ppermute(value, 'row', [(s * plane + i, t * plane + i) for s, t in pa...  52.3 us
    ppermute x12, starting transfers between devices, move(): lax.ppermute(value, 'row', [(s * plane + i, t * plane + i) for s, t in pa...  21 us
    ppermute x12, waiting for transfers between devices, swap(): lax.ppermute(value, 'row', [(i, i ^ 1 << bit) for i in range(devices)])  12.3 us
    ppermute x12, starting transfers between devices, swap(): lax.ppermute(value, 'row', [(i, i ^ 1 << bit) for i in range(devices)])  10.1 us
    slice x2, local copies, waits for them, and re-layouts, local(): piece = far[i][start:stop]  3.57 us
    convert_element_type x1, other arithmetic, gated(): (jax.nn.silu(gate_pre.astype(jnp.float32)) * up_pre.astype(jnp.float32))....  3.5 us
  transfers between devices with their start and end apart: 24, of which 12 were waited for; matrix products, arithmetic and copies ran while one was open for 4% of the time, Pallas kernels for 36%

profile of v3, /device:TPU:0, one launch (start us, length us, event | category | flops | bytes accessed | tf_op | source)
XLA Modules:
  0.0 171.3 jit_solution(5635722406235070055)
XLA Ops:
  0.6 3.5 %fusion.8 = (bf16[256,2048]{1,0:T(8,128)(2,1)S(1)}, bf16[256,2048]{1,0:T(8,128)(2,1)S(1)}) fusion(bf16[512,2048]{1,0:T(8,128)(2,1)} %param.6, bf16[512,2048]{1,0:T(8,128)(2,1)} %param.5), kind=kLoop, calls=%fused_computation.12 | loop fusion | flops 8388608 | bytes 6291456 | tf_op jit(solution)/shard_map/convert_element_type | solution.py:14
  4.1 3.1 %collective-permute-start = (bf16[256,2048]{1,0:T(8,128)(2,1)S(1)}, bf16[256,2048]{1,0:T(8,128)(2,1)}, u32[]{:S(2)}, u32[]{:S(2)}) collective-permute-start(bf16[256,2048]{1,0:T(8,128)(2,1)S(1)} %get-tuple-element.51.refs_0_.refs_1_), channel_id=1, source_target_pairs={{0,4},{1,5},{2,6},{3,7},{4,0},{5,1},{6,2},{7,3},{8,12},{9,13},{10,... | collective-permute-start | bytes 3145736 | tf_op jit(solution)/shard_map/ppermute | solution.py:101
  7.2 1.6 collective-permute-start.3
  8.9 3.5 %collective-permute-start.7 = (bf16[256,2048]{1,0:T(8,128)(2,1)S(1)}, bf16[256,2048]{1,0:T(8,128)(2,1)S(1)}, u32[]{:S(2)}, u32[]{:S(2)}) collective-permute-start(bf16[256,2048]{1,0:T(8,128)(2,1)S(1)} %get-tuple-element.50.refs_0_.refs_1_), channel_id=1, source_target_pairs={{0,4},{1,5},{2,6},{3,7},{4,0},{5,1},{6,2},{7,3},{8,12},{9,13},{10,... | collective-permute-start | bytes 3145736 | tf_op jit(solution)/shard_map/ppermute | solution.py:101
  12.4 19.0 %collective-permute-done.refs_0_.refs_1_ = bf16[256,2048]{1,0:T(8,128)(2,1)} collective-permute-done((bf16[256,2048]{1,0:T(8,128)(2,1)S(1)}, bf16[256,2048]{1,0:T(8,128)(2,1)}, u32[]{:S(2)}, u32[]{:S(2)}) %collective-permute-start) | collective-permute-done | bytes 1048608 | tf_op jit(solution)/shard_map/ppermute | solution.py:101
  31.3 1.7 collective-permute-start.1
  33.0 1.6 collective-permute-start.10
  34.6 0.1 add_add_fusion.place
  34.7 1.3 collective-permute-start.4
  36.0 0.1 pad_add_fusion.place
  36.1 17.6 %collective-permute-done.7.refs_0_.refs_1_ = bf16[256,2048]{1,0:T(8,128)(2,1)S(1)} collective-permute-done((bf16[256,2048]{1,0:T(8,128)(2,1)S(1)}, bf16[256,2048]{1,0:T(8,128)(2,1)S(1)}, u32[]{:S(2)}, u32[]{:S(2)}) %collective-permute-start.7) | collective-permute-done | bytes 1048608 | tf_op jit(solution)/shard_map/ppermute | solution.py:101
  53.7 1.6 collective-permute-start.8
  55.3 2.3 %fusion.33 = (bf16[128,2048]{1,0:T(8,128)(2,1)}, bf16[128,2048]{1,0:T(8,128)(2,1)}) fusion(bf16[256,2048]{1,0:T(8,128)(2,1)} %collective-permute-done.1), kind=kLoop, calls=%fused_computation.57 | loop fusion | bytes 2097152 | tf_op jit(solution)/shard_map/slice | solution.py:143
  57.6 1.3 collective-permute-start.2
  58.9 6.1 %shard_map.68 = (f32[2,256,512]{2,1,0:T(8,128)S(1)}, f32[2,256,512]{2,1,0:T(8,128)S(1)}) custom-call(s32[3]{0:T(128)S(1)} %pad_add_fusion.place, bf16[256,2048]{1,0:T(8,128)(2,1)S(1)} %get-tuple-element.51.refs_0_.refs_1_, bf16[256,2048]{1,0:T(8,128)(2,1)S(1)} %get-tuple-element.51.refs_0_.refs_1_, bf16[8192,2048]{1,0:T(8,128)(2,1)} %refs_3_.3), custom_call_target="tpu_custom_call" | custom-call | flops 966367616 | bytes 6134169 | tf_op jit(solution)/shard_map/pallas_call | solution.py:65
  65.0 1.0 copy-done.1
  66.0 1.0 copy-done.3
  67.0 1.4 collective-permute-start.14
  68.4 6.1 %shard_map.72 = (f32[2,256,512]{2,1,0:T(8,128)S(1)}, f32[2,256,512]{2,1,0:T(8,128)S(1)}) custom-call(s32[3]{0:T(128)S(1)} %pad_add_fusion.place, bf16[256,2048]{1,0:T(8,128)(2,1)S(1)} %get-tuple-element.50.refs_0_.refs_1_, bf16[256,2048]{1,0:T(8,128)(2,1)S(1)} %get-tuple-element.50.refs_0_.refs_1_, bf16[8192,2048]{1,0:T(8,128)(2,1)} %refs_3_.3), custom_call_target="tpu_custom_call" | custom-call | flops 966367616 | bytes 6134169 | tf_op jit(solution)/shard_map/pallas_call | solution.py:65
  74.5 0.1 add_add_fusion.1.place
  74.6 0.1 pad_add_fusion.1.place
  74.7 1.3 collective-permute-start.11
  76.0 7.4 %shard_map.69 = (f32[2,256,512]{2,1,0:T(8,128)S(1)}, f32[2,256,512]{2,1,0:T(8,128)S(1)}) custom-call(s32[3]{0:T(128)S(1)} %pad_add_fusion.1.place, bf16[256,2048]{1,0:T(8,128)(2,1)} %collective-permute-done.refs_0_.refs_1_, bf16[256,2048]{1,0:T(8,128)(2,1)} %collective-permute-done.refs_0_.refs_1_, bf16[8192,2048]{1,0:T(8,128)(2,1)} %refs_3_.3, ...), custom_call_target="tpu_custom_call" | custom-call | flops 966367616 | bytes 6134169 | tf_op jit(solution)/shard_map/pallas_call | solution.py:65
  83.5 6.8 %shard_map.70 = (f32[2,256,512]{2,1,0:T(8,128)S(1)}, f32[2,256,512]{2,1,0:T(8,128)S(1)}) custom-call(s32[3]{0:T(128)S(1)} %add_add_fusion.1.place, bf16[256,2048]{1,0:T(8,128)(2,1)} %collective-permute-done.3.refs_0_, bf16[256,2048]{1,0:T(8,128)(2,1)} %collective-permute-done.4.refs_1_, bf16[8192,2048]{1,0:T(8,128)(2,1)} %refs_3_.3, ...), custom_call_target="tpu_custom_call" | custom-call | flops 966367616 | bytes 6134169 | tf_op jit(solution)/shard_map/pallas_call | solution.py:65
  90.3 5.9 %shard_map.71 = (f32[2,128,512]{2,1,0:T(8,128)S(1)}, f32[2,128,512]{2,1,0:T(8,128)S(1)}) custom-call(s32[3]{0:T(128)S(1)} %add_add_fusion.place, bf16[128,2048]{1,0:T(8,128)(2,1)} %get-tuple-element.54.refs_0_, bf16[128,2048]{1,0:T(8,128)(2,1)} %collective-permute-done.2.refs_1_, bf16[8192,2048]{1,0:T(8,128)(2,1)} %refs_3_.3, ...), custom_call_target="tpu_custom_call" | custom-call | flops 483183808 | bytes 4954521 | tf_op jit(solution)/shard_map/pallas_call | solution.py:65
  96.2 0.1 collective-permute-start.5
  96.3 2.3 %collective-permute-done.14.refs_1_ = bf16[128,2048]{1,0:T(8,128)(2,1)S(1)} collective-permute-done((bf16[128,2048]{1,0:T(8,128)(2,1)}, bf16[128,2048]{1,0:T(8,128)(2,1)S(1)}, u32[]{:S(2)}, u32[]{:S(2)}) %collective-permute-start.14) | collective-permute-done | bytes 524320 | tf_op jit(solution)/shard_map/ppermute | solution.py:101
  98.6 5.6 %shard_map.76 = (f32[2,128,512]{2,1,0:T(8,128)S(1)}, f32[2,128,512]{2,1,0:T(8,128)S(1)}) custom-call(s32[3]{0:T(128)S(1)} %add_add_fusion.place, bf16[128,2048]{1,0:T(8,128)(2,1)S(1)} %copy-done, bf16[128,2048]{1,0:T(8,128)(2,1)S(1)} %collective-permute-done.14.refs_1_, bf16[8192,2048]{1,0:T(8,128)(2,1)} %refs_3_.3, ...), custom_call_target="tpu_custom_call" | custom-call | flops 483183808 | bytes 4954521 | tf_op jit(solution)/shard_map/pallas_call | solution.py:65
  104.3 0.1 collective-permute-start.15
  104.3 1.3 fusion.32
  105.7 1.3 collective-permute-start.9
  107.0 0.1 add_bitcast_fusion.3
  107.1 2.1 %collective-permute-start.6 = (bf16[1,128,512]{2,1,0:T(8,128)(2,1)S(1)}, bf16[1,128,512]{2,1,0:T(8,128)(2,1)S(1)}, u32[]{:S(2)}, u32[]{:S(2)}) collective-permute-start(bf16[1,128,512]{2,1,0:T(8,128)(2,1)S(1)} %fusion.23), channel_id=1, source_target_pairs={{0,2},{1,3},{2,0},{3,1},{4,6},{5,7},{6,4},{7,5},{8,10},{9,11},{10,... | collective-permute-start | bytes 393224 | tf_op jit(solution)/shard_map/ppermute | solution.py:106
  109.1 0.1 add_bitcast_fusion.1
  109.3 0.1 collective-permute-start.16
  109.3 6.2 %shard_map.73 = (f32[2,256,512]{2,1,0:T(8,128)S(1)}, f32[2,256,512]{2,1,0:T(8,128)S(1)}) custom-call(s32[3]{0:T(128)S(1)} %pad_add_fusion.1.place, bf16[256,2048]{1,0:T(8,128)(2,1)S(1)} %collective-permute-done.7.refs_0_.refs_1_, bf16[256,2048]{1,0:T(8,128)(2,1)S(1)} %collective-permute-done.7.refs_0_.refs_1_, bf16[8192,2048]{1,0:T(8,128)(2,1)} %refs_3_.3, ...), custom_call_target="tpu_custom_call" | custom-call | flops 966367616 | bytes 6134169 | tf_op jit(solution)/shard_map/pallas_call | solution.py:65
  115.6 1.3 collective-permute-start.17
  116.9 4.2 %collective-permute-done.11.refs_1_ = bf16[256,2048]{1,0:T(8,128)(2,1)S(1)} collective-permute-done((bf16[256,2048]{1,0:T(8,128)(2,1)}, bf16[256,2048]{1,0:T(8,128)(2,1)S(1)}, u32[]{:S(2)}, u32[]{:S(2)}) %collective-permute-start.11) | collective-permute-done | bytes 1048608 | tf_op jit(solution)/shard_map/ppermute | solution.py:101
  121.1 6.6 %shard_map.74 = (f32[2,256,512]{2,1,0:T(8,128)S(1)}, f32[2,256,512]{2,1,0:T(8,128)S(1)}) custom-call(s32[3]{0:T(128)S(1)} %add_add_fusion.1.place, bf16[256,2048]{1,0:T(8,128)(2,1)} %collective-permute-done.10.refs_0_, bf16[256,2048]{1,0:T(8,128)(2,1)S(1)} %collective-permute-done.11.refs_1_, bf16[8192,2048]{1,0:T(8,128)(2,1)} %refs_3_.3, ...), custom_call_target="tpu_custom_call" | custom-call | flops 966367616 | bytes 6134169 | tf_op jit(solution)/shard_map/pallas_call | solution.py:65
  127.8 0.2 multiply_reduce_fusion.1
  128.0 4.4 %collective-permute-done.9.refs_2_ = bf16[128,2048]{1,0:T(8,128)(2,1)S(1)} collective-permute-done((bf16[128,2048]{1,0:T(8,128)(2,1)S(1)}, bf16[128,2048]{1,0:T(8,128)(2,1)S(1)}, u32[]{:S(2)}, u32[]{:S(2)}) %collective-permute-start.9) | collective-permute-done | bytes 524320 | tf_op jit(solution)/shard_map/ppermute | solution.py:101
  132.3 5.6 %shard_map.75 = (f32[2,128,512]{2,1,0:T(8,128)S(1)}, f32[2,128,512]{2,1,0:T(8,128)S(1)}) custom-call(s32[3]{0:T(128)S(1)} %add_add_fusion.place, f32[128,512]{1,0:T(8,128)S(1)} %get-tuple-element.47.refs_0_, bf16[128,2048]{1,0:T(8,128)(2,1)S(1)} %get-tuple-element.52.refs_1_, bf16[128,2048]{1,0:T(8,128)(2,1)S(1)} %collective-permute-done.9.refs_2_, ...), custom_call_target="tpu_custom_call" | custom-call | flops 483183808 | bytes 4954521 | tf_op jit(solution)/shard_map/pallas_call | solution.py:65
  137.9 0.1 collective-permute-start.12
  138.0 4.8 %collective-permute-done.17.refs_2_ = bf16[128,2048]{1,0:T(8,128)(2,1)S(1)} collective-permute-done((bf16[128,2048]{1,0:T(8,128)(2,1)S(1)}, bf16[128,2048]{1,0:T(8,128)(2,1)S(1)}, u32[]{:S(2)}, u32[]{:S(2)}) %collective-permute-start.17) | collective-permute-done | bytes 524320 | tf_op jit(solution)/shard_map/ppermute | solution.py:101
  142.7 5.5 %shard_map.77 = (f32[2,128,512]{2,1,0:T(8,128)S(1)}, f32[2,128,512]{2,1,0:T(8,128)S(1)}) custom-call(s32[3]{0:T(128)S(1)} %add_add_fusion.place, f32[128,512]{1,0:T(8,128)S(1)} %get-tuple-element.59.refs_0_, bf16[128,2048]{1,0:T(8,128)(2,1)S(1)} %get-tuple-element.53.refs_1_, bf16[128,2048]{1,0:T(8,128)(2,1)S(1)} %collective-permute-done.17.refs_2_, ...), custom_call_target="tpu_custom_call" | custom-call | flops 483183808 | bytes 4954521 | tf_op jit(solution)/shard_map/pallas_call | solution.py:65
  148.3 0.1 collective-permute-start.18
  148.3 0.1 add_bitcast_fusion.2
  148.5 1.7 %collective-permute-start.13 = (bf16[1,128,512]{2,1,0:T(8,128)(2,1)S(1)}, bf16[1,128,512]{2,1,0:T(8,128)(2,1)S(1)}, u32[]{:S(2)}, u32[]{:S(2)}) collective-permute-start(bf16[1,128,512]{2,1,0:T(8,128)(2,1)S(1)} %fusion.24), channel_id=1, source_target_pairs={{0,2},{1,3},{2,0},{3,1},{4,6},{5,7},{6,4},{7,5},{8,10},{9,11},{10,... | collective-permute-start | bytes 393224 | tf_op jit(solution)/shard_map/ppermute | solution.py:106
  150.2 0.0 collective-permute-done.18
  150.2 0.1 add_bitcast_fusion
  150.3 1.7 %collective-permute-start.19 = (bf16[1,128,512]{2,1,0:T(8,128)(2,1)S(1)}, bf16[1,128,512]{2,1,0:T(8,128)(2,1)S(1)}, u32[]{:S(2)}, u32[]{:S(2)}) collective-permute-start(bf16[1,128,512]{2,1,0:T(8,128)(2,1)S(1)} %fusion.26), channel_id=1, source_target_pairs={{0,2},{1,3},{2,0},{3,1},{4,6},{5,7},{6,4},{7,5},{8,10},{9,11},{10,... | collective-permute-start | bytes 393224 | tf_op jit(solution)/shard_map/ppermute | solution.py:106
  152.1 2.7 %collective-permute-done.13 = bf16[1,128,512]{2,1,0:T(8,128)(2,1)S(1)} collective-permute-done((bf16[1,128,512]{2,1,0:T(8,128)(2,1)S(1)}, bf16[1,128,512]{2,1,0:T(8,128)(2,1)S(1)}, u32[]{:S(2)}, u32[]{:S(2)}) %collective-permute-start.13) | collective-permute-done | bytes 131104 | tf_op jit(solution)/shard_map/ppermute | solution.py:106
  154.8 2.4 %collective-permute-done.19 = bf16[1,128,512]{2,1,0:T(8,128)(2,1)S(1)} collective-permute-done((bf16[1,128,512]{2,1,0:T(8,128)(2,1)S(1)}, bf16[1,128,512]{2,1,0:T(8,128)(2,1)S(1)}, u32[]{:S(2)}, u32[]{:S(2)}) %collective-permute-start.19) | collective-permute-done | bytes 131104 | tf_op jit(solution)/shard_map/ppermute | solution.py:106
  157.2 0.2 multiply_reduce_fusion.3
  157.4 0.1 collective-permute-start.20
  157.5 1.1 collective-permute-done.20
  158.7 1.7 %collective-permute-start.21 = (f32[512]{0:T(512)S(1)}, f32[512]{0:T(512)S(1)}, u32[]{:S(2)}, u32[]{:S(2)}) collective-permute-start(f32[512]{0:T(512)S(1)} %fusion.27), channel_id=1, source_target_pairs={{0,2},{1,3},{2,0},{3,1},{4,6},{5,7},{6,4},{7,5},{8,10},{9,11},{10,... | collective-permute-start | bytes 6152 | tf_op jit(solution)/shard_map/ppermute | solution.py:106
  160.4 1.9 %collective-permute-done.21 = f32[512]{0:T(512)S(1)} collective-permute-done((f32[512]{0:T(512)S(1)}, f32[512]{0:T(512)S(1)}, u32[]{:S(2)}, u32[]{:S(2)}) %collective-permute-start.21) | collective-permute-done | bytes 2080 | tf_op jit(solution)/shard_map/ppermute | solution.py:106
  162.3 0.8 dynamic_slice.3
  163.1 2.8 %collective-permute-done.22 = f32[512]{0:T(512)S(1)} collective-permute-done((f32[512]{0:T(512)S(1)}, f32[512]{0:T(512)S(1)}, u32[]{:S(2)}, u32[]{:S(2)}) %collective-permute-start.22) | collective-permute-done | bytes 2080 | tf_op jit(solution)/shard_map/ppermute | solution.py:106
  165.9 2.3 %collective-permute-start.23 = (f32[512]{0:T(512)S(1)}, f32[512]{0:T(512)S(1)}, u32[]{:S(2)}, u32[]{:S(2)}) collective-permute-start(f32[512]{0:T(512)S(1)} %add.86), channel_id=1, source_target_pairs={{0,8},{1,9},{2,10},{3,11},{4,12},{5,13},{6,14},{7,15},{8,0},{9,1},... | collective-permute-start | bytes 6152 | tf_op jit(solution)/shard_map/ppermute | solution.py:106
  168.2 0.9 fusion.10
  169.1 1.3 collective-permute-done.23
  170.4 1.0 multiply_convert_fusion
  (31 shorter events, 0.2 us)
Async XLA Ops:
  4.1 27.2 %collective-permute-start = (bf16[256,2048]{1,0:T(8,128)(2,1)S(1)}, bf16[256,2048]{1,0:T(8,128)(2,1)}, u32[]{:S(2)}, u32[]{:S(2)}) collective-permute-start(bf16[256,2048]{1,0:T(8,128)(2,1)S(1)} %get-tuple-element.51.refs_0_.refs_1_), channel_id=1, source_target_pairs={{0,4},{1,5},{2,6},{3,7},{4,0},{5,1},{6,2},{7,3},{8,12},{9,13},{10,... | collective-permute-start | bytes 3145736 | tf_op jit(solution)/shard_map/ppermute | solution.py:101
  7.2 27.5 %collective-permute-start.3 = (bf16[256,2048]{1,0:T(8,128)(2,1)S(1)}, bf16[256,2048]{1,0:T(8,128)(2,1)}, u32[]{:S(2)}, u32[]{:S(2)}) collective-permute-start(bf16[256,2048]{1,0:T(8,128)(2,1)S(1)} %get-tuple-element.51.refs_0_.refs_1_), channel_id=1, source_target_pairs={{4,8},{5,9},{6,10},{7,11},{8,4},{9,5},{10,6},{11,7},{20,24},{21,25... | collective-permute-start | bytes 3145736 | tf_op jit(solution)/shard_map/ppermute | solution.py:101
  8.9 44.8 %collective-permute-start.7 = (bf16[256,2048]{1,0:T(8,128)(2,1)S(1)}, bf16[256,2048]{1,0:T(8,128)(2,1)S(1)}, u32[]{:S(2)}, u32[]{:S(2)}) collective-permute-start(bf16[256,2048]{1,0:T(8,128)(2,1)S(1)} %get-tuple-element.50.refs_0_.refs_1_), channel_id=1, source_target_pairs={{0,4},{1,5},{2,6},{3,7},{4,0},{5,1},{6,2},{7,3},{8,12},{9,13},{10,... | collective-permute-start | bytes 3145736 | tf_op jit(solution)/shard_map/ppermute | solution.py:101
  31.3 24.0 %collective-permute-start.1 = (bf16[256,2048]{1,0:T(8,128)(2,1)}, bf16[256,2048]{1,0:T(8,128)(2,1)}, u32[]{:S(2)}, u32[]{:S(2)}) collective-permute-start(bf16[256,2048]{1,0:T(8,128)(2,1)} %collective-permute-done.refs_0_.refs_1_), channel_id=1, source_target_pairs={{4,8},{5,9},{6,10},{7,11},{8,4},{9,5},{10,6},{11,7},{20,24},{21,25... | collective-permute-start | bytes 3145736 | tf_op jit(solution)/shard_map/ppermute | solution.py:101
  33.0 41.7 %collective-permute-start.10 = (bf16[256,2048]{1,0:T(8,128)(2,1)S(1)}, bf16[256,2048]{1,0:T(8,128)(2,1)}, u32[]{:S(2)}, u32[]{:S(2)}) collective-permute-start(bf16[256,2048]{1,0:T(8,128)(2,1)S(1)} %get-tuple-element.50.refs_0_.refs_1_), channel_id=1, source_target_pairs={{4,8},{5,9},{6,10},{7,11},{8,4},{9,5},{10,6},{11,7},{20,24},{21,25... | collective-permute-start | bytes 3145736 | tf_op jit(solution)/shard_map/ppermute | solution.py:101
  34.7 48.8 %collective-permute-start.4 = (bf16[256,2048]{1,0:T(8,128)(2,1)}, bf16[256,2048]{1,0:T(8,128)(2,1)}, u32[]{:S(2)}, u32[]{:S(2)}) collective-permute-start(bf16[256,2048]{1,0:T(8,128)(2,1)} %collective-permute-done.3.refs_0_), channel_id=1, source_target_pairs={{4,0},{5,1},{6,2},{7,3},{8,12},{9,13},{10,14},{11,15},{20,16},{21,... | collective-permute-start | bytes 3145736 | tf_op jit(solution)/shard_map/ppermute | solution.py:101
  53.7 50.6 %collective-permute-start.8 = (bf16[256,2048]{1,0:T(8,128)(2,1)S(1)}, bf16[256,2048]{1,0:T(8,128)(2,1)}, u32[]{:S(2)}, u32[]{:S(2)}) collective-permute-start(bf16[256,2048]{1,0:T(8,128)(2,1)S(1)} %collective-permute-done.7.refs_0_.refs_1_), channel_id=1, source_target_pairs={{4,8},{5,9},{6,10},{7,11},{8,4},{9,5},{10,6},{11,7},{20,24},{21,25... | collective-permute-start | bytes 3145736 | tf_op jit(solution)/shard_map/ppermute | solution.py:101
  57.6 32.7 %collective-permute-start.2 = (bf16[128,2048]{1,0:T(8,128)(2,1)}, bf16[128,2048]{1,0:T(8,128)(2,1)}, u32[]{:S(2)}, u32[]{:S(2)}) collective-permute-start(bf16[128,2048]{1,0:T(8,128)(2,1)} %get-tuple-element.54.refs_0_), channel_id=1, source_target_pairs={{4,0},{5,1},{6,2},{7,3},{8,12},{9,13},{10,14},{11,15},{20,16},{21,... | collective-permute-start | bytes 1572872 | tf_op jit(solution)/shard_map/ppermute | solution.py:101
  65.0 1.0 copy-start.1
  66.0 1.0 copy-start.3
  67.0 9.0 %copy-start.2 = (f32[2,256,512]{2,1,0:T(8,128)S(1)}, f32[2,256,512]{2,1,0:T(8,128)}, u32[]{:S(2)}) copy-start(f32[2,256,512]{2,1,0:T(8,128)} %copy-done.1) | copy-start | bytes 3145732
  67.0 9.0 %copy-start.4 = (f32[2,256,512]{2,1,0:T(8,128)S(1)}, f32[2,256,512]{2,1,0:T(8,128)}, u32[]{:S(2)}) copy-start(f32[2,256,512]{2,1,0:T(8,128)} %copy-done.3) | copy-start | bytes 3145732
  67.0 31.6 %collective-permute-start.14 = (bf16[128,2048]{1,0:T(8,128)(2,1)}, bf16[128,2048]{1,0:T(8,128)(2,1)S(1)}, u32[]{:S(2)}, u32[]{:S(2)}) collective-permute-start(bf16[128,2048]{1,0:T(8,128)(2,1)} %get-tuple-element.55.refs_0_), channel_id=1, source_target_pairs={{4,0},{5,1},{6,2},{7,3},{8,12},{9,13},{10,14},{11,15},{20,16},{21,... | collective-permute-start | bytes 1572872 | tf_op jit(solution)/shard_map/ppermute | solution.py:101
  74.7 46.4 %collective-permute-start.11 = (bf16[256,2048]{1,0:T(8,128)(2,1)}, bf16[256,2048]{1,0:T(8,128)(2,1)S(1)}, u32[]{:S(2)}, u32[]{:S(2)}) collective-permute-start(bf16[256,2048]{1,0:T(8,128)(2,1)} %collective-permute-done.10.refs_0_), channel_id=1, source_target_pairs={{4,0},{5,1},{6,2},{7,3},{8,12},{9,13},{10,14},{11,15},{20,16},{21,... | collective-permute-start | bytes 3145736 | tf_op jit(solution)/shard_map/ppermute | solution.py:101
  90.3 8.3 %copy-start = (bf16[128,2048]{1,0:T(8,128)(2,1)S(1)}, bf16[128,2048]{1,0:T(8,128)(2,1)}, u32[]{:S(2)}) copy-start(bf16[128,2048]{1,0:T(8,128)(2,1)} %get-tuple-element.55.refs_0_) | copy-start | bytes 1572868
  96.2 10.7 %collective-permute-start.5 = (f32[2,128,512]{2,1,0:T(8,128)S(1)}, f32[2,128,512]{2,1,0:T(8,128)S(1)}, u32[]{:S(2)}, u32[]{:S(2)}) collective-permute-start(f32[2,128,512]{2,1,0:T(8,128)S(1)} %get-tuple-element.29), channel_id=1, source_target_pairs={{0,1},{1,0},{2,3},{3,2},{4,5},{5,4},{6,7},{7,6},{8,9},{9,8},{10,11... | collective-permute-start | bytes 1572872 | tf_op jit(solution)/shard_map/ppermute | solution.py:106
  104.3 4.9 %collective-permute-start.15 = (f32[2,128,512]{2,1,0:T(8,128)S(1)}, f32[2,128,512]{2,1,0:T(8,128)S(1)}, u32[]{:S(2)}, u32[]{:S(2)}) collective-permute-start(f32[2,128,512]{2,1,0:T(8,128)S(1)} %get-tuple-element.39), channel_id=1, source_target_pairs={{0,1},{1,0},{2,3},{3,2},{4,5},{5,4},{6,7},{7,6},{8,9},{9,8},{10,11... | collective-permute-start | bytes 1572872 | tf_op jit(solution)/shard_map/ppermute | solution.py:106
  105.7 26.7 %collective-permute-start.9 = (bf16[128,2048]{1,0:T(8,128)(2,1)S(1)}, bf16[128,2048]{1,0:T(8,128)(2,1)S(1)}, u32[]{:S(2)}, u32[]{:S(2)}) collective-permute-start(bf16[128,2048]{1,0:T(8,128)(2,1)S(1)} %get-tuple-element.52.refs_1_), channel_id=1, source_target_pairs={{4,0},{5,1},{6,2},{7,3},{8,12},{9,13},{10,14},{11,15},{20,16},{21,... | collective-permute-start | bytes 1572872 | tf_op jit(solution)/shard_map/ppermute | solution.py:101
  107.1 20.7 %collective-permute-start.6 = (bf16[1,128,512]{2,1,0:T(8,128)(2,1)S(1)}, bf16[1,128,512]{2,1,0:T(8,128)(2,1)S(1)}, u32[]{:S(2)}, u32[]{:S(2)}) collective-permute-start(bf16[1,128,512]{2,1,0:T(8,128)(2,1)S(1)} %fusion.23), channel_id=1, source_target_pairs={{0,2},{1,3},{2,0},{3,1},{4,6},{5,7},{6,4},{7,5},{8,10},{9,11},{10,... | collective-permute-start | bytes 393224 | tf_op jit(solution)/shard_map/ppermute | solution.py:106
  109.3 18.5 %collective-permute-start.16 = (bf16[1,128,512]{2,1,0:T(8,128)(2,1)S(1)}, bf16[1,128,512]{2,1,0:T(8,128)(2,1)S(1)}, u32[]{:S(2)}, u32[]{:S(2)}) collective-permute-start(bf16[1,128,512]{2,1,0:T(8,128)(2,1)S(1)} %fusion.25), channel_id=1, source_target_pairs={{0,2},{1,3},{2,0},{3,1},{4,6},{5,7},{6,4},{7,5},{8,10},{9,11},{10,... | collective-permute-start | bytes 393224 | tf_op jit(solution)/shard_map/ppermute | solution.py:106
  115.6 27.2 %collective-permute-start.17 = (bf16[128,2048]{1,0:T(8,128)(2,1)S(1)}, bf16[128,2048]{1,0:T(8,128)(2,1)S(1)}, u32[]{:S(2)}, u32[]{:S(2)}) collective-permute-start(bf16[128,2048]{1,0:T(8,128)(2,1)S(1)} %get-tuple-element.53.refs_1_), channel_id=1, source_target_pairs={{4,0},{5,1},{6,2},{7,3},{8,12},{9,13},{10,14},{11,15},{20,16},{21,... | collective-permute-start | bytes 1572872 | tf_op jit(solution)/shard_map/ppermute | solution.py:101
  121.1 6.7 %copy-start.5 = (bf16[512,512]{1,0:T(8,128)(2,1)S(1)}, bf16[512,512]{1,0:T(8,128)(2,1)}, u32[]{:S(2)}) copy-start(bf16[512,512]{1,0:T(8,128)(2,1)} %param.7) | copy-start | bytes 1572868
  137.9 10.4 %collective-permute-start.12 = (f32[2,128,512]{2,1,0:T(8,128)S(1)}, f32[2,128,512]{2,1,0:T(8,128)S(1)}, u32[]{:S(2)}, u32[]{:S(2)}) collective-permute-start(f32[2,128,512]{2,1,0:T(8,128)S(1)} %get-tuple-element.37), channel_id=1, source_target_pairs={{0,1},{1,0},{2,3},{3,2},{4,5},{5,4},{6,7},{7,6},{8,9},{9,8},{10,11... | collective-permute-start | bytes 1572872 | tf_op jit(solution)/shard_map/ppermute | solution.py:106
  148.3 2.0 %collective-permute-start.18 = (f32[2,128,512]{2,1,0:T(8,128)S(1)}, f32[2,128,512]{2,1,0:T(8,128)S(1)}, u32[]{:S(2)}, u32[]{:S(2)}) collective-permute-start(f32[2,128,512]{2,1,0:T(8,128)S(1)} %get-tuple-element.41), channel_id=1, source_target_pairs={{0,1},{1,0},{2,3},{3,2},{4,5},{5,4},{6,7},{7,6},{8,9},{9,8},{10,11... | collective-permute-start | bytes 1572872 | tf_op jit(solution)/shard_map/ppermute | solution.py:106
  148.5 6.4 %collective-permute-start.13 = (bf16[1,128,512]{2,1,0:T(8,128)(2,1)S(1)}, bf16[1,128,512]{2,1,0:T(8,128)(2,1)S(1)}, u32[]{:S(2)}, u32[]{:S(2)}) collective-permute-start(bf16[1,128,512]{2,1,0:T(8,128)(2,1)S(1)} %fusion.24), channel_id=1, source_target_pairs={{0,2},{1,3},{2,0},{3,1},{4,6},{5,7},{6,4},{7,5},{8,10},{9,11},{10,... | collective-permute-start | bytes 393224 | tf_op jit(solution)/shard_map/ppermute | solution.py:106
  150.3 6.9 %collective-permute-start.19 = (bf16[1,128,512]{2,1,0:T(8,128)(2,1)S(1)}, bf16[1,128,512]{2,1,0:T(8,128)(2,1)S(1)}, u32[]{:S(2)}, u32[]{:S(2)}) collective-permute-start(bf16[1,128,512]{2,1,0:T(8,128)(2,1)S(1)} %fusion.26), channel_id=1, source_target_pairs={{0,2},{1,3},{2,0},{3,1},{4,6},{5,7},{6,4},{7,5},{8,10},{9,11},{10,... | collective-permute-start | bytes 393224 | tf_op jit(solution)/shard_map/ppermute | solution.py:106
  157.4 1.2 collective-permute-start.20
  158.7 3.7 %collective-permute-start.21 = (f32[512]{0:T(512)S(1)}, f32[512]{0:T(512)S(1)}, u32[]{:S(2)}, u32[]{:S(2)}) collective-permute-start(f32[512]{0:T(512)S(1)} %fusion.27), channel_id=1, source_target_pairs={{0,2},{1,3},{2,0},{3,1},{4,6},{5,7},{6,4},{7,5},{8,10},{9,11},{10,... | collective-permute-start | bytes 6152 | tf_op jit(solution)/shard_map/ppermute | solution.py:106
  162.3 3.6 %collective-permute-start.22 = (f32[512]{0:T(512)S(1)}, f32[512]{0:T(512)S(1)}, u32[]{:S(2)}, u32[]{:S(2)}) collective-permute-start(f32[512]{0:T(512)S(1)} %add.85), channel_id=1, source_target_pairs={{0,4},{1,5},{2,6},{3,7},{4,0},{5,1},{6,2},{7,3},{8,12},{9,13},{10,... | collective-permute-start | bytes 6152 | tf_op jit(solution)/shard_map/ppermute | solution.py:106
  165.9 4.5 %collective-permute-start.23 = (f32[512]{0:T(512)S(1)}, f32[512]{0:T(512)S(1)}, u32[]{:S(2)}, u32[]{:S(2)}) collective-permute-start(f32[512]{0:T(512)S(1)} %add.86), channel_id=1, source_target_pairs={{0,8},{1,9},{2,10},{3,11},{4,12},{5,13},{6,14},{7,15},{8,0},{9,1},... | collective-permute-start | bytes 6152 | tf_op jit(solution)/shard_map/ppermute | solution.py:106

commit v4 on v3

--- a/solution.py
+++ b/solution.py
@@ -19,20 +19,24 @@
 def product_kernel(half, with_total, waits, place, *refs):
     refs = refs[waits:]
     if with_total:
-        hidden, other_hidden, weight, total_send, total_keep, send, keep = refs
+        hidden, other_hidden, weight, weight_2, total_send, total_keep, send, keep = refs
     else:
-        hidden, other_hidden, weight, send, keep = refs
+        hidden, other_hidden, weight, weight_2, send, keep = refs
     step = pl.program_id(0)
     left = jnp.where(place[2] == 1, hidden[...], other_hidden[...])
-    value = jnp.dot(left, weight[...], preferred_element_type=jnp.float32)
+    values = [
+        jnp.dot(left, part[...], preferred_element_type=jnp.float32) for part in (weight, weight_2)
+    ]
 
-    @pl.when(step < half)
+    @pl.when(step < half // 2)
     def _():
-        send[0] = value + total_send[0] if with_total else value
+        for i in range(2):
+            send[i] = values[i] + total_send[i] if with_total else values[i]
 
-    @pl.when(step >= half)
+    @pl.when(step >= half // 2)
     def _():
-        keep[0] = value + total_keep[0] if with_total else value
+        for i in range(2):
+            keep[i] = values[i] + total_keep[i] if with_total else values[i]
 
 
 def product(hidden, other_hidden, first_hidden, weight, slot, own, blocks, cols, total=None, token_block=0, wait=()):
@@ -40,25 +44,26 @@
     half = blocks // 2
 
     def first(step):
-        return jnp.minimum(step, half - 1)
+        return jnp.minimum(step, half // 2 - 1)
 
     def second(step):
-        return jnp.maximum(step - half, 0)
+        return jnp.maximum(step - half // 2, 0)
 
-    def weight_at(step, place):
-        block = jnp.where(step < half, 2 * step + 1, 2 * (step - half))
+    def weight_at(i, step, place):
+        block = jnp.where(step < half // 2, 4 * step + 1, 4 * step - 2 * half) + 2 * i
         return place[0], lax.bitwise_xor(place[1], block)
 
     in_specs = [pl.BlockSpec((16, 128), lambda step, place: (0, 0)) for _ in wait] + [
         pl.BlockSpec((tokens, units), lambda step, place: (0, 0)),
         pl.BlockSpec((tokens, units), lambda step, place: (0, 0)),
-        pl.BlockSpec((units, cols), weight_at),
+        pl.BlockSpec((units, cols), functools.partial(weight_at, 0)),
+        pl.BlockSpec((units, cols), functools.partial(weight_at, 1)),
     ]
-    operands = [*wait, hidden, other_hidden, weight]
+    operands = [*wait, hidden, other_hidden, weight, weight]
     if total is not None:
         in_specs += [
-            pl.BlockSpec((1, tokens, cols), lambda step, place: (first(step), token_block, 0)),
-            pl.BlockSpec((1, tokens, cols), lambda step, place: (second(step), token_block, 0)),
+            pl.BlockSpec((2, tokens, cols), lambda step, place: (first(step), token_block, 0)),
+            pl.BlockSpec((2, tokens, cols), lambda step, place: (second(step), token_block, 0)),
         ]
         operands += list(total)
     out = jax.ShapeDtypeStruct((half, tokens, cols), jnp.float32)
@@ -66,11 +71,11 @@
         functools.partial(product_kernel, half, total is not None, len(wait)),
         grid_spec=pltpu.PrefetchScalarGridSpec(
             num_scalar_prefetch=1,
-            grid=(blocks,),
+            grid=(blocks // 2,),
             in_specs=in_specs,
             out_specs=[
-                pl.BlockSpec((1, tokens, cols), lambda step, place: (first(step), 0, 0)),
-                pl.BlockSpec((1, tokens, cols), lambda step, place: (second(step), 0, 0)),
+                pl.BlockSpec((2, tokens, cols), lambda step, place: (first(step), 0, 0)),
+                pl.BlockSpec((2, tokens, cols), lambda step, place: (second(step), 0, 0)),
             ],
         ),
         out_shape=[out, out],

time: 172 us -> 171 us (level)
  Pallas kernels: 61.9 us -> 56 us
  waiting for transfers between devices: 64.7 us -> 69.9 us
    pallas_call x10, Pallas kernels: 61.9 us -> 56 us  [product(): pl.pallas_call(functools.partial(product_kernel, half, total is not None,...]
    ppermute x12, waiting for transfers between devices: 52.3 us -> 57.5 us  [move(): lax.ppermute(value, 'row', [(s * plane + i, t * plane + i) for s, t in pa...]
  transfers between devices with their start and end apart: 24 -> 24, of which waited for: 12 -> 12; matrix products, arithmetic and copies ran while one was open for 4% -> 4% of each run, Pallas kernels for 36% -> 33%
where the time goes in v4:
time: 171 us
  waiting for transfers between devices  69.9 us (41%)
  Pallas kernels  56 us (33%)
  starting transfers between devices  31.2 us (18%)
  local copies, waits for them, and re-layouts  6.38 us (4%)
  other arithmetic  6.36 us (4%)
    ppermute x12, waiting for transfers between devices, move(): lax.ppermute(value, 'row', [(s * plane + i, t * plane + i) for s, t in pa...  57.5 us
    pallas_call x10, Pallas kernels, product(): pl.pallas_call(functools.partial(product_kernel, half, total is not None,...  56 us
    ppermute x12, starting transfers between devices, move(): lax.ppermute(value, 'row', [(s * plane + i, t * plane + i) for s, t in pa...  21.2 us
    ppermute x12, waiting for transfers between devices, swap(): lax.ppermute(value, 'row', [(i, i ^ 1 << bit) for i in range(devices)])  12.4 us
    ppermute x12, starting transfers between devices, swap(): lax.ppermute(value, 'row', [(i, i ^ 1 << bit) for i in range(devices)])  10.1 us
    slice x2, local copies, waits for them, and re-layouts, local(): piece = far[i][start:stop]  3.57 us
    convert_element_type x1, other arithmetic, gated(): (jax.nn.silu(gate_pre.astype(jnp.float32)) * up_pre.astype(jnp.float32))....  3.5 us
  transfers between devices with their start and end apart: 24, of which 12 were waited for; matrix products, arithmetic and copies ran while one was open for 4% of the time, Pallas kernels for 33%

profile of v4, /device:TPU:0, one launch (start us, length us, event | category | flops | bytes accessed | tf_op | source)
XLA Modules:
  0.0 170.8 jit_solution(18180042390223389714)
XLA Ops:
  0.6 3.5 %fusion.8 = (bf16[256,2048]{1,0:T(8,128)(2,1)S(1)}, bf16[256,2048]{1,0:T(8,128)(2,1)S(1)}) fusion(bf16[512,2048]{1,0:T(8,128)(2,1)} %param.6, bf16[512,2048]{1,0:T(8,128)(2,1)} %param.5), kind=kLoop, calls=%fused_computation.12 | loop fusion | flops 8388608 | bytes 6291456 | tf_op jit(solution)/shard_map/convert_element_type | solution.py:14
  4.1 3.1 %collective-permute-start = (bf16[256,2048]{1,0:T(8,128)(2,1)S(1)}, bf16[256,2048]{1,0:T(8,128)(2,1)}, u32[]{:S(2)}, u32[]{:S(2)}) collective-permute-start(bf16[256,2048]{1,0:T(8,128)(2,1)S(1)} %get-tuple-element.51.refs_0_.refs_1_), channel_id=1, source_target_pairs={{0,4},{1,5},{2,6},{3,7},{4,0},{5,1},{6,2},{7,3},{8,12},{9,13},{10,... | collective-permute-start | bytes 3145736 | tf_op jit(solution)/shard_map/ppermute | solution.py:106
  7.2 1.6 collective-permute-start.3
  8.9 3.5 %collective-permute-start.7 = (bf16[256,2048]{1,0:T(8,128)(2,1)S(1)}, bf16[256,2048]{1,0:T(8,128)(2,1)S(1)}, u32[]{:S(2)}, u32[]{:S(2)}) collective-permute-start(bf16[256,2048]{1,0:T(8,128)(2,1)S(1)} %get-tuple-element.50.refs_0_.refs_1_), channel_id=1, source_target_pairs={{0,4},{1,5},{2,6},{3,7},{4,0},{5,1},{6,2},{7,3},{8,12},{9,13},{10,... | collective-permute-start | bytes 3145736 | tf_op jit(solution)/shard_map/ppermute | solution.py:106
  12.4 19.0 %collective-permute-done.refs_0_.refs_1_ = bf16[256,2048]{1,0:T(8,128)(2,1)} collective-permute-done((bf16[256,2048]{1,0:T(8,128)(2,1)S(1)}, bf16[256,2048]{1,0:T(8,128)(2,1)}, u32[]{:S(2)}, u32[]{:S(2)}) %collective-permute-start) | collective-permute-done | bytes 1048608 | tf_op jit(solution)/shard_map/ppermute | solution.py:106
  31.3 1.7 collective-permute-start.1
  33.0 1.6 collective-permute-start.10
  34.6 0.1 add_add_fusion.place
  34.7 1.3 collective-permute-start.4
  36.0 0.1 pad_add_fusion.place
  36.1 17.6 %collective-permute-done.7.refs_0_.refs_1_ = bf16[256,2048]{1,0:T(8,128)(2,1)S(1)} collective-permute-done((bf16[256,2048]{1,0:T(8,128)(2,1)S(1)}, bf16[256,2048]{1,0:T(8,128)(2,1)S(1)}, u32[]{:S(2)}, u32[]{:S(2)}) %collective-permute-start.7) | collective-permute-done | bytes 1048608 | tf_op jit(solution)/shard_map/ppermute | solution.py:106
  53.7 1.6 collective-permute-start.8
  55.3 2.3 %fusion.33 = (bf16[128,2048]{1,0:T(8,128)(2,1)}, bf16[128,2048]{1,0:T(8,128)(2,1)}) fusion(bf16[256,2048]{1,0:T(8,128)(2,1)} %collective-permute-done.1), kind=kLoop, calls=%fused_computation.57 | loop fusion | bytes 2097152 | tf_op jit(solution)/shard_map/slice | solution.py:148
  57.6 1.3 collective-permute-start.2
  58.9 5.5 %shard_map.68 = (f32[2,256,512]{2,1,0:T(8,128)S(1)}, f32[2,256,512]{2,1,0:T(8,128)S(1)}) custom-call(s32[3]{0:T(128)S(1)} %pad_add_fusion.place, bf16[256,2048]{1,0:T(8,128)(2,1)S(1)} %get-tuple-element.51.refs_0_.refs_1_, bf16[256,2048]{1,0:T(8,128)(2,1)S(1)} %get-tuple-element.51.refs_0_.refs_1_, bf16[8192,2048]{1,0:T(8,128)(2,1)} %refs_4_.3, ...), custom_call_target="tpu_custom_call" | custom-call | flops 966367616 | bytes 6134169 | tf_op jit(solution)/shard_map/pallas_call | solution.py:70
  64.4 1.0 copy-done.1
  65.4 1.0 copy-done.3
  66.3 1.4 collective-permute-start.14
  67.7 5.5 %shard_map.72 = (f32[2,256,512]{2,1,0:T(8,128)S(1)}, f32[2,256,512]{2,1,0:T(8,128)S(1)}) custom-call(s32[3]{0:T(128)S(1)} %pad_add_fusion.place, bf16[256,2048]{1,0:T(8,128)(2,1)S(1)} %get-tuple-element.50.refs_0_.refs_1_, bf16[256,2048]{1,0:T(8,128)(2,1)S(1)} %get-tuple-element.50.refs_0_.refs_1_, bf16[8192,2048]{1,0:T(8,128)(2,1)} %refs_4_.3, ...), custom_call_target="tpu_custom_call" | custom-call | flops 966367616 | bytes 6134169 | tf_op jit(solution)/shard_map/pallas_call | solution.py:70
  73.2 0.1 add_add_fusion.1.place
  73.3 0.1 pad_add_fusion.1.place
  73.4 1.3 collective-permute-start.11
  74.7 7.3 %shard_map.69 = (f32[2,256,512]{2,1,0:T(8,128)S(1)}, f32[2,256,512]{2,1,0:T(8,128)S(1)}) custom-call(s32[3]{0:T(128)S(1)} %pad_add_fusion.1.place, bf16[256,2048]{1,0:T(8,128)(2,1)} %collective-permute-done.refs_0_.refs_1_, bf16[256,2048]{1,0:T(8,128)(2,1)} %collective-permute-done.refs_0_.refs_1_, bf16[8192,2048]{1,0:T(8,128)(2,1)} %refs_4_.3, ...), custom_call_target="tpu_custom_call" | custom-call | flops 966367616 | bytes 6134169 | tf_op jit(solution)/shard_map/pallas_call | solution.py:70
  82.0 6.2 %shard_map.70 = (f32[2,256,512]{2,1,0:T(8,128)S(1)}, f32[2,256,512]{2,1,0:T(8,128)S(1)}) custom-call(s32[3]{0:T(128)S(1)} %add_add_fusion.1.place, bf16[256,2048]{1,0:T(8,128)(2,1)} %collective-permute-done.3.refs_0_, bf16[256,2048]{1,0:T(8,128)(2,1)} %collective-permute-done.4.refs_1_, bf16[8192,2048]{1,0:T(8,128)(2,1)} %refs_4_.3, ...), custom_call_target="tpu_custom_call" | custom-call | flops 966367616 | bytes 6134169 | tf_op jit(solution)/shard_map/pallas_call | solution.py:70
  88.2 5.2 %shard_map.71 = (f32[2,128,512]{2,1,0:T(8,128)S(1)}, f32[2,128,512]{2,1,0:T(8,128)S(1)}) custom-call(s32[3]{0:T(128)S(1)} %add_add_fusion.place, bf16[128,2048]{1,0:T(8,128)(2,1)} %get-tuple-element.54.refs_0_, bf16[128,2048]{1,0:T(8,128)(2,1)} %collective-permute-done.2.refs_1_, bf16[8192,2048]{1,0:T(8,128)(2,1)} %refs_4_.3, bf16[8192,2048]{1,0:T(8,128)(2,1)} %refs_4_.3, ...), custom_call_target="tpu_custom_call" | custom-call | flops 483183808 | bytes 4954521 | tf_op jit(solution)/shard_map/pallas_call | solution.py:70
  93.5 0.1 collective-permute-start.5
  93.5 5.1 %collective-permute-done.14.refs_1_ = bf16[128,2048]{1,0:T(8,128)(2,1)S(1)} collective-permute-done((bf16[128,2048]{1,0:T(8,128)(2,1)}, bf16[128,2048]{1,0:T(8,128)(2,1)S(1)}, u32[]{:S(2)}, u32[]{:S(2)}) %collective-permute-start.14) | collective-permute-done | bytes 524320 | tf_op jit(solution)/shard_map/ppermute | solution.py:106
  98.6 5.0 %shard_map.76 = (f32[2,128,512]{2,1,0:T(8,128)S(1)}, f32[2,128,512]{2,1,0:T(8,128)S(1)}) custom-call(s32[3]{0:T(128)S(1)} %add_add_fusion.place, bf16[128,2048]{1,0:T(8,128)(2,1)S(1)} %copy-done, bf16[128,2048]{1,0:T(8,128)(2,1)S(1)} %collective-permute-done.14.refs_1_, bf16[8192,2048]{1,0:T(8,128)(2,1)} %refs_4_.3, bf16[8192,2048]{1,0:T(8,128)(2,1)} %refs_4_.3, ...), custom_call_target="tpu_custom_call" | custom-call | flops 483183808 | bytes 4954521 | tf_op jit(solution)/shard_map/pallas_call | solution.py:70
  103.6 0.1 collective-permute-start.15
  103.7 1.3 fusion.32
  105.0 1.3 collective-permute-start.9
  106.3 0.1 add_bitcast_fusion.3
  106.4 2.1 %collective-permute-start.6 = (bf16[1,128,512]{2,1,0:T(8,128)(2,1)S(1)}, bf16[1,128,512]{2,1,0:T(8,128)(2,1)S(1)}, u32[]{:S(2)}, u32[]{:S(2)}) collective-permute-start(bf16[1,128,512]{2,1,0:T(8,128)(2,1)S(1)} %fusion.23), channel_id=1, source_target_pairs={{0,2},{1,3},{2,0},{3,1},{4,6},{5,7},{6,4},{7,5},{8,10},{9,11},{10,... | collective-permute-start | bytes 393224 | tf_op jit(solution)/shard_map/ppermute | solution.py:111
  108.5 0.1 add_bitcast_fusion.1
  108.6 0.1 collective-permute-start.16
  108.7 5.6 %shard_map.73 = (f32[2,256,512]{2,1,0:T(8,128)S(1)}, f32[2,256,512]{2,1,0:T(8,128)S(1)}) custom-call(s32[3]{0:T(128)S(1)} %pad_add_fusion.1.place, bf16[256,2048]{1,0:T(8,128)(2,1)S(1)} %collective-permute-done.7.refs_0_.refs_1_, bf16[256,2048]{1,0:T(8,128)(2,1)S(1)} %collective-permute-done.7.refs_0_.refs_1_, bf16[8192,2048]{1,0:T(8,128)(2,1)} %refs_4_.3, ...), custom_call_target="tpu_custom_call" | custom-call | flops 966367616 | bytes 6134169 | tf_op jit(solution)/shard_map/pallas_call | solution.py:70
  114.3 1.5 collective-permute-start.17
  115.8 5.3 %collective-permute-done.11.refs_1_ = bf16[256,2048]{1,0:T(8,128)(2,1)S(1)} collective-permute-done((bf16[256,2048]{1,0:T(8,128)(2,1)}, bf16[256,2048]{1,0:T(8,128)(2,1)S(1)}, u32[]{:S(2)}, u32[]{:S(2)}) %collective-permute-start.11) | collective-permute-done | bytes 1048608 | tf_op jit(solution)/shard_map/ppermute | solution.py:106
  121.1 5.9 %shard_map.74 = (f32[2,256,512]{2,1,0:T(8,128)S(1)}, f32[2,256,512]{2,1,0:T(8,128)S(1)}) custom-call(s32[3]{0:T(128)S(1)} %add_add_fusion.1.place, bf16[256,2048]{1,0:T(8,128)(2,1)} %collective-permute-done.10.refs_0_, bf16[256,2048]{1,0:T(8,128)(2,1)S(1)} %collective-permute-done.11.refs_1_, bf16[8192,2048]{1,0:T(8,128)(2,1)} %refs_4_.3, ...), custom_call_target="tpu_custom_call" | custom-call | flops 966367616 | bytes 6134169 | tf_op jit(solution)/shard_map/pallas_call | solution.py:70
  127.1 0.2 multiply_reduce_fusion.1
  127.3 5.1 %collective-permute-done.9.refs_2_ = bf16[128,2048]{1,0:T(8,128)(2,1)S(1)} collective-permute-done((bf16[128,2048]{1,0:T(8,128)(2,1)S(1)}, bf16[128,2048]{1,0:T(8,128)(2,1)S(1)}, u32[]{:S(2)}, u32[]{:S(2)}) %collective-permute-start.9) | collective-permute-done | bytes 524320 | tf_op jit(solution)/shard_map/ppermute | solution.py:106
  132.3 4.9 %shard_map.75 = (f32[2,128,512]{2,1,0:T(8,128)S(1)}, f32[2,128,512]{2,1,0:T(8,128)S(1)}) custom-call(s32[3]{0:T(128)S(1)} %add_add_fusion.place, f32[128,512]{1,0:T(8,128)S(1)} %get-tuple-element.47.refs_0_, bf16[128,2048]{1,0:T(8,128)(2,1)S(1)} %get-tuple-element.52.refs_1_, bf16[128,2048]{1,0:T(8,128)(2,1)S(1)} %collective-permute-done.9.refs_2_, ...), custom_call_target="tpu_custom_call" | custom-call | flops 483183808 | bytes 4954521 | tf_op jit(solution)/shard_map/pallas_call | solution.py:70
  137.3 0.1 collective-permute-start.12
  137.4 5.4 %collective-permute-done.17.refs_2_ = bf16[128,2048]{1,0:T(8,128)(2,1)S(1)} collective-permute-done((bf16[128,2048]{1,0:T(8,128)(2,1)S(1)}, bf16[128,2048]{1,0:T(8,128)(2,1)S(1)}, u32[]{:S(2)}, u32[]{:S(2)}) %collective-permute-start.17) | collective-permute-done | bytes 524320 | tf_op jit(solution)/shard_map/ppermute | solution.py:106
  142.7 4.9 %shard_map.77 = (f32[2,128,512]{2,1,0:T(8,128)S(1)}, f32[2,128,512]{2,1,0:T(8,128)S(1)}) custom-call(s32[3]{0:T(128)S(1)} %add_add_fusion.place, f32[128,512]{1,0:T(8,128)S(1)} %get-tuple-element.59.refs_0_, bf16[128,2048]{1,0:T(8,128)(2,1)S(1)} %get-tuple-element.53.refs_1_, bf16[128,2048]{1,0:T(8,128)(2,1)S(1)} %collective-permute-done.17.refs_2_, ...), custom_call_target="tpu_custom_call" | custom-call | flops 483183808 | bytes 4954521 | tf_op jit(solution)/shard_map/pallas_call | solution.py:70
  147.7 0.1 collective-permute-start.18
  147.8 0.1 add_bitcast_fusion.2
  147.9 1.7 %collective-permute-start.13 = (bf16[1,128,512]{2,1,0:T(8,128)(2,1)S(1)}, bf16[1,128,512]{2,1,0:T(8,128)(2,1)S(1)}, u32[]{:S(2)}, u32[]{:S(2)}) collective-permute-start(bf16[1,128,512]{2,1,0:T(8,128)(2,1)S(1)} %fusion.24), channel_id=1, source_target_pairs={{0,2},{1,3},{2,0},{3,1},{4,6},{5,7},{6,4},{7,5},{8,10},{9,11},{10,... | collective-permute-start | bytes 393224 | tf_op jit(solution)/shard_map/ppermute | solution.py:111
  149.6 0.0 collective-permute-done.18
  149.6 0.1 add_bitcast_fusion
  149.8 1.7 %collective-permute-start.19 = (bf16[1,128,512]{2,1,0:T(8,128)(2,1)S(1)}, bf16[1,128,512]{2,1,0:T(8,128)(2,1)S(1)}, u32[]{:S(2)}, u32[]{:S(2)}) collective-permute-start(bf16[1,128,512]{2,1,0:T(8,128)(2,1)S(1)} %fusion.26), channel_id=1, source_target_pairs={{0,2},{1,3},{2,0},{3,1},{4,6},{5,7},{6,4},{7,5},{8,10},{9,11},{10,... | collective-permute-start | bytes 393224 | tf_op jit(solution)/shard_map/ppermute | solution.py:111
  151.5 2.7 %collective-permute-done.13 = bf16[1,128,512]{2,1,0:T(8,128)(2,1)S(1)} collective-permute-done((bf16[1,128,512]{2,1,0:T(8,128)(2,1)S(1)}, bf16[1,128,512]{2,1,0:T(8,128)(2,1)S(1)}, u32[]{:S(2)}, u32[]{:S(2)}) %collective-permute-start.13) | collective-permute-done | bytes 131104 | tf_op jit(solution)/shard_map/ppermute | solution.py:111
  154.2 2.4 %collective-permute-done.19 = bf16[1,128,512]{2,1,0:T(8,128)(2,1)S(1)} collective-permute-done((bf16[1,128,512]{2,1,0:T(8,128)(2,1)S(1)}, bf16[1,128,512]{2,1,0:T(8,128)(2,1)S(1)}, u32[]{:S(2)}, u32[]{:S(2)}) %collective-permute-start.19) | collective-permute-done | bytes 131104 | tf_op jit(solution)/shard_map/ppermute | solution.py:111
  156.6 0.2 multiply_reduce_fusion.3
  156.8 0.1 collective-permute-start.20
  156.9 1.1 collective-permute-done.20
  158.1 1.7 %collective-permute-start.21 = (f32[512]{0:T(512)S(1)}, f32[512]{0:T(512)S(1)}, u32[]{:S(2)}, u32[]{:S(2)}) collective-permute-start(f32[512]{0:T(512)S(1)} %fusion.27), channel_id=1, source_target_pairs={{0,2},{1,3},{2,0},{3,1},{4,6},{5,7},{6,4},{7,5},{8,10},{9,11},{10,... | collective-permute-start | bytes 6152 | tf_op jit(solution)/shard_map/ppermute | solution.py:111
  159.8 1.9 %collective-permute-done.21 = f32[512]{0:T(512)S(1)} collective-permute-done((f32[512]{0:T(512)S(1)}, f32[512]{0:T(512)S(1)}, u32[]{:S(2)}, u32[]{:S(2)}) %collective-permute-start.21) | collective-permute-done | bytes 2080 | tf_op jit(solution)/shard_map/ppermute | solution.py:111
  161.7 0.8 dynamic_slice.3
  162.5 2.8 %collective-permute-done.22 = f32[512]{0:T(512)S(1)} collective-permute-done((f32[512]{0:T(512)S(1)}, f32[512]{0:T(512)S(1)}, u32[]{:S(2)}, u32[]{:S(2)}) %collective-permute-start.22) | collective-permute-done | bytes 2080 | tf_op jit(solution)/shard_map/ppermute | solution.py:111
  165.3 2.3 %collective-permute-start.23 = (f32[512]{0:T(512)S(1)}, f32[512]{0:T(512)S(1)}, u32[]{:S(2)}, u32[]{:S(2)}) collective-permute-start(f32[512]{0:T(512)S(1)} %add.86), channel_id=1, source_target_pairs={{0,8},{1,9},{2,10},{3,11},{4,12},{5,13},{6,14},{7,15},{8,0},{9,1},... | collective-permute-start | bytes 6152 | tf_op jit(solution)/shard_map/ppermute | solution.py:111
  167.6 0.9 fusion.10
  168.5 1.3 collective-permute-done.23
  169.8 1.0 multiply_convert_fusion
  (31 shorter events, 0.2 us)
Async XLA Ops:
  4.1 27.2 %collective-permute-start = (bf16[256,2048]{1,0:T(8,128)(2,1)S(1)}, bf16[256,2048]{1,0:T(8,128)(2,1)}, u32[]{:S(2)}, u32[]{:S(2)}) collective-permute-start(bf16[256,2048]{1,0:T(8,128)(2,1)S(1)} %get-tuple-element.51.refs_0_.refs_1_), channel_id=1, source_target_pairs={{0,4},{1,5},{2,6},{3,7},{4,0},{5,1},{6,2},{7,3},{8,12},{9,13},{10,... | collective-permute-start | bytes 3145736 | tf_op jit(solution)/shard_map/ppermute | solution.py:106
  7.2 27.5 %collective-permute-start.3 = (bf16[256,2048]{1,0:T(8,128)(2,1)S(1)}, bf16[256,2048]{1,0:T(8,128)(2,1)}, u32[]{:S(2)}, u32[]{:S(2)}) collective-permute-start(bf16[256,2048]{1,0:T(8,128)(2,1)S(1)} %get-tuple-element.51.refs_0_.refs_1_), channel_id=1, source_target_pairs={{4,8},{5,9},{6,10},{7,11},{8,4},{9,5},{10,6},{11,7},{20,24},{21,25... | collective-permute-start | bytes 3145736 | tf_op jit(solution)/shard_map/ppermute | solution.py:106
  8.9 44.8 %collective-permute-start.7 = (bf16[256,2048]{1,0:T(8,128)(2,1)S(1)}, bf16[256,2048]{1,0:T(8,128)(2,1)S(1)}, u32[]{:S(2)}, u32[]{:S(2)}) collective-permute-start(bf16[256,2048]{1,0:T(8,128)(2,1)S(1)} %get-tuple-element.50.refs_0_.refs_1_), channel_id=1, source_target_pairs={{0,4},{1,5},{2,6},{3,7},{4,0},{5,1},{6,2},{7,3},{8,12},{9,13},{10,... | collective-permute-start | bytes 3145736 | tf_op jit(solution)/shard_map/ppermute | solution.py:106
  31.3 24.0 %collective-permute-start.1 = (bf16[256,2048]{1,0:T(8,128)(2,1)}, bf16[256,2048]{1,0:T(8,128)(2,1)}, u32[]{:S(2)}, u32[]{:S(2)}) collective-permute-start(bf16[256,2048]{1,0:T(8,128)(2,1)} %collective-permute-done.refs_0_.refs_1_), channel_id=1, source_target_pairs={{4,8},{5,9},{6,10},{7,11},{8,4},{9,5},{10,6},{11,7},{20,24},{21,25... | collective-permute-start | bytes 3145736 | tf_op jit(solution)/shard_map/ppermute | solution.py:106
  33.0 40.4 %collective-permute-start.10 = (bf16[256,2048]{1,0:T(8,128)(2,1)S(1)}, bf16[256,2048]{1,0:T(8,128)(2,1)}, u32[]{:S(2)}, u32[]{:S(2)}) collective-permute-start(bf16[256,2048]{1,0:T(8,128)(2,1)S(1)} %get-tuple-element.50.refs_0_.refs_1_), channel_id=1, source_target_pairs={{4,8},{5,9},{6,10},{7,11},{8,4},{9,5},{10,6},{11,7},{20,24},{21,25... | collective-permute-start | bytes 3145736 | tf_op jit(solution)/shard_map/ppermute | solution.py:106
  34.7 47.3 %collective-permute-start.4 = (bf16[256,2048]{1,0:T(8,128)(2,1)}, bf16[256,2048]{1,0:T(8,128)(2,1)}, u32[]{:S(2)}, u32[]{:S(2)}) collective-permute-start(bf16[256,2048]{1,0:T(8,128)(2,1)} %collective-permute-done.3.refs_0_), channel_id=1, source_target_pairs={{4,0},{5,1},{6,2},{7,3},{8,12},{9,13},{10,14},{11,15},{20,16},{21,... | collective-permute-start | bytes 3145736 | tf_op jit(solution)/shard_map/ppermute | solution.py:106
  53.7 50.0 %collective-permute-start.8 = (bf16[256,2048]{1,0:T(8,128)(2,1)S(1)}, bf16[256,2048]{1,0:T(8,128)(2,1)}, u32[]{:S(2)}, u32[]{:S(2)}) collective-permute-start(bf16[256,2048]{1,0:T(8,128)(2,1)S(1)} %collective-permute-done.7.refs_0_.refs_1_), channel_id=1, source_target_pairs={{4,8},{5,9},{6,10},{7,11},{8,4},{9,5},{10,6},{11,7},{20,24},{21,25... | collective-permute-start | bytes 3145736 | tf_op jit(solution)/shard_map/ppermute | solution.py:106
  57.6 30.6 %collective-permute-start.2 = (bf16[128,2048]{1,0:T(8,128)(2,1)}, bf16[128,2048]{1,0:T(8,128)(2,1)}, u32[]{:S(2)}, u32[]{:S(2)}) collective-permute-start(bf16[128,2048]{1,0:T(8,128)(2,1)} %get-tuple-element.54.refs_0_), channel_id=1, source_target_pairs={{4,0},{5,1},{6,2},{7,3},{8,12},{9,13},{10,14},{11,15},{20,16},{21,... | collective-permute-start | bytes 1572872 | tf_op jit(solution)/shard_map/ppermute | solution.py:106
  64.4 1.0 copy-start.1
  65.4 1.0 copy-start.3
  66.3 8.4 %copy-start.2 = (f32[2,256,512]{2,1,0:T(8,128)S(1)}, f32[2,256,512]{2,1,0:T(8,128)}, u32[]{:S(2)}) copy-start(f32[2,256,512]{2,1,0:T(8,128)} %copy-done.1) | copy-start | bytes 3145732
  66.3 8.4 %copy-start.4 = (f32[2,256,512]{2,1,0:T(8,128)S(1)}, f32[2,256,512]{2,1,0:T(8,128)}, u32[]{:S(2)}) copy-start(f32[2,256,512]{2,1,0:T(8,128)} %copy-done.3) | copy-start | bytes 3145732
  66.3 32.3 %collective-permute-start.14 = (bf16[128,2048]{1,0:T(8,128)(2,1)}, bf16[128,2048]{1,0:T(8,128)(2,1)S(1)}, u32[]{:S(2)}, u32[]{:S(2)}) collective-permute-start(bf16[128,2048]{1,0:T(8,128)(2,1)} %get-tuple-element.55.refs_0_), channel_id=1, source_target_pairs={{4,0},{5,1},{6,2},{7,3},{8,12},{9,13},{10,14},{11,15},{20,16},{21,... | collective-permute-start | bytes 1572872 | tf_op jit(solution)/shard_map/ppermute | solution.py:106
  73.4 47.7 %collective-permute-start.11 = (bf16[256,2048]{1,0:T(8,128)(2,1)}, bf16[256,2048]{1,0:T(8,128)(2,1)S(1)}, u32[]{:S(2)}, u32[]{:S(2)}) collective-permute-start(bf16[256,2048]{1,0:T(8,128)(2,1)} %collective-permute-done.10.refs_0_), channel_id=1, source_target_pairs={{4,0},{5,1},{6,2},{7,3},{8,12},{9,13},{10,14},{11,15},{20,16},{21,... | collective-permute-start | bytes 3145736 | tf_op jit(solution)/shard_map/ppermute | solution.py:106
  88.2 10.4 %copy-start = (bf16[128,2048]{1,0:T(8,128)(2,1)S(1)}, bf16[128,2048]{1,0:T(8,128)(2,1)}, u32[]{:S(2)}) copy-start(bf16[128,2048]{1,0:T(8,128)(2,1)} %get-tuple-element.55.refs_0_) | copy-start | bytes 1572868
  93.5 12.8 %collective-permute-start.5 = (f32[2,128,512]{2,1,0:T(8,128)S(1)}, f32[2,128,512]{2,1,0:T(8,128)S(1)}, u32[]{:S(2)}, u32[]{:S(2)}) collective-permute-start(f32[2,128,512]{2,1,0:T(8,128)S(1)} %get-tuple-element.29), channel_id=1, source_target_pairs={{0,1},{1,0},{2,3},{3,2},{4,5},{5,4},{6,7},{7,6},{8,9},{9,8},{10,11... | collective-permute-start | bytes 1572872 | tf_op jit(solution)/shard_map/ppermute | solution.py:111
  103.6 4.9 %collective-permute-start.15 = (f32[2,128,512]{2,1,0:T(8,128)S(1)}, f32[2,128,512]{2,1,0:T(8,128)S(1)}, u32[]{:S(2)}, u32[]{:S(2)}) collective-permute-start(f32[2,128,512]{2,1,0:T(8,128)S(1)} %get-tuple-element.39), channel_id=1, source_target_pairs={{0,1},{1,0},{2,3},{3,2},{4,5},{5,4},{6,7},{7,6},{8,9},{9,8},{10,11... | collective-permute-start | bytes 1572872 | tf_op jit(solution)/shard_map/ppermute | solution.py:111
  105.0 27.3 %collective-permute-start.9 = (bf16[128,2048]{1,0:T(8,128)(2,1)S(1)}, bf16[128,2048]{1,0:T(8,128)(2,1)S(1)}, u32[]{:S(2)}, u32[]{:S(2)}) collective-permute-start(bf16[128,2048]{1,0:T(8,128)(2,1)S(1)} %get-tuple-element.52.refs_1_), channel_id=1, source_target_pairs={{4,0},{5,1},{6,2},{7,3},{8,12},{9,13},{10,14},{11,15},{20,16},{21,... | collective-permute-start | bytes 1572872 | tf_op jit(solution)/shard_map/ppermute | solution.py:106
  106.4 20.6 %collective-permute-start.6 = (bf16[1,128,512]{2,1,0:T(8,128)(2,1)S(1)}, bf16[1,128,512]{2,1,0:T(8,128)(2,1)S(1)}, u32[]{:S(2)}, u32[]{:S(2)}) collective-permute-start(bf16[1,128,512]{2,1,0:T(8,128)(2,1)S(1)} %fusion.23), channel_id=1, source_target_pairs={{0,2},{1,3},{2,0},{3,1},{4,6},{5,7},{6,4},{7,5},{8,10},{9,11},{10,... | collective-permute-start | bytes 393224 | tf_op jit(solution)/shard_map/ppermute | solution.py:111
  108.6 18.4 %collective-permute-start.16 = (bf16[1,128,512]{2,1,0:T(8,128)(2,1)S(1)}, bf16[1,128,512]{2,1,0:T(8,128)(2,1)S(1)}, u32[]{:S(2)}, u32[]{:S(2)}) collective-permute-start(bf16[1,128,512]{2,1,0:T(8,128)(2,1)S(1)} %fusion.25), channel_id=1, source_target_pairs={{0,2},{1,3},{2,0},{3,1},{4,6},{5,7},{6,4},{7,5},{8,10},{9,11},{10,... | collective-permute-start | bytes 393224 | tf_op jit(solution)/shard_map/ppermute | solution.py:111
  114.3 28.5 %collective-permute-start.17 = (bf16[128,2048]{1,0:T(8,128)(2,1)S(1)}, bf16[128,2048]{1,0:T(8,128)(2,1)S(1)}, u32[]{:S(2)}, u32[]{:S(2)}) collective-permute-start(bf16[128,2048]{1,0:T(8,128)(2,1)S(1)} %get-tuple-element.53.refs_1_), channel_id=1, source_target_pairs={{4,0},{5,1},{6,2},{7,3},{8,12},{9,13},{10,14},{11,15},{20,16},{21,... | collective-permute-start | bytes 1572872 | tf_op jit(solution)/shard_map/ppermute | solution.py:106
  121.1 6.0 %copy-start.5 = (bf16[512,512]{1,0:T(8,128)(2,1)S(1)}, bf16[512,512]{1,0:T(8,128)(2,1)}, u32[]{:S(2)}) copy-start(bf16[512,512]{1,0:T(8,128)(2,1)} %param.7) | copy-start | bytes 1572868
  137.3 10.5 %collective-permute-start.12 = (f32[2,128,512]{2,1,0:T(8,128)S(1)}, f32[2,128,512]{2,1,0:T(8,128)S(1)}, u32[]{:S(2)}, u32[]{:S(2)}) collective-permute-start(f32[2,128,512]{2,1,0:T(8,128)S(1)} %get-tuple-element.37), channel_id=1, source_target_pairs={{0,1},{1,0},{2,3},{3,2},{4,5},{5,4},{6,7},{7,6},{8,9},{9,8},{10,11... | collective-permute-start | bytes 1572872 | tf_op jit(solution)/shard_map/ppermute | solution.py:111
  147.7 2.0 %collective-permute-start.18 = (f32[2,128,512]{2,1,0:T(8,128)S(1)}, f32[2,128,512]{2,1,0:T(8,128)S(1)}, u32[]{:S(2)}, u32[]{:S(2)}) collective-permute-start(f32[2,128,512]{2,1,0:T(8,128)S(1)} %get-tuple-element.41), channel_id=1, source_target_pairs={{0,1},{1,0},{2,3},{3,2},{4,5},{5,4},{6,7},{7,6},{8,9},{9,8},{10,11... | collective-permute-start | bytes 1572872 | tf_op jit(solution)/shard_map/ppermute | solution.py:111
  147.9 6.4 %collective-permute-start.13 = (bf16[1,128,512]{2,1,0:T(8,128)(2,1)S(1)}, bf16[1,128,512]{2,1,0:T(8,128)(2,1)S(1)}, u32[]{:S(2)}, u32[]{:S(2)}) collective-permute-start(bf16[1,128,512]{2,1,0:T(8,128)(2,1)S(1)} %fusion.24), channel_id=1, source_target_pairs={{0,2},{1,3},{2,0},{3,1},{4,6},{5,7},{6,4},{7,5},{8,10},{9,11},{10,... | collective-permute-start | bytes 393224 | tf_op jit(solution)/shard_map/ppermute | solution.py:111
  149.8 6.9 %collective-permute-start.19 = (bf16[1,128,512]{2,1,0:T(8,128)(2,1)S(1)}, bf16[1,128,512]{2,1,0:T(8,128)(2,1)S(1)}, u32[]{:S(2)}, u32[]{:S(2)}) collective-permute-start(bf16[1,128,512]{2,1,0:T(8,128)(2,1)S(1)} %fusion.26), channel_id=1, source_target_pairs={{0,2},{1,3},{2,0},{3,1},{4,6},{5,7},{6,4},{7,5},{8,10},{9,11},{10,... | collective-permute-start | bytes 393224 | tf_op jit(solution)/shard_map/ppermute | solution.py:111
  156.8 1.2 collective-permute-start.20
  158.1 3.7 %collective-permute-start.21 = (f32[512]{0:T(512)S(1)}, f32[512]{0:T(512)S(1)}, u32[]{:S(2)}, u32[]{:S(2)}) collective-permute-start(f32[512]{0:T(512)S(1)} %fusion.27), channel_id=1, source_target_pairs={{0,2},{1,3},{2,0},{3,1},{4,6},{5,7},{6,4},{7,5},{8,10},{9,11},{10,... | collective-permute-start | bytes 6152 | tf_op jit(solution)/shard_map/ppermute | solution.py:111
  161.7 3.6 %collective-permute-start.22 = (f32[512]{0:T(512)S(1)}, f32[512]{0:T(512)S(1)}, u32[]{:S(2)}, u32[]{:S(2)}) collective-permute-start(f32[512]{0:T(512)S(1)} %add.85), channel_id=1, source_target_pairs={{0,4},{1,5},{2,6},{3,7},{4,0},{5,1},{6,2},{7,3},{8,12},{9,13},{10,... | collective-permute-start | bytes 6152 | tf_op jit(solution)/shard_map/ppermute | solution.py:111
  165.3 4.5 %collective-permute-start.23 = (f32[512]{0:T(512)S(1)}, f32[512]{0:T(512)S(1)}, u32[]{:S(2)}, u32[]{:S(2)}) collective-permute-start(f32[512]{0:T(512)S(1)} %add.86), channel_id=1, source_target_pairs={{0,8},{1,9},{2,10},{3,11},{4,12},{5,13},{6,14},{7,15},{8,0},{9,1},... | collective-permute-start | bytes 6152 | tf_op jit(solution)/shard_map/ppermute | solution.py:111

commit v5 on v4

--- a/solution.py
+++ b/solution.py
@@ -160,7 +160,7 @@
             streams[i * part + start] = value[0] + rows.astype(jnp.float32)
     streams = [streams[k] for k in sorted(streams)]
     squares = jnp.concatenate([jnp.sum(s * s, axis=1) for s in streams])
-    for bit in range(all_bits):
+    for bit in reversed(range(all_bits)):
         squares = squares + swap(squares, bit)
     scale = lax.rsqrt(squares / width + 1e-05)
     gain_part = lax.dynamic_slice_in_dim(gain, position * cols, cols, 0)

time: 171 us -> 171 us (level)
  no operation moved by 1% of the time
where the time goes in v5:
time: 171 us
  waiting for transfers between devices  68.9 us (40%)
  Pallas kernels  56 us (33%)
  starting transfers between devices  32.1 us (19%)
  local copies, waits for them, and re-layouts  6.38 us (4%)
  other arithmetic  6.36 us (4%)
    ppermute x12, waiting for transfers between devices, move(): lax.ppermute(value, 'row', [(s * plane + i, t * plane + i) for s, t in pa...  57.5 us
    pallas_call x10, Pallas kernels, product(): pl.pallas_call(functools.partial(product_kernel, half, total is not None,...  56 us
    ppermute x12, starting transfers between devices, move(): lax.ppermute(value, 'row', [(s * plane + i, t * plane + i) for s, t in pa...  21.2 us
    ppermute x12, waiting for transfers between devices, swap(): lax.ppermute(value, 'row', [(i, i ^ 1 << bit) for i in range(devices)])  11.4 us
    ppermute x12, starting transfers between devices, swap(): lax.ppermute(value, 'row', [(i, i ^ 1 << bit) for i in range(devices)])  11 us
    slice x2, local copies, waits for them, and re-layouts, local(): piece = far[i][start:stop]  3.57 us
    convert_element_type x1, other arithmetic, gated(): (jax.nn.silu(gate_pre.astype(jnp.float32)) * up_pre.astype(jnp.float32))....  3.5 us
  transfers between devices with their start and end apart: 24, of which 12 were waited for; matrix products, arithmetic and copies ran while one was open for 4% of the time, Pallas kernels for 33%

profile of v5, /device:TPU:0, one launch (start us, length us, event | category | flops | bytes accessed | tf_op | source)
XLA Modules:
  0.0 170.8 jit_solution(14533846650691404345)
XLA Ops:
  0.6 3.5 %fusion.8 = (bf16[256,2048]{1,0:T(8,128)(2,1)S(1)}, bf16[256,2048]{1,0:T(8,128)(2,1)S(1)}) fusion(bf16[512,2048]{1,0:T(8,128)(2,1)} %param.6, bf16[512,2048]{1,0:T(8,128)(2,1)} %param.5), kind=kLoop, calls=%fused_computation.12 | loop fusion | flops 8388608 | bytes 6291456 | tf_op jit(solution)/shard_map/convert_element_type | solution.py:14
  4.1 3.1 %collective-permute-start = (bf16[256,2048]{1,0:T(8,128)(2,1)S(1)}, bf16[256,2048]{1,0:T(8,128)(2,1)}, u32[]{:S(2)}, u32[]{:S(2)}) collective-permute-start(bf16[256,2048]{1,0:T(8,128)(2,1)S(1)} %get-tuple-element.51.refs_0_.refs_1_), channel_id=1, source_target_pairs={{0,4},{1,5},{2,6},{3,7},{4,0},{5,1},{6,2},{7,3},{8,12},{9,13},{10,... | collective-permute-start | bytes 3145736 | tf_op jit(solution)/shard_map/ppermute | solution.py:106
  7.2 1.6 collective-permute-start.3
  8.9 3.5 %collective-permute-start.7 = (bf16[256,2048]{1,0:T(8,128)(2,1)S(1)}, bf16[256,2048]{1,0:T(8,128)(2,1)S(1)}, u32[]{:S(2)}, u32[]{:S(2)}) collective-permute-start(bf16[256,2048]{1,0:T(8,128)(2,1)S(1)} %get-tuple-element.50.refs_0_.refs_1_), channel_id=1, source_target_pairs={{0,4},{1,5},{2,6},{3,7},{4,0},{5,1},{6,2},{7,3},{8,12},{9,13},{10,... | collective-permute-start | bytes 3145736 | tf_op jit(solution)/shard_map/ppermute | solution.py:106
  12.4 19.0 %collective-permute-done.refs_0_.refs_1_ = bf16[256,2048]{1,0:T(8,128)(2,1)} collective-permute-done((bf16[256,2048]{1,0:T(8,128)(2,1)S(1)}, bf16[256,2048]{1,0:T(8,128)(2,1)}, u32[]{:S(2)}, u32[]{:S(2)}) %collective-permute-start) | collective-permute-done | bytes 1048608 | tf_op jit(solution)/shard_map/ppermute | solution.py:106
  31.3 1.7 collective-permute-start.1
  33.0 1.6 collective-permute-start.10
  34.6 0.1 add_add_fusion.place
  34.7 1.3 collective-permute-start.4
  36.0 0.1 pad_add_fusion.place
  36.1 17.6 %collective-permute-done.7.refs_0_.refs_1_ = bf16[256,2048]{1,0:T(8,128)(2,1)S(1)} collective-permute-done((bf16[256,2048]{1,0:T(8,128)(2,1)S(1)}, bf16[256,2048]{1,0:T(8,128)(2,1)S(1)}, u32[]{:S(2)}, u32[]{:S(2)}) %collective-permute-start.7) | collective-permute-done | bytes 1048608 | tf_op jit(solution)/shard_map/ppermute | solution.py:106
  53.7 1.6 collective-permute-start.8
  55.3 2.3 %fusion.33 = (bf16[128,2048]{1,0:T(8,128)(2,1)}, bf16[128,2048]{1,0:T(8,128)(2,1)}) fusion(bf16[256,2048]{1,0:T(8,128)(2,1)} %collective-permute-done.1), kind=kLoop, calls=%fused_computation.57 | loop fusion | bytes 2097152 | tf_op jit(solution)/shard_map/slice | solution.py:148
  57.6 1.3 collective-permute-start.2
  58.9 5.5 %shard_map.68 = (f32[2,256,512]{2,1,0:T(8,128)S(1)}, f32[2,256,512]{2,1,0:T(8,128)S(1)}) custom-call(s32[3]{0:T(128)S(1)} %pad_add_fusion.place, bf16[256,2048]{1,0:T(8,128)(2,1)S(1)} %get-tuple-element.51.refs_0_.refs_1_, bf16[256,2048]{1,0:T(8,128)(2,1)S(1)} %get-tuple-element.51.refs_0_.refs_1_, bf16[8192,2048]{1,0:T(8,128)(2,1)} %refs_4_.3, ...), custom_call_target="tpu_custom_call" | custom-call | flops 966367616 | bytes 6134169 | tf_op jit(solution)/shard_map/pallas_call | solution.py:70
  64.4 1.0 copy-done.1
  65.4 1.0 copy-done.3
  66.3 1.4 collective-permute-start.14
  67.7 5.5 %shard_map.72 = (f32[2,256,512]{2,1,0:T(8,128)S(1)}, f32[2,256,512]{2,1,0:T(8,128)S(1)}) custom-call(s32[3]{0:T(128)S(1)} %pad_add_fusion.place, bf16[256,2048]{1,0:T(8,128)(2,1)S(1)} %get-tuple-element.50.refs_0_.refs_1_, bf16[256,2048]{1,0:T(8,128)(2,1)S(1)} %get-tuple-element.50.refs_0_.refs_1_, bf16[8192,2048]{1,0:T(8,128)(2,1)} %refs_4_.3, ...), custom_call_target="tpu_custom_call" | custom-call | flops 966367616 | bytes 6134169 | tf_op jit(solution)/shard_map/pallas_call | solution.py:70
  73.2 0.1 add_add_fusion.1.place
  73.3 0.1 pad_add_fusion.1.place
  73.4 1.3 collective-permute-start.11
  74.7 7.3 %shard_map.69 = (f32[2,256,512]{2,1,0:T(8,128)S(1)}, f32[2,256,512]{2,1,0:T(8,128)S(1)}) custom-call(s32[3]{0:T(128)S(1)} %pad_add_fusion.1.place, bf16[256,2048]{1,0:T(8,128)(2,1)} %collective-permute-done.refs_0_.refs_1_, bf16[256,2048]{1,0:T(8,128)(2,1)} %collective-permute-done.refs_0_.refs_1_, bf16[8192,2048]{1,0:T(8,128)(2,1)} %refs_4_.3, ...), custom_call_target="tpu_custom_call" | custom-call | flops 966367616 | bytes 6134169 | tf_op jit(solution)/shard_map/pallas_call | solution.py:70
  82.0 6.2 %shard_map.70 = (f32[2,256,512]{2,1,0:T(8,128)S(1)}, f32[2,256,512]{2,1,0:T(8,128)S(1)}) custom-call(s32[3]{0:T(128)S(1)} %add_add_fusion.1.place, bf16[256,2048]{1,0:T(8,128)(2,1)} %collective-permute-done.3.refs_0_, bf16[256,2048]{1,0:T(8,128)(2,1)} %collective-permute-done.4.refs_1_, bf16[8192,2048]{1,0:T(8,128)(2,1)} %refs_4_.3, ...), custom_call_target="tpu_custom_call" | custom-call | flops 966367616 | bytes 6134169 | tf_op jit(solution)/shard_map/pallas_call | solution.py:70
  88.2 5.2 %shard_map.71 = (f32[2,128,512]{2,1,0:T(8,128)S(1)}, f32[2,128,512]{2,1,0:T(8,128)S(1)}) custom-call(s32[3]{0:T(128)S(1)} %add_add_fusion.place, bf16[128,2048]{1,0:T(8,128)(2,1)} %get-tuple-element.54.refs_0_, bf16[128,2048]{1,0:T(8,128)(2,1)} %collective-permute-done.2.refs_1_, bf16[8192,2048]{1,0:T(8,128)(2,1)} %refs_4_.3, bf16[8192,2048]{1,0:T(8,128)(2,1)} %refs_4_.3, ...), custom_call_target="tpu_custom_call" | custom-call | flops 483183808 | bytes 4954521 | tf_op jit(solution)/shard_map/pallas_call | solution.py:70
  93.5 0.1 collective-permute-start.5
  93.5 5.1 %collective-permute-done.14.refs_1_ = bf16[128,2048]{1,0:T(8,128)(2,1)S(1)} collective-permute-done((bf16[128,2048]{1,0:T(8,128)(2,1)}, bf16[128,2048]{1,0:T(8,128)(2,1)S(1)}, u32[]{:S(2)}, u32[]{:S(2)}) %collective-permute-start.14) | collective-permute-done | bytes 524320 | tf_op jit(solution)/shard_map/ppermute | solution.py:106
  98.6 5.0 %shard_map.76 = (f32[2,128,512]{2,1,0:T(8,128)S(1)}, f32[2,128,512]{2,1,0:T(8,128)S(1)}) custom-call(s32[3]{0:T(128)S(1)} %add_add_fusion.place, bf16[128,2048]{1,0:T(8,128)(2,1)S(1)} %copy-done, bf16[128,2048]{1,0:T(8,128)(2,1)S(1)} %collective-permute-done.14.refs_1_, bf16[8192,2048]{1,0:T(8,128)(2,1)} %refs_4_.3, bf16[8192,2048]{1,0:T(8,128)(2,1)} %refs_4_.3, ...), custom_call_target="tpu_custom_call" | custom-call | flops 483183808 | bytes 4954521 | tf_op jit(solution)/shard_map/pallas_call | solution.py:70
  103.6 0.1 collective-permute-start.15
  103.7 1.3 fusion.32
  105.0 1.3 collective-permute-start.9
  106.3 0.1 add_bitcast_fusion.3
  106.4 2.1 %collective-permute-start.6 = (bf16[1,128,512]{2,1,0:T(8,128)(2,1)S(1)}, bf16[1,128,512]{2,1,0:T(8,128)(2,1)S(1)}, u32[]{:S(2)}, u32[]{:S(2)}) collective-permute-start(bf16[1,128,512]{2,1,0:T(8,128)(2,1)S(1)} %fusion.23), channel_id=1, source_target_pairs={{0,2},{1,3},{2,0},{3,1},{4,6},{5,7},{6,4},{7,5},{8,10},{9,11},{10,... | collective-permute-start | bytes 393224 | tf_op jit(solution)/shard_map/ppermute | solution.py:111
  108.5 0.1 add_bitcast_fusion.1
  108.6 0.1 collective-permute-start.16
  108.7 5.6 %shard_map.73 = (f32[2,256,512]{2,1,0:T(8,128)S(1)}, f32[2,256,512]{2,1,0:T(8,128)S(1)}) custom-call(s32[3]{0:T(128)S(1)} %pad_add_fusion.1.place, bf16[256,2048]{1,0:T(8,128)(2,1)S(1)} %collective-permute-done.7.refs_0_.refs_1_, bf16[256,2048]{1,0:T(8,128)(2,1)S(1)} %collective-permute-done.7.refs_0_.refs_1_, bf16[8192,2048]{1,0:T(8,128)(2,1)} %refs_4_.3, ...), custom_call_target="tpu_custom_call" | custom-call | flops 966367616 | bytes 6134169 | tf_op jit(solution)/shard_map/pallas_call | solution.py:70
  114.3 1.5 collective-permute-start.17
  115.8 5.3 %collective-permute-done.11.refs_1_ = bf16[256,2048]{1,0:T(8,128)(2,1)S(1)} collective-permute-done((bf16[256,2048]{1,0:T(8,128)(2,1)}, bf16[256,2048]{1,0:T(8,128)(2,1)S(1)}, u32[]{:S(2)}, u32[]{:S(2)}) %collective-permute-start.11) | collective-permute-done | bytes 1048608 | tf_op jit(solution)/shard_map/ppermute | solution.py:106
  121.1 5.9 %shard_map.74 = (f32[2,256,512]{2,1,0:T(8,128)S(1)}, f32[2,256,512]{2,1,0:T(8,128)S(1)}) custom-call(s32[3]{0:T(128)S(1)} %add_add_fusion.1.place, bf16[256,2048]{1,0:T(8,128)(2,1)} %collective-permute-done.10.refs_0_, bf16[256,2048]{1,0:T(8,128)(2,1)S(1)} %collective-permute-done.11.refs_1_, bf16[8192,2048]{1,0:T(8,128)(2,1)} %refs_4_.3, ...), custom_call_target="tpu_custom_call" | custom-call | flops 966367616 | bytes 6134169 | tf_op jit(solution)/shard_map/pallas_call | solution.py:70
  127.1 0.2 multiply_reduce_fusion.1
  127.3 5.1 %collective-permute-done.9.refs_2_ = bf16[128,2048]{1,0:T(8,128)(2,1)S(1)} collective-permute-done((bf16[128,2048]{1,0:T(8,128)(2,1)S(1)}, bf16[128,2048]{1,0:T(8,128)(2,1)S(1)}, u32[]{:S(2)}, u32[]{:S(2)}) %collective-permute-start.9) | collective-permute-done | bytes 524320 | tf_op jit(solution)/shard_map/ppermute | solution.py:106
  132.3 4.9 %shard_map.75 = (f32[2,128,512]{2,1,0:T(8,128)S(1)}, f32[2,128,512]{2,1,0:T(8,128)S(1)}) custom-call(s32[3]{0:T(128)S(1)} %add_add_fusion.place, f32[128,512]{1,0:T(8,128)S(1)} %get-tuple-element.47.refs_0_, bf16[128,2048]{1,0:T(8,128)(2,1)S(1)} %get-tuple-element.52.refs_1_, bf16[128,2048]{1,0:T(8,128)(2,1)S(1)} %collective-permute-done.9.refs_2_, ...), custom_call_target="tpu_custom_call" | custom-call | flops 483183808 | bytes 4954521 | tf_op jit(solution)/shard_map/pallas_call | solution.py:70
  137.3 0.1 collective-permute-start.12
  137.4 5.4 %collective-permute-done.17.refs_2_ = bf16[128,2048]{1,0:T(8,128)(2,1)S(1)} collective-permute-done((bf16[128,2048]{1,0:T(8,128)(2,1)S(1)}, bf16[128,2048]{1,0:T(8,128)(2,1)S(1)}, u32[]{:S(2)}, u32[]{:S(2)}) %collective-permute-start.17) | collective-permute-done | bytes 524320 | tf_op jit(solution)/shard_map/ppermute | solution.py:106
  142.7 4.9 %shard_map.77 = (f32[2,128,512]{2,1,0:T(8,128)S(1)}, f32[2,128,512]{2,1,0:T(8,128)S(1)}) custom-call(s32[3]{0:T(128)S(1)} %add_add_fusion.place, f32[128,512]{1,0:T(8,128)S(1)} %get-tuple-element.59.refs_0_, bf16[128,2048]{1,0:T(8,128)(2,1)S(1)} %get-tuple-element.53.refs_1_, bf16[128,2048]{1,0:T(8,128)(2,1)S(1)} %collective-permute-done.17.refs_2_, ...), custom_call_target="tpu_custom_call" | custom-call | flops 483183808 | bytes 4954521 | tf_op jit(solution)/shard_map/pallas_call | solution.py:70
  147.7 0.1 collective-permute-start.18
  147.8 0.1 add_bitcast_fusion.2
  147.9 1.7 %collective-permute-start.13 = (bf16[1,128,512]{2,1,0:T(8,128)(2,1)S(1)}, bf16[1,128,512]{2,1,0:T(8,128)(2,1)S(1)}, u32[]{:S(2)}, u32[]{:S(2)}) collective-permute-start(bf16[1,128,512]{2,1,0:T(8,128)(2,1)S(1)} %fusion.24), channel_id=1, source_target_pairs={{0,2},{1,3},{2,0},{3,1},{4,6},{5,7},{6,4},{7,5},{8,10},{9,11},{10,... | collective-permute-start | bytes 393224 | tf_op jit(solution)/shard_map/ppermute | solution.py:111
  149.6 0.0 collective-permute-done.18
  149.6 0.1 add_bitcast_fusion
  149.8 1.7 %collective-permute-start.19 = (bf16[1,128,512]{2,1,0:T(8,128)(2,1)S(1)}, bf16[1,128,512]{2,1,0:T(8,128)(2,1)S(1)}, u32[]{:S(2)}, u32[]{:S(2)}) collective-permute-start(bf16[1,128,512]{2,1,0:T(8,128)(2,1)S(1)} %fusion.26), channel_id=1, source_target_pairs={{0,2},{1,3},{2,0},{3,1},{4,6},{5,7},{6,4},{7,5},{8,10},{9,11},{10,... | collective-permute-start | bytes 393224 | tf_op jit(solution)/shard_map/ppermute | solution.py:111
  151.5 2.7 %collective-permute-done.13 = bf16[1,128,512]{2,1,0:T(8,128)(2,1)S(1)} collective-permute-done((bf16[1,128,512]{2,1,0:T(8,128)(2,1)S(1)}, bf16[1,128,512]{2,1,0:T(8,128)(2,1)S(1)}, u32[]{:S(2)}, u32[]{:S(2)}) %collective-permute-start.13) | collective-permute-done | bytes 131104 | tf_op jit(solution)/shard_map/ppermute | solution.py:111
  154.2 2.4 %collective-permute-done.19 = bf16[1,128,512]{2,1,0:T(8,128)(2,1)S(1)} collective-permute-done((bf16[1,128,512]{2,1,0:T(8,128)(2,1)S(1)}, bf16[1,128,512]{2,1,0:T(8,128)(2,1)S(1)}, u32[]{:S(2)}, u32[]{:S(2)}) %collective-permute-start.19) | collective-permute-done | bytes 131104 | tf_op jit(solution)/shard_map/ppermute | solution.py:111
  156.6 0.2 multiply_reduce_fusion.3
  156.8 1.9 %collective-permute-start.20 = (f32[512]{0:T(512)S(1)}, f32[512]{0:T(512)S(1)}, u32[]{:S(2)}, u32[]{:S(2)}) collective-permute-start(f32[512]{0:T(512)S(1)} %pad_maximum_fusion.1), channel_id=1, source_target_pairs={{0,8},{1,9},{2,10},{3,11},{4,12},{5,13},{6,14},{7,15},{8,0},{9,1},... | collective-permute-start | bytes 6152 | tf_op jit(solution)/shard_map/ppermute | solution.py:111
  158.7 2.6 %collective-permute-done.20 = f32[512]{0:T(512)S(1)} collective-permute-done((f32[512]{0:T(512)S(1)}, f32[512]{0:T(512)S(1)}, u32[]{:S(2)}, u32[]{:S(2)}) %collective-permute-start.20) | collective-permute-done | bytes 2080 | tf_op jit(solution)/shard_map/ppermute | solution.py:111
  161.4 1.5 collective-permute-start.21
  162.9 2.2 %collective-permute-done.21 = f32[512]{0:T(512)S(1)} collective-permute-done((f32[512]{0:T(512)S(1)}, f32[512]{0:T(512)S(1)}, u32[]{:S(2)}, u32[]{:S(2)}) %collective-permute-start.21) | collective-permute-done | bytes 2080 | tf_op jit(solution)/shard_map/ppermute | solution.py:111
  165.1 1.7 collective-permute-start.22
  166.7 0.8 dynamic_slice.3
  167.5 1.1 collective-permute-done.22
  168.6 0.9 fusion.10
  169.5 0.3 collective-permute-done.23
  169.8 1.0 multiply_convert_fusion
  (31 shorter events, 0.2 us)
Async XLA Ops:
  4.1 27.2 %collective-permute-start = (bf16[256,2048]{1,0:T(8,128)(2,1)S(1)}, bf16[256,2048]{1,0:T(8,128)(2,1)}, u32[]{:S(2)}, u32[]{:S(2)}) collective-permute-start(bf16[256,2048]{1,0:T(8,128)(2,1)S(1)} %get-tuple-element.51.refs_0_.refs_1_), channel_id=1, source_target_pairs={{0,4},{1,5},{2,6},{3,7},{4,0},{5,1},{6,2},{7,3},{8,12},{9,13},{10,... | collective-permute-start | bytes 3145736 | tf_op jit(solution)/shard_map/ppermute | solution.py:106
  7.2 27.5 %collective-permute-start.3 = (bf16[256,2048]{1,0:T(8,128)(2,1)S(1)}, bf16[256,2048]{1,0:T(8,128)(2,1)}, u32[]{:S(2)}, u32[]{:S(2)}) collective-permute-start(bf16[256,2048]{1,0:T(8,128)(2,1)S(1)} %get-tuple-element.51.refs_0_.refs_1_), channel_id=1, source_target_pairs={{4,8},{5,9},{6,10},{7,11},{8,4},{9,5},{10,6},{11,7},{20,24},{21,25... | collective-permute-start | bytes 3145736 | tf_op jit(solution)/shard_map/ppermute | solution.py:106
  8.9 44.8 %collective-permute-start.7 = (bf16[256,2048]{1,0:T(8,128)(2,1)S(1)}, bf16[256,2048]{1,0:T(8,128)(2,1)S(1)}, u32[]{:S(2)}, u32[]{:S(2)}) collective-permute-start(bf16[256,2048]{1,0:T(8,128)(2,1)S(1)} %get-tuple-element.50.refs_0_.refs_1_), channel_id=1, source_target_pairs={{0,4},{1,5},{2,6},{3,7},{4,0},{5,1},{6,2},{7,3},{8,12},{9,13},{10,... | collective-permute-start | bytes 3145736 | tf_op jit(solution)/shard_map/ppermute | solution.py:106
  31.3 24.0 %collective-permute-start.1 = (bf16[256,2048]{1,0:T(8,128)(2,1)}, bf16[256,2048]{1,0:T(8,128)(2,1)}, u32[]{:S(2)}, u32[]{:S(2)}) collective-permute-start(bf16[256,2048]{1,0:T(8,128)(2,1)} %collective-permute-done.refs_0_.refs_1_), channel_id=1, source_target_pairs={{4,8},{5,9},{6,10},{7,11},{8,4},{9,5},{10,6},{11,7},{20,24},{21,25... | collective-permute-start | bytes 3145736 | tf_op jit(solution)/shard_map/ppermute | solution.py:106
  33.0 40.4 %collective-permute-start.10 = (bf16[256,2048]{1,0:T(8,128)(2,1)S(1)}, bf16[256,2048]{1,0:T(8,128)(2,1)}, u32[]{:S(2)}, u32[]{:S(2)}) collective-permute-start(bf16[256,2048]{1,0:T(8,128)(2,1)S(1)} %get-tuple-element.50.refs_0_.refs_1_), channel_id=1, source_target_pairs={{4,8},{5,9},{6,10},{7,11},{8,4},{9,5},{10,6},{11,7},{20,24},{21,25... | collective-permute-start | bytes 3145736 | tf_op jit(solution)/shard_map/ppermute | solution.py:106
  34.7 47.3 %collective-permute-start.4 = (bf16[256,2048]{1,0:T(8,128)(2,1)}, bf16[256,2048]{1,0:T(8,128)(2,1)}, u32[]{:S(2)}, u32[]{:S(2)}) collective-permute-start(bf16[256,2048]{1,0:T(8,128)(2,1)} %collective-permute-done.3.refs_0_), channel_id=1, source_target_pairs={{4,0},{5,1},{6,2},{7,3},{8,12},{9,13},{10,14},{11,15},{20,16},{21,... | collective-permute-start | bytes 3145736 | tf_op jit(solution)/shard_map/ppermute | solution.py:106
  53.7 50.0 %collective-permute-start.8 = (bf16[256,2048]{1,0:T(8,128)(2,1)S(1)}, bf16[256,2048]{1,0:T(8,128)(2,1)}, u32[]{:S(2)}, u32[]{:S(2)}) collective-permute-start(bf16[256,2048]{1,0:T(8,128)(2,1)S(1)} %collective-permute-done.7.refs_0_.refs_1_), channel_id=1, source_target_pairs={{4,8},{5,9},{6,10},{7,11},{8,4},{9,5},{10,6},{11,7},{20,24},{21,25... | collective-permute-start | bytes 3145736 | tf_op jit(solution)/shard_map/ppermute | solution.py:106
  57.6 30.6 %collective-permute-start.2 = (bf16[128,2048]{1,0:T(8,128)(2,1)}, bf16[128,2048]{1,0:T(8,128)(2,1)}, u32[]{:S(2)}, u32[]{:S(2)}) collective-permute-start(bf16[128,2048]{1,0:T(8,128)(2,1)} %get-tuple-element.54.refs_0_), channel_id=1, source_target_pairs={{4,0},{5,1},{6,2},{7,3},{8,12},{9,13},{10,14},{11,15},{20,16},{21,... | collective-permute-start | bytes 1572872 | tf_op jit(solution)/shard_map/ppermute | solution.py:106
  64.4 1.0 copy-start.1
  65.4 1.0 copy-start.3
  66.3 8.4 %copy-start.2 = (f32[2,256,512]{2,1,0:T(8,128)S(1)}, f32[2,256,512]{2,1,0:T(8,128)}, u32[]{:S(2)}) copy-start(f32[2,256,512]{2,1,0:T(8,128)} %copy-done.1) | copy-start | bytes 3145732
  66.3 8.4 %copy-start.4 = (f32[2,256,512]{2,1,0:T(8,128)S(1)}, f32[2,256,512]{2,1,0:T(8,128)}, u32[]{:S(2)}) copy-start(f32[2,256,512]{2,1,0:T(8,128)} %copy-done.3) | copy-start | bytes 3145732
  66.3 32.3 %collective-permute-start.14 = (bf16[128,2048]{1,0:T(8,128)(2,1)}, bf16[128,2048]{1,0:T(8,128)(2,1)S(1)}, u32[]{:S(2)}, u32[]{:S(2)}) collective-permute-start(bf16[128,2048]{1,0:T(8,128)(2,1)} %get-tuple-element.55.refs_0_), channel_id=1, source_target_pairs={{4,0},{5,1},{6,2},{7,3},{8,12},{9,13},{10,14},{11,15},{20,16},{21,... | collective-permute-start | bytes 1572872 | tf_op jit(solution)/shard_map/ppermute | solution.py:106
  73.4 47.7 %collective-permute-start.11 = (bf16[256,2048]{1,0:T(8,128)(2,1)}, bf16[256,2048]{1,0:T(8,128)(2,1)S(1)}, u32[]{:S(2)}, u32[]{:S(2)}) collective-permute-start(bf16[256,2048]{1,0:T(8,128)(2,1)} %collective-permute-done.10.refs_0_), channel_id=1, source_target_pairs={{4,0},{5,1},{6,2},{7,3},{8,12},{9,13},{10,14},{11,15},{20,16},{21,... | collective-permute-start | bytes 3145736 | tf_op jit(solution)/shard_map/ppermute | solution.py:106
  88.2 10.4 %copy-start = (bf16[128,2048]{1,0:T(8,128)(2,1)S(1)}, bf16[128,2048]{1,0:T(8,128)(2,1)}, u32[]{:S(2)}) copy-start(bf16[128,2048]{1,0:T(8,128)(2,1)} %get-tuple-element.55.refs_0_) | copy-start | bytes 1572868
  93.5 12.8 %collective-permute-start.5 = (f32[2,128,512]{2,1,0:T(8,128)S(1)}, f32[2,128,512]{2,1,0:T(8,128)S(1)}, u32[]{:S(2)}, u32[]{:S(2)}) collective-permute-start(f32[2,128,512]{2,1,0:T(8,128)S(1)} %get-tuple-element.29), channel_id=1, source_target_pairs={{0,1},{1,0},{2,3},{3,2},{4,5},{5,4},{6,7},{7,6},{8,9},{9,8},{10,11... | collective-permute-start | bytes 1572872 | tf_op jit(solution)/shard_map/ppermute | solution.py:111
  103.6 4.9 %collective-permute-start.15 = (f32[2,128,512]{2,1,0:T(8,128)S(1)}, f32[2,128,512]{2,1,0:T(8,128)S(1)}, u32[]{:S(2)}, u32[]{:S(2)}) collective-permute-start(f32[2,128,512]{2,1,0:T(8,128)S(1)} %get-tuple-element.39), channel_id=1, source_target_pairs={{0,1},{1,0},{2,3},{3,2},{4,5},{5,4},{6,7},{7,6},{8,9},{9,8},{10,11... | collective-permute-start | bytes 1572872 | tf_op jit(solution)/shard_map/ppermute | solution.py:111
  105.0 27.3 %collective-permute-start.9 = (bf16[128,2048]{1,0:T(8,128)(2,1)S(1)}, bf16[128,2048]{1,0:T(8,128)(2,1)S(1)}, u32[]{:S(2)}, u32[]{:S(2)}) collective-permute-start(bf16[128,2048]{1,0:T(8,128)(2,1)S(1)} %get-tuple-element.52.refs_1_), channel_id=1, source_target_pairs={{4,0},{5,1},{6,2},{7,3},{8,12},{9,13},{10,14},{11,15},{20,16},{21,... | collective-permute-start | bytes 1572872 | tf_op jit(solution)/shard_map/ppermute | solution.py:106
  106.4 20.6 %collective-permute-start.6 = (bf16[1,128,512]{2,1,0:T(8,128)(2,1)S(1)}, bf16[1,128,512]{2,1,0:T(8,128)(2,1)S(1)}, u32[]{:S(2)}, u32[]{:S(2)}) collective-permute-start(bf16[1,128,512]{2,1,0:T(8,128)(2,1)S(1)} %fusion.23), channel_id=1, source_target_pairs={{0,2},{1,3},{2,0},{3,1},{4,6},{5,7},{6,4},{7,5},{8,10},{9,11},{10,... | collective-permute-start | bytes 393224 | tf_op jit(solution)/shard_map/ppermute | solution.py:111
  108.6 18.4 %collective-permute-start.16 = (bf16[1,128,512]{2,1,0:T(8,128)(2,1)S(1)}, bf16[1,128,512]{2,1,0:T(8,128)(2,1)S(1)}, u32[]{:S(2)}, u32[]{:S(2)}) collective-permute-start(bf16[1,128,512]{2,1,0:T(8,128)(2,1)S(1)} %fusion.25), channel_id=1, source_target_pairs={{0,2},{1,3},{2,0},{3,1},{4,6},{5,7},{6,4},{7,5},{8,10},{9,11},{10,... | collective-permute-start | bytes 393224 | tf_op jit(solution)/shard_map/ppermute | solution.py:111
  114.3 28.5 %collective-permute-start.17 = (bf16[128,2048]{1,0:T(8,128)(2,1)S(1)}, bf16[128,2048]{1,0:T(8,128)(2,1)S(1)}, u32[]{:S(2)}, u32[]{:S(2)}) collective-permute-start(bf16[128,2048]{1,0:T(8,128)(2,1)S(1)} %get-tuple-element.53.refs_1_), channel_id=1, source_target_pairs={{4,0},{5,1},{6,2},{7,3},{8,12},{9,13},{10,14},{11,15},{20,16},{21,... | collective-permute-start | bytes 1572872 | tf_op jit(solution)/shard_map/ppermute | solution.py:106
  121.1 6.0 %copy-start.5 = (bf16[512,512]{1,0:T(8,128)(2,1)S(1)}, bf16[512,512]{1,0:T(8,128)(2,1)}, u32[]{:S(2)}) copy-start(bf16[512,512]{1,0:T(8,128)(2,1)} %param.7) | copy-start | bytes 1572868
  137.3 10.5 %collective-permute-start.12 = (f32[2,128,512]{2,1,0:T(8,128)S(1)}, f32[2,128,512]{2,1,0:T(8,128)S(1)}, u32[]{:S(2)}, u32[]{:S(2)}) collective-permute-start(f32[2,128,512]{2,1,0:T(8,128)S(1)} %get-tuple-element.37), channel_id=1, source_target_pairs={{0,1},{1,0},{2,3},{3,2},{4,5},{5,4},{6,7},{7,6},{8,9},{9,8},{10,11... | collective-permute-start | bytes 1572872 | tf_op jit(solution)/shard_map/ppermute | solution.py:111
  147.7 2.0 %collective-permute-start.18 = (f32[2,128,512]{2,1,0:T(8,128)S(1)}, f32[2,128,512]{2,1,0:T(8,128)S(1)}, u32[]{:S(2)}, u32[]{:S(2)}) collective-permute-start(f32[2,128,512]{2,1,0:T(8,128)S(1)} %get-tuple-element.41), channel_id=1, source_target_pairs={{0,1},{1,0},{2,3},{3,2},{4,5},{5,4},{6,7},{7,6},{8,9},{9,8},{10,11... | collective-permute-start | bytes 1572872 | tf_op jit(solution)/shard_map/ppermute | solution.py:111
  147.9 6.4 %collective-permute-start.13 = (bf16[1,128,512]{2,1,0:T(8,128)(2,1)S(1)}, bf16[1,128,512]{2,1,0:T(8,128)(2,1)S(1)}, u32[]{:S(2)}, u32[]{:S(2)}) collective-permute-start(bf16[1,128,512]{2,1,0:T(8,128)(2,1)S(1)} %fusion.24), channel_id=1, source_target_pairs={{0,2},{1,3},{2,0},{3,1},{4,6},{5,7},{6,4},{7,5},{8,10},{9,11},{10,... | collective-permute-start | bytes 393224 | tf_op jit(solution)/shard_map/ppermute | solution.py:111
  149.8 6.9 %collective-permute-start.19 = (bf16[1,128,512]{2,1,0:T(8,128)(2,1)S(1)}, bf16[1,128,512]{2,1,0:T(8,128)(2,1)S(1)}, u32[]{:S(2)}, u32[]{:S(2)}) collective-permute-start(bf16[1,128,512]{2,1,0:T(8,128)(2,1)S(1)} %fusion.26), channel_id=1, source_target_pairs={{0,2},{1,3},{2,0},{3,1},{4,6},{5,7},{6,4},{7,5},{8,10},{9,11},{10,... | collective-permute-start | bytes 393224 | tf_op jit(solution)/shard_map/ppermute | solution.py:111
  156.8 4.5 %collective-permute-start.20 = (f32[512]{0:T(512)S(1)}, f32[512]{0:T(512)S(1)}, u32[]{:S(2)}, u32[]{:S(2)}) collective-permute-start(f32[512]{0:T(512)S(1)} %pad_maximum_fusion.1), channel_id=1, source_target_pairs={{0,8},{1,9},{2,10},{3,11},{4,12},{5,13},{6,14},{7,15},{8,0},{9,1},... | collective-permute-start | bytes 6152 | tf_op jit(solution)/shard_map/ppermute | solution.py:111
  161.4 3.7 %collective-permute-start.21 = (f32[512]{0:T(512)S(1)}, f32[512]{0:T(512)S(1)}, u32[]{:S(2)}, u32[]{:S(2)}) collective-permute-start(f32[512]{0:T(512)S(1)} %fusion.27), channel_id=1, source_target_pairs={{0,4},{1,5},{2,6},{3,7},{4,0},{5,1},{6,2},{7,3},{8,12},{9,13},{10,... | collective-permute-start | bytes 6152 | tf_op jit(solution)/shard_map/ppermute | solution.py:111
  165.1 3.6 %collective-permute-start.22 = (f32[512]{0:T(512)S(1)}, f32[512]{0:T(512)S(1)}, u32[]{:S(2)}, u32[]{:S(2)}) collective-permute-start(f32[512]{0:T(512)S(1)} %add.85), channel_id=1, source_target_pairs={{0,2},{1,3},{2,0},{3,1},{4,6},{5,7},{6,4},{7,5},{8,10},{9,11},{10,... | collective-permute-start | bytes 6152 | tf_op jit(solution)/shard_map/ppermute | solution.py:111
  168.6 1.2 collective-permute-start.23
